TPU v7x, 1024 devices: a whole 8x8x8 slice. The times are simulated.
1024 devices in a mesh: dp: 4 (over z_lo, core), expert: 64 (over y, x), tensor: 4 (over z_hi).
Axes of the slice: x: 8, y: 8, z: 8 (z_hi: 4, z_lo: 2; z = z_hi * 2 + z_lo), core: 2. Of those that a mesh axis runs over, the one named last changes fastest.
Arguments:
- attn_out: bfloat16 [2048, 16384], P(('dp', 'expert'), 'tensor'), parts along dimension 0, may hold values from -6 to 6
- w_proj: bfloat16 [16384, 7168], P('tensor', 'expert'), may hold values from -0.046875 to 0.046875
- w_in: bfloat16 [64, 7168, 2, 512], P('expert', 'tensor'), may hold values from -0.0625 to 0.0625
- w_out: bfloat16 [64, 512, 7168], P('expert', None, 'tensor'), may hold values from -0.125 to 0.125
- expert_ids: int32 [2048, 8], P(('dp', 'expert')), parts along dimension 0, may hold values from 0 to 255, as said below
- slots: int32 [2048, 8], P(('dp', 'expert')), parts along dimension 0, may hold values from -1 to 1, as said below
- gates: float32 [2048, 8], P(('dp', 'expert')), parts along dimension 0, may hold values from 0.2 to 1
Outputs:
- projected: bfloat16 [2048, 7168], P(('dp', 'expert'), 'tensor'), parts along dimension 0
- moe_out: bfloat16 [2048, 7168], P(('dp', 'expert'), 'tensor'), parts along dimension 0
There are 4 independent parts, one for each index of `dp`. A program takes and returns all parts, laid end to end along the dimension named above; an argument that names none is the same for every part. Nothing has to cross between parts.
Inputs may be any that keep to these rules, and one draw needn't show every extreme that they name: `expert_ids`: each row names 8 different experts. Within each aligned block of 8 rows, the picks of one expert that are not dropped hold the slots 0, 1, ... in order of the rows, and a pick is dropped only when 2 earlier picks of its block already name the same expert. In every block some expert of the wave fills all 2 slots.
All inputs are finite; a program needn't handle non-finite values.
Results may differ from a plain program's by a relative error of at most 0.012.
Values may be sent and summed in bfloat16 or wider, within the bound.
No kernel may reach another device: no remote copies, remote signals or barrier semaphores. Data moves between devices by JAX's collectives and lax.ppermute only.
A program may use at most 32 MiB of HBM per device.

v0:
```python
import jax
import jax.numpy as jnp
from jax import lax
from jax.sharding import PartitionSpec as P

HSPLIT = 4
CAP = 2


def per_device(attn_out, w_proj, w_in, w_out, expert_ids, slots, gates):
    groups = lax.axis_size("expert")
    flight = groups // HSPLIT
    width_block = w_in.shape[1]
    slice_units = w_in.shape[3]
    partial_value = jnp.dot(
        lax.all_gather(attn_out, "expert", axis=0, tiled=True),
        w_proj,
        preferred_element_type=jnp.float32,
    )
    spread = lax.all_to_all(partial_value, "expert", split_axis=0, concat_axis=1, tiled=True)
    projected = lax.psum_scatter(spread, "tensor", scatter_dimension=1, tiled=True).astype(
        jnp.bfloat16
    )
    wave_pos = jnp.arange(flight * CAP, dtype=jnp.int32)
    matches = (expert_ids[:, :, None] == wave_pos // CAP) & (slots[:, :, None] == wave_pos % CAP)
    dispatch_w = jnp.sum(matches.astype(jnp.float32), axis=1).astype(jnp.bfloat16)
    combine_w = jnp.sum(jnp.where(matches, gates[:, :, None], jnp.float32(0.0)), axis=1)
    routed = jnp.einsum("tw,td->wd", dispatch_w, projected, preferred_element_type=jnp.float32)
    routed = routed.astype(jnp.bfloat16).reshape(flight, 1, CAP, width_block)
    outgoing = jnp.broadcast_to(routed, (flight, HSPLIT, CAP, width_block)).reshape(
        groups, CAP, width_block
    )
    gate_up_w = w_in.reshape(width_block, 2 * slice_units)
    down_w = w_out.reshape(slice_units, width_block)
    received = lax.all_to_all(outgoing, "expert", split_axis=0, concat_axis=0, tiled=True)
    n_items = received.shape[1]
    flat_rows = received.reshape(groups * n_items, width_block)
    gate_up = jnp.dot(flat_rows, gate_up_w, preferred_element_type=jnp.float32)
    gate_up = lax.psum(gate_up, "tensor")
    hidden = (jax.nn.silu(gate_up[:, :slice_units]) * gate_up[:, slice_units:]).astype(jnp.bfloat16)
    result = jnp.dot(hidden, down_w, preferred_element_type=jnp.float32)
    returned = lax.all_to_all(
        result.reshape(groups, n_items, width_block).astype(jnp.bfloat16),
        "expert",
        split_axis=0,
        concat_axis=0,
        tiled=True,
    ).astype(jnp.float32)
    expert_sum = jnp.sum(returned.reshape(flight, HSPLIT, CAP, width_block), axis=1)
    expert_sum = expert_sum.reshape(flight * CAP, width_block)
    moe_out = jnp.dot(
        combine_w, expert_sum, precision=lax.Precision.HIGHEST, preferred_element_type=jnp.float32
    )
    return (projected, moe_out.astype(jnp.bfloat16))


def solution(mesh):
    placed = (
        P(("dp", "expert"), "tensor"),
        P("tensor", "expert"),
        P("expert", "tensor", None, None),
        P("expert", None, "tensor"),
        P(("dp", "expert"), None),
        P(("dp", "expert"), None),
        P(("dp", "expert"), None),
    )
    return jax.shard_map(
        per_device,
        mesh=mesh,
        in_specs=placed,
        out_specs=(P(("dp", "expert"), "tensor"), P(("dp", "expert"), "tensor")),
        check_vma=False,
    )
```

profile of v0, /device:TPU:2, one launch (start us, length us, event | category | flops | bytes accessed | tf_op | source)
XLA Modules:
  0.0 299.3 jit_solution(17551141399700728510)
XLA Ops:
  7.2 0.0 copy-start
  7.2 0.0 copy-start.4
  7.2 0.0 all-gather.2.cloned.1.call-start
  7.3 0.7 all-gather.2.cloned.1.call-update
  7.9 0.0 reduce-scatter.2.cloned.1.call-start
  8.0 107.4 %all-gather.2.cloned.1.call-done = bf16[512,4096]{1,0:T(8,128)(2,1)} async-done(((bf16[8,4096]{1,0:T(8,128)(2,1)}), bf16[512,4096]{1,0:T(8,128)(2,1)}) %all-gather.2.cloned.1.call-update) | async-done | bytes 4194320 | tf_op jit(solution)/shard_map/all_gather | solution.py:16
  115.4 3.7 %convolution_bitcast_fusion = f32[64,8,112]{2,1,0:T(8,128)S(1)} fusion(bf16[512,4096]{1,0:T(8,128)(2,1)} %all-gather.2.cloned.1.call-done, bf16[4096,112]{0,1:T(8,128)(2,1)} %param.8), kind=kOutput, calls=%fused_computation.4 | convolution fusion | flops 469762048 | bytes 5341184 | tf_op jit(solution)/shard_map/dot_general | solution.py:15
  119.1 22.1 %all_to_all.29 = f32[64,8,112]{2,1,0:T(8,128)S(1)} all-to-all(f32[64,8,112]{2,1,0:T(8,128)S(1)} %convolution_bitcast_fusion), channel_id=1, replica_groups=mesh['dp'=4,'expert'=64,'tensor'=4] {'expert'}, dimensions={0} | all-to-all | bytes 458752 | tf_op jit(solution)/shard_map/all_to_all | solution.py:20
  141.2 0.1 copy.28
  141.2 0.9 all_to_all.23
  142.1 0.0 reduce-scatter.2.cloned.1.call-update
  142.2 0.1 convert_reduce_fusion.1
  142.3 26.3 %reduce-scatter.2.cloned.1.call-done = f32[8,1792]{1,0:T(8,128)} async-done(((f32[8,7168]{1,0:T(8,128)}), f32[8,1792]{1,0:T(8,128)}) %reduce-scatter.2.cloned.1.call-update) | async-done | bytes 57360 | tf_op jit(solution)/shard_map/reduce_scatter | solution.py:21
  168.5 0.8 convert_element_type.22
  169.4 0.2 convolution_convert_fusion.1
  169.6 1.0 broadcast_in_dim.27
  170.7 12.8 %all-to-all-start.1 = ((bf16[64,2,1792]{2,1,0:T(2,128)(2,1)}), bf16[64,2,1792]{2,1,0:T(2,128)(2,1)S(1)}, u32[]{:S(2)}, u32[]{:S(2)}) async-start(bf16[64,2,1792]{2,1,0:T(2,128)(2,1)} %bitcast.2), calls=%async_computation.2 | async-start | bytes 917504 | tf_op jit(solution)/shard_map/all_to_all | solution.py:35
  183.5 0.0 all-reduce.2.cloned.1.call-start
  183.5 4.8 %copy.35 = bf16[224,8,2,512]{3,1,2,0:T(8,128)(2,1)} copy(bf16[224,8,2,512]{3,2,1,0:T(2,128)(2,1)} %bitcast.23) | data formatting | bytes 7340032
  188.3 11.1 %all-to-all-done.1 = bf16[64,2,1792]{2,1,0:T(2,128)(2,1)S(1)} async-done(((bf16[64,2,1792]{2,1,0:T(2,128)(2,1)}), bf16[64,2,1792]{2,1,0:T(2,128)(2,1)S(1)}, u32[]{:S(2)}, u32[]{:S(2)}) %all-to-all-start.1) | async-done | bytes 458784 | tf_op jit(solution)/shard_map/all_to_all | solution.py:35
  199.5 0.2 reshape.58
  199.7 3.5 %fusion.4 = f32[128,1024]{1,0:T(8,128)} fusion(bf16[128,1792]{1,0:T(8,128)(2,1)S(1)} %reshape.58, bf16[1792,1024]{1,0:T(8,128)(2,1)} %bitcast.22), kind=kOutput, calls=%fused_computation.18 | convolution fusion | flops 469762048 | bytes 4653056 | tf_op jit(solution)/shard_map/dot_general | solution.py:38
  203.1 0.0 all-reduce.2.cloned.1.call-update
  203.2 57.9 %all-reduce.2.cloned.1.call-done = f32[128,1024]{1,0:T(8,128)} async-done(((f32[128,1024]{1,0:T(8,128)}), f32[128,1024]{1,0:T(8,128)}) %all-reduce.2.cloned.1.call-update) | async-done | bytes 524304 | tf_op jit(solution)/shard_map/psum | solution.py:39
  261.1 1.1 fusion.1
  262.2 0.1 dot_general.20
  262.2 0.4 convolution_convert_fusion
  262.7 0.5 copy.30
  263.1 28.2 %all_to_all.30 = bf16[64,2,1792]{2,1,0:T(2,128)(2,1)S(1)} all-to-all(bf16[64,2,1792]{2,1,0:T(2,128)(2,1)S(1)} %copy.30), channel_id=1, replica_groups=mesh['dp'=4,'expert'=64,'tensor'=4] {'expert'}, dimensions={0} | all-to-all | bytes 917504 | tf_op jit(solution)/shard_map/all_to_all | solution.py:42
  291.3 0.4 convert_reduce_fusion
  291.8 0.2 reshape.63
  291.9 0.8 convolution_convert_fusion.2
  (10 shorter events, 0.1 us)
Async XLA Ops:
  7.2 255.1 %copy-start = (bf16[1,512,1792]{2,1,0:T(8,128)(2,1)S(1)}, bf16[1,512,1792]{2,1,0:T(8,128)(2,1)}, u32[]{:S(2)}) copy-start(bf16[1,512,1792]{2,1,0:T(8,128)(2,1)} %param.10) | copy-start | bytes 5505028
  7.2 134.9 %copy-start.4 = (f32[8,8]{1,0:T(8,128)S(1)}, f32[8,8]{1,0:T(8,128)}, u32[]{:S(2)}) copy-start(f32[8,8]{1,0:T(8,128)} %param.13) | copy-start | bytes 772
  7.2 134.9 %copy-start.2 = (s32[8,8]{1,0:T(8,128)S(1)}, s32[8,8]{1,0:T(8,128)}, u32[]{:S(2)}) copy-start(s32[8,8]{1,0:T(8,128)} %param.12) | copy-start | bytes 772
  7.2 134.9 %copy-start.3 = (s32[8,8]{1,0:T(8,128)S(1)}, s32[8,8]{1,0:T(8,128)}, u32[]{:S(2)}) copy-start(s32[8,8]{1,0:T(8,128)} %param.11) | copy-start | bytes 772
  7.2 108.2 %all-gather.2.cloned.1.call-start = ((), (), s32[]{:S(2)}) async-start(), calls=%async_computation.4 | async-start | bytes 4259840 | tf_op jit(solution)/shard_map/all_gather | solution.py:16
  7.9 160.6 %reduce-scatter.2.cloned.1.call-start = ((), (), s32[]{:S(2)}) async-start(), calls=%async_computation.5 | async-start | bytes 286720 | tf_op jit(solution)/shard_map/reduce_scatter | solution.py:21
  169.4 19.0 %copy-start.1 = (bf16[8,1792]{1,0:T(8,128)(2,1)}, bf16[8,1792]{1,0:T(8,128)(2,1)S(1)}, u32[]{:S(2)}) copy-start(bf16[8,1792]{1,0:T(8,128)(2,1)S(1)} %convert_element_type.22) | copy-start | bytes 86020
  170.7 28.8 %all-to-all-start.1 = ((bf16[64,2,1792]{2,1,0:T(2,128)(2,1)}), bf16[64,2,1792]{2,1,0:T(2,128)(2,1)S(1)}, u32[]{:S(2)}, u32[]{:S(2)}) async-start(bf16[64,2,1792]{2,1,0:T(2,128)(2,1)} %bitcast.2), calls=%async_computation.2 | async-start | bytes 917504 | tf_op jit(solution)/shard_map/all_to_all | solution.py:35
  183.5 77.6 %all-reduce.2.cloned.1.call-start = ((), (), s32[]{:S(2)}) async-start(), calls=%async_computation.6 | async-start | bytes 1048576 | tf_op jit(solution)/shard_map/psum | solution.py:39
Sparse Core Ops, SparseCore 0:
  12.3 103.0 all-gather.1
  142.2 26.2 reduce-scatter.1
  203.3 57.7 all-reduce.1
where the time goes:
time: 300 us; the launch traced here: 299 us
  waiting for transfers between devices  203 us (68%)
  blocking collectives  50.3 us (17%)
  between operations  13.9 us (5%)
  starting transfers between devices  12.9 us (4%)
  matrix products  8.62 us (3%)
  local copies, waits for them, and re-layouts  7.71 us (3%)
    all_gather x1, waiting for transfers between devices, per_device(): lax.all_gather(attn_out, 'expert', axis=0, tiled=True)  107 us
    psum x1, waiting for transfers between devices, per_device(): gate_up = lax.psum(gate_up, 'tensor')  57.9 us
    all_to_all x1, blocking collectives, per_device(): lax.all_to_all(result.reshape(groups, n_items, width_block).astype(jnp.bf...  28.2 us
    reduce_scatter x1, waiting for transfers between devices, per_device(): lax.psum_scatter(spread, 'tensor', scatter_dimension=1, tiled=True)  26.3 us
    all_to_all x1, blocking collectives, per_device(): lax.all_to_all(partial_value, 'expert', split_axis=0, concat_axis=1, tile...  22.1 us
    all_to_all x1, starting transfers between devices, per_device(): lax.all_to_all(outgoing, 'expert', split_axis=0, concat_axis=0, tiled=True)  12.8 us
    all_to_all x1, waiting for transfers between devices, per_device(): lax.all_to_all(outgoing, 'expert', split_axis=0, concat_axis=0, tiled=True)  11.1 us
  transfers between devices with their start and end apart: 4, of which 4 were waited for; matrix products, arithmetic and copies ran while one was open for 2% of the time, Pallas kernels for 0%

commit v1 on v0

v1 whole, which is shorter than its diff:
```python
import jax
import jax.numpy as jnp
from jax import lax
from jax.sharding import Mesh, PartitionSpec as P

HSPLIT = 4
CAP = 2
EXPERT = ("yh", "yl", "xh", "xl")
TURNED = ("tensor", "yl", "xh", "xl")
BF16 = jnp.bfloat16
F32 = jnp.float32


def project(attn_out, w_proj):
    rows, depth = attn_out.shape
    cols = w_proj.shape[1]
    part = depth // 4
    me = lax.axis_index(("yl", "xl"))
    w_cols = w_proj.T
    blocks = []
    for d in range(4):
        piece = lax.dynamic_slice(w_cols, (0, (me ^ d) * part), (cols, part))
        if d:
            piece = lax.ppermute(piece, ("yl", "xl"), [(i, i ^ d) for i in range(4)])
        blocks.append(piece)
    sent = attn_out.reshape(rows, 2, 2, part).transpose(1, 2, 0, 3)
    sent = jnp.broadcast_to(sent[None, :, None, :], (4, 2, 4, 2, rows, part))
    tokens = lax.all_to_all(
        sent.reshape(64, rows, part), EXPERT, split_axis=0, concat_axis=0, tiled=True
    ).reshape(64 * rows, part)
    wide = jnp.zeros((4, cols, part), BF16)
    for d in range(4):
        wide = lax.dynamic_update_slice(wide, blocks[d][None], (me ^ d, 0, 0))
    partial = lax.dot_general(
        tokens, wide.reshape(4 * cols, part), (((1,), (1,)), ((), ())), preferred_element_type=F32
    ).astype(BF16)
    got = lax.all_to_all(
        partial.reshape(64, rows, 4 * cols), TURNED, split_axis=0, concat_axis=0, tiled=True
    )
    got = got.reshape(4, 2, 4, 2, rows, 4 * cols).astype(F32)
    total = jnp.sum(got, axis=(0, 1, 3)).astype(BF16)
    total = total.reshape(4, rows, 2, 2, cols).transpose(1, 2, 0, 3, 4).reshape(rows, 16 * cols)
    return lax.ppermute(
        total, ("yh", "tensor"), [(a * 4 + b, b * 4 + a) for a in range(4) for b in range(4)]
    )


def per_device(attn_out, w_proj, w_in, w_out, expert_ids, slots, gates):
    groups = lax.axis_size(EXPERT)
    flight = groups // HSPLIT
    width_block = w_in.shape[1]
    slice_units = w_in.shape[3]
    wave_pos = jnp.arange(flight * CAP, dtype=jnp.int32)
    matches = (expert_ids[:, :, None] == wave_pos // CAP) & (slots[:, :, None] == wave_pos % CAP)
    dispatch_w = jnp.sum(matches.astype(F32), axis=1).astype(BF16)
    combine_w = jnp.sum(jnp.where(matches, gates[:, :, None], F32(0.0)), axis=1)
    projected = project(attn_out, w_proj)
    routed = jnp.einsum("tw,td->wd", dispatch_w, projected, preferred_element_type=F32)
    routed = routed.astype(BF16).reshape(flight, 1, CAP, width_block)
    outgoing = jnp.broadcast_to(routed, (flight, HSPLIT, CAP, width_block)).reshape(
        groups, CAP, width_block
    )
    gate_up_w = w_in.reshape(width_block, 2 * slice_units)
    down_w = w_out.reshape(slice_units, width_block)
    received = lax.all_to_all(outgoing, EXPERT, split_axis=0, concat_axis=0, tiled=True)
    flat_rows = received.reshape(groups * CAP, width_block)
    gate_up = jnp.dot(flat_rows, gate_up_w, preferred_element_type=F32).astype(BF16)
    quarter = groups * CAP // 4
    gate_up = lax.all_to_all(
        gate_up.reshape(4, quarter, 2 * slice_units), "tensor", split_axis=0, concat_axis=0, tiled=True
    )
    gate_up = jnp.sum(gate_up.astype(F32), axis=0)
    hidden = (jax.nn.silu(gate_up[:, :slice_units]) * gate_up[:, slice_units:]).astype(BF16)
    hidden = lax.all_to_all(
        jnp.broadcast_to(hidden[None], (4, quarter, slice_units)),
        "tensor",
        split_axis=0,
        concat_axis=0,
        tiled=True,
    ).reshape(groups * CAP, slice_units)
    result = jnp.dot(hidden, down_w, preferred_element_type=F32)
    returned = lax.all_to_all(
        result.reshape(groups, CAP, width_block).astype(BF16),
        EXPERT,
        split_axis=0,
        concat_axis=0,
        tiled=True,
    ).astype(F32)
    expert_sum = jnp.sum(returned.reshape(flight, HSPLIT, CAP, width_block), axis=1)
    expert_sum = expert_sum.reshape(flight * CAP, width_block)
    moe_out = jnp.dot(
        combine_w, expert_sum, precision=lax.Precision.HIGHEST, preferred_element_type=F32
    )
    return (projected, moe_out.astype(BF16))


def solution(mesh):
    split = Mesh(
        mesh.devices.reshape(4, 4, 2, 4, 2, 4), ("dp", "yh", "yl", "xh", "xl", "tensor")
    )
    rows = ("dp",) + EXPERT
    placed = (
        P(rows, "tensor"),
        P("tensor", EXPERT),
        P(EXPERT, "tensor", None, None),
        P(EXPERT, None, "tensor"),
        P(rows, None),
        P(rows, None),
        P(rows, None),
    )
    return jax.shard_map(
        per_device,
        mesh=split,
        in_specs=placed,
        out_specs=(P(rows, "tensor"), P(rows, "tensor")),
        check_vma=False,
    )
```

time: 300 us -> 187 us (0.62)
  waiting for transfers between devices: 203 us -> 46.6 us
  starting transfers between devices: 12.9 us -> 69.4 us
  between operations: 13.9 us -> 0.9 us
  local copies, waits for them, and re-layouts: 7.71 us -> 18.6 us
  blocking collectives: 50.3 us -> 44.5 us
    all_gather x1 -> x0, waiting for transfers between devices: 107 us -> none  [per_device(): lax.all_gather(attn_out, 'expert', axis=0, tiled=True)]
    psum x1 -> x0, waiting for transfers between devices: 57.9 us -> none  [per_device(): gate_up = lax.psum(gate_up, 'tensor')]
    all_to_all x1 -> x3, starting transfers between devices: 12.8 us -> 59.5 us  [the longest x1 21.8 us: per_device(): lax.all_to_all(outgoing, EXPERT, split_axis=0, concat_axis=0, tiled=True)]
    reduce_scatter x1 -> x0, waiting for transfers between devices: 26.3 us -> none  [per_device(): lax.psum_scatter(spread, 'tensor', scatter_dimension=1, tiled=True)]
    all_to_all x1 -> x3, waiting for transfers between devices: 11.1 us -> 29.7 us  [the longest x1 19.1 us: project(): lax.all_to_all(partial.reshape(64, rows, 4 * cols), TURNED, split_axis=0,...]
    ppermute x0 -> x4, waiting for transfers between devices: none -> 16.9 us  [the longest x3 16.9 us: project(): piece = lax.ppermute(piece, ('yl', 'xl'), [(i, i ^ d) for i in range(4)])]
    ppermute x0 -> x4, starting transfers between devices: none -> 9.86 us  [the longest x3 9.2 us: project(): piece = lax.ppermute(piece, ('yl', 'xl'), [(i, i ^ d) for i in range(4)])]
    all_to_all x2 -> x3, blocking collectives: 50.3 us -> 44.5 us  [the longest x1 20.5 us: per_device(): lax.all_to_all(result.reshape(groups, CAP, width_block).astype(BF16), EXP...]
  transfers between devices with their start and end apart: 4 -> 7, of which waited for: 4 -> 4; matrix products, arithmetic and copies ran while one was open for 2% -> 7% of each run, Pallas kernels for 0% -> 0%
where the time goes in v1:
time: 187 us
  starting transfers between devices  69.4 us (37%)
  waiting for transfers between devices  46.6 us (25%)
  blocking collectives  44.5 us (24%)
  local copies, waits for them, and re-layouts  18.6 us (10%)
  matrix products  6.01 us (3%)
    all_to_all x1, starting transfers between devices, per_device(): lax.all_to_all(outgoing, EXPERT, split_axis=0, concat_axis=0, tiled=True)  21.8 us
    all_to_all x1, blocking collectives, per_device(): lax.all_to_all(result.reshape(groups, CAP, width_block).astype(BF16), EXP...  20.5 us
    all_to_all x1, starting transfers between devices, project(): lax.all_to_all(partial.reshape(64, rows, 4 * cols), TURNED, split_axis=0,...  20.5 us
    all_to_all x1, waiting for transfers between devices, project(): lax.all_to_all(partial.reshape(64, rows, 4 * cols), TURNED, split_axis=0,...  19.1 us
    all_to_all x1, starting transfers between devices, project(): lax.all_to_all(sent.reshape(64, rows, part), EXPERT, split_axis=0, concat...  17.3 us
    ppermute x3, waiting for transfers between devices, project(): piece = lax.ppermute(piece, ('yl', 'xl'), [(i, i ^ d) for i in range(4)])  16.9 us
    all_to_all x1, blocking collectives, per_device(): lax.all_to_all(gate_up.reshape(4, quarter, 2 * slice_units), 'tensor', sp...  13.3 us
    all_to_all x1, blocking collectives, per_device(): lax.all_to_all(jnp.broadcast_to(hidden[None], (4, quarter, slice_units)),...  10.8 us
  transfers between devices with their start and end apart: 7, of which 4 were waited for; matrix products, arithmetic and copies ran while one was open for 7% of the time, Pallas kernels for 0%

profile of v1, /device:TPU:2, one launch (start us, length us, event | category | flops | bytes accessed | tf_op | source)
XLA Modules:
  0.0 186.6 jit_solution(5320682919040921816)
XLA Ops:
  0.6 2.1 %broadcast_in_dim.56 = bf16[4,2,4,2,8,1024]{5,4,3,2,1,0:T(8,128)(2,1)} broadcast(bf16[2,2,8,1024]{3,2,1,0:T(8,128)(2,1)} %bitcast.53), dimensions={1,3,4,5} | broadcast | bytes 1114112 | tf_op jit(solution)/shard_map/broadcast_in_dim | solution.py:27
  2.7 17.3 %all-to-all-start = ((bf16[64,8,1024]{2,1,0:T(8,128)(2,1)}), bf16[64,8,1024]{2,1,0:T(8,128)(2,1)S(1)}, u32[]{:S(2)}, u32[]{:S(2)}) async-start(bf16[64,8,1024]{2,1,0:T(8,128)(2,1)} %bitcast.11), calls=%async_computation | async-start | bytes 2097152 | tf_op jit(solution)/shard_map/all_to_all | solution.py:28
  20.0 2.0 %dynamic-slice_bitcast_fusion = (bf16[112,1024]{1,0:T(8,128)(2,1)}, bf16[112,1024]{1,0:T(8,128)(2,1)}, bf16[112,1024]{1,0:T(8,128)(2,1)}) fusion(bf16[4096,112]{0,1:T(8,128)(2,1)} %param.8, s32[]{:T(128)S(6)} %select_n.54, s32[]{:T(128)S(6)} %select_n.50, s32[]{:T(128)S(6)} %select_n.52), kind=kLoop, calls=%fused_computation.14 | loop fusion | bytes 1376268 | tf_op jit(solution)/shard_map/dynamic_slice | solution.py:22
  22.1 2.5 %collective-permute-start = (bf16[112,1024]{1,0:T(8,128)(2,1)}, bf16[112,1024]{1,0:T(8,128)(2,1)S(1)}, u32[]{:S(2)}, u32[]{:S(2)}) collective-permute-start(bf16[112,1024]{1,0:T(8,128)(2,1)} %get-tuple-element.5), channel_id=1, source_target_pairs={{0,4},{4,0},{32,36},{36,32},{1,5},{5,1},{33,37},{37,33},{2,6},{6,2... | collective-permute-start | bytes 688136 | tf_op jit(solution)/shard_map/ppermute | solution.py:24
  24.5 4.3 %collective-permute-start.2 = (bf16[112,1024]{1,0:T(8,128)(2,1)}, bf16[112,1024]{1,0:T(8,128)(2,1)S(1)}, u32[]{:S(2)}, u32[]{:S(2)}) collective-permute-start(bf16[112,1024]{1,0:T(8,128)(2,1)} %get-tuple-element.4), channel_id=1, source_target_pairs={{0,36},{4,32},{32,4},{36,0},{1,37},{5,33},{33,5},{37,1},{2,38},{6,... | collective-permute-start | bytes 688136 | tf_op jit(solution)/shard_map/ppermute | solution.py:24
  28.9 2.4 %collective-permute-start.1 = (bf16[112,1024]{1,0:T(8,128)(2,1)}, bf16[112,1024]{1,0:T(8,128)(2,1)}, u32[]{:S(2)}, u32[]{:S(2)}) collective-permute-start(bf16[112,1024]{1,0:T(8,128)(2,1)} %get-tuple-element.6), channel_id=1, source_target_pairs={{0,32},{4,36},{32,0},{36,4},{1,33},{5,37},{33,1},{37,5},{2,34},{6,... | collective-permute-start | bytes 688136 | tf_op jit(solution)/shard_map/ppermute | solution.py:24
  31.3 1.1 broadcast_in_dim.51
  32.4 1.7 bitcast_dynamic-update-slice_fusion
  34.1 12.6 %collective-permute-done = bf16[112,1024]{1,0:T(8,128)(2,1)S(1)} collective-permute-done((bf16[112,1024]{1,0:T(8,128)(2,1)}, bf16[112,1024]{1,0:T(8,128)(2,1)S(1)}, u32[]{:S(2)}, u32[]{:S(2)}) %collective-permute-start) | collective-permute-done | bytes 229408 | tf_op jit(solution)/shard_map/ppermute | solution.py:24
  46.7 0.7 bitcast_dynamic-update-slice_fusion.3
  47.4 4.2 %collective-permute-done.1 = bf16[112,1024]{1,0:T(8,128)(2,1)} collective-permute-done((bf16[112,1024]{1,0:T(8,128)(2,1)}, bf16[112,1024]{1,0:T(8,128)(2,1)}, u32[]{:S(2)}, u32[]{:S(2)}) %collective-permute-start.1) | collective-permute-done | bytes 229408 | tf_op jit(solution)/shard_map/ppermute | solution.py:24
  51.7 1.6 bitcast_dynamic-update-slice_fusion.2
  53.3 0.7 bitcast_dynamic-update-slice_fusion.1
  54.0 1.9 fusion.1
  55.9 1.0 copy.25
  56.9 20.5 %all-to-all-start.1 = ((bf16[64,8,448]{2,1,0:T(8,128)(2,1)}), bf16[64,8,448]{2,1,0:T(8,128)(2,1)S(1)}, u32[]{:S(2)}, u32[]{:S(2)}) async-start(bf16[64,8,448]{2,1,0:T(8,128)(2,1)} %bitcast.14), calls=%async_computation.1 | async-start | bytes 1048576 | tf_op jit(solution)/shard_map/all_to_all | solution.py:37
  77.4 19.1 %all-to-all-done.1 = bf16[64,8,448]{2,1,0:T(8,128)(2,1)S(1)} async-done(((bf16[64,8,448]{2,1,0:T(8,128)(2,1)}), bf16[64,8,448]{2,1,0:T(8,128)(2,1)S(1)}, u32[]{:S(2)}, u32[]{:S(2)}) %all-to-all-start.1) | async-done | bytes 458784 | tf_op jit(solution)/shard_map/all_to_all | solution.py:37
  96.8 0.7 collective-permute-start.3
  97.6 0.2 convolution_convert_fusion.1
  97.9 1.0 broadcast_in_dim.60
  98.9 21.8 %all-to-all-start.2 = ((bf16[64,2,1792]{2,1,0:T(2,128)(2,1)}), bf16[64,2,1792]{2,1,0:T(2,128)(2,1)S(1)}, u32[]{:S(2)}, u32[]{:S(2)}) async-start(bf16[64,2,1792]{2,1,0:T(2,128)(2,1)} %bitcast.17), calls=%async_computation.2 | async-start | bytes 917504 | tf_op jit(solution)/shard_map/all_to_all | solution.py:65
  120.7 4.8 %copy.32 = bf16[224,8,2,512]{3,1,2,0:T(8,128)(2,1)} copy(bf16[224,8,2,512]{3,2,1,0:T(2,128)(2,1)} %bitcast.49) | data formatting | bytes 7340032
  125.6 10.6 %all-to-all-done.2 = bf16[64,2,1792]{2,1,0:T(2,128)(2,1)S(1)} async-done(((bf16[64,2,1792]{2,1,0:T(2,128)(2,1)}), bf16[64,2,1792]{2,1,0:T(2,128)(2,1)S(1)}, u32[]{:S(2)}, u32[]{:S(2)}) %all-to-all-start.2) | async-done | bytes 458784 | tf_op jit(solution)/shard_map/all_to_all | solution.py:65
  136.3 2.7 %convolution_convert_fusion.4 = bf16[128,1024]{1,0:T(8,128)(2,1)S(1)} fusion(bf16[128,1792]{1,0:T(8,128)(2,1)S(1)} %reshape.94, bf16[1792,1024]{1,0:T(8,128)(2,1)} %bitcast.48), kind=kOutput, calls=%fused_computation.6 | convolution fusion | flops 469893120 | bytes 4390912 | tf_op jit(solution)/shard_map/dot_general | solution.py:67
  139.0 13.3 %all_to_all.30 = bf16[4,32,1024]{2,1,0:T(8,128)(2,1)S(1)} all-to-all(bf16[4,32,1024]{2,1,0:T(8,128)(2,1)S(1)} %bitcast.51), channel_id=1, replica_groups=mesh['dp'=4,'yh'=4,'yl'=2,'xh'=4,'xl'=2,'tensor'=4] {'tensor'}, dimensions={0} | all-to-all | bytes 524288 | tf_op jit(solution)/shard_map/all_to_all | solution.py:69
  152.4 10.8 %all_to_all.31 = bf16[4,32,512]{2,1,0:T(8,128)(2,1)S(1)} all-to-all(bf16[4,32,512]{2,1,0:T(8,128)(2,1)S(1)} %broadcast_in_dim.61), channel_id=1, replica_groups=mesh['dp'=4,'yh'=4,'yl'=2,'xh'=4,'xl'=2,'tensor'=4] {'tensor'}, dimensions={0} | all-to-all | bytes 262144 | tf_op jit(solution)/shard_map/all_to_all | solution.py:74
  163.2 0.4 convolution_convert_fusion
  163.6 0.5 copy.28
  164.1 20.5 %all_to_all.32 = bf16[64,2,1792]{2,1,0:T(2,128)(2,1)S(1)} all-to-all(bf16[64,2,1792]{2,1,0:T(2,128)(2,1)S(1)} %copy.28), channel_id=1, replica_groups=mesh['dp'=4,'yh'=4,'yl'=2,'xh'=4,'xl'=2,'tensor'=4] {'yh','yl','xh','xl'}, dimensions={0} | all-to-all | bytes 917504 | tf_op jit(solution)/shard_map/all_to_all | solution.py:82
  184.6 0.4 convert_reduce_fusion
  185.2 0.8 convolution_convert_fusion.2
  186.0 0.6 copy.40
  (24 shorter events, 1.0 us)
Async XLA Ops:
  0.6 162.6 %copy-start = (bf16[1,512,1792]{2,1,0:T(8,128)(2,1)S(1)}, bf16[1,512,1792]{2,1,0:T(8,128)(2,1)}, u32[]{:S(2)}) copy-start(bf16[1,512,1792]{2,1,0:T(8,128)(2,1)} %param.10) | copy-start | bytes 5505028
  2.7 51.3 %all-to-all-start = ((bf16[64,8,1024]{2,1,0:T(8,128)(2,1)}), bf16[64,8,1024]{2,1,0:T(8,128)(2,1)S(1)}, u32[]{:S(2)}, u32[]{:S(2)}) async-start(bf16[64,8,1024]{2,1,0:T(8,128)(2,1)} %bitcast.11), calls=%async_computation | async-start | bytes 2097152 | tf_op jit(solution)/shard_map/all_to_all | solution.py:28
  22.1 24.7 %collective-permute-start = (bf16[112,1024]{1,0:T(8,128)(2,1)}, bf16[112,1024]{1,0:T(8,128)(2,1)S(1)}, u32[]{:S(2)}, u32[]{:S(2)}) collective-permute-start(bf16[112,1024]{1,0:T(8,128)(2,1)} %get-tuple-element.5), channel_id=1, source_target_pairs={{0,4},{4,0},{32,36},{36,32},{1,5},{5,1},{33,37},{37,33},{2,6},{6,2... | collective-permute-start | bytes 688136 | tf_op jit(solution)/shard_map/ppermute | solution.py:24
  24.5 28.8 %collective-permute-start.2 = (bf16[112,1024]{1,0:T(8,128)(2,1)}, bf16[112,1024]{1,0:T(8,128)(2,1)S(1)}, u32[]{:S(2)}, u32[]{:S(2)}) collective-permute-start(bf16[112,1024]{1,0:T(8,128)(2,1)} %get-tuple-element.4), channel_id=1, source_target_pairs={{0,36},{4,32},{32,4},{36,0},{1,37},{5,33},{33,5},{37,1},{2,38},{6,... | collective-permute-start | bytes 688136 | tf_op jit(solution)/shard_map/ppermute | solution.py:24
  28.9 22.8 %collective-permute-start.1 = (bf16[112,1024]{1,0:T(8,128)(2,1)}, bf16[112,1024]{1,0:T(8,128)(2,1)}, u32[]{:S(2)}, u32[]{:S(2)}) collective-permute-start(bf16[112,1024]{1,0:T(8,128)(2,1)} %get-tuple-element.6), channel_id=1, source_target_pairs={{0,32},{4,36},{32,0},{36,4},{1,33},{5,37},{33,1},{37,5},{2,34},{6,... | collective-permute-start | bytes 688136 | tf_op jit(solution)/shard_map/ppermute | solution.py:24
  34.1 63.4 %copy-start.1 = (s32[8,8]{1,0:T(8,128)S(1)}, s32[8,8]{1,0:T(8,128)}, u32[]{:S(2)}) copy-start(s32[8,8]{1,0:T(8,128)} %param.12) | copy-start | bytes 772
  34.1 63.4 %copy-start.2 = (s32[8,8]{1,0:T(8,128)S(1)}, s32[8,8]{1,0:T(8,128)}, u32[]{:S(2)}) copy-start(s32[8,8]{1,0:T(8,128)} %param.11) | copy-start | bytes 772
  34.1 63.4 %copy-start.3 = (f32[8,8]{1,0:T(8,128)S(1)}, f32[8,8]{1,0:T(8,128)}, u32[]{:S(2)}) copy-start(f32[8,8]{1,0:T(8,128)} %param.13) | copy-start | bytes 772
  56.9 39.6 %all-to-all-start.1 = ((bf16[64,8,448]{2,1,0:T(8,128)(2,1)}), bf16[64,8,448]{2,1,0:T(8,128)(2,1)S(1)}, u32[]{:S(2)}, u32[]{:S(2)}) async-start(bf16[64,8,448]{2,1,0:T(8,128)(2,1)} %bitcast.14), calls=%async_computation.1 | async-start | bytes 1048576 | tf_op jit(solution)/shard_map/all_to_all | solution.py:37
  96.8 0.8 collective-permute-start.3
  98.9 37.2 %all-to-all-start.2 = ((bf16[64,2,1792]{2,1,0:T(2,128)(2,1)}), bf16[64,2,1792]{2,1,0:T(2,128)(2,1)S(1)}, u32[]{:S(2)}, u32[]{:S(2)}) async-start(bf16[64,2,1792]{2,1,0:T(2,128)(2,1)} %bitcast.17), calls=%async_computation.2 | async-start | bytes 917504 | tf_op jit(solution)/shard_map/all_to_all | solution.py:65

commit v2 on v1

v2 whole, which is shorter than its diff:
```python
import jax
import jax.numpy as jnp
from jax import lax
from jax.experimental import pallas as pl
from jax.experimental.pallas import tpu as pltpu
from jax.sharding import Mesh, PartitionSpec as P

HSPLIT = 4
CAP = 2
EXPERT = ("yh", "yl", "xh", "xl")
TURNED = ("tensor", "yl", "xh", "xl")
BF16 = jnp.bfloat16
F32 = jnp.float32


def pack_kernel(where, attn_ref, w_ref, sent_ref, *refs):
    pieces, own_ref, (staged, sems) = refs[:3], refs[3], refs[4:]
    part = attn_ref.shape[1] // 4
    half = part // 2
    me, core = where[0], where[1]
    copies = []
    for d in range(1, 4):
        start = pl.multiple_of((me ^ d) * part + core * half, half)
        copies.append(
            pltpu.make_async_copy(w_ref.at[:, pl.ds(start, half)], pieces[d - 1], sems.at[d - 1])
        )
        copies[-1].start()
    start = pl.multiple_of(me * part, part)
    copies.append(pltpu.make_async_copy(w_ref.at[:, pl.ds(start, part)], own_ref, sems.at[7]))
    copies[-1].start()
    for yl in range(2):
        for x in range(8):
            m = yl * 2 + x % 2
            staged[yl * 8 + x] = attn_ref[:, m * part : (m + 1) * part]
    for yh in range(4):
        copies.append(
            pltpu.make_async_copy(staged, sent_ref.at[pl.ds(yh * 16, 16)], sems.at[3 + yh])
        )
        copies[-1].start()
    for copy in copies:
        copy.wait()


def pack(where, attn_out, w_cols):
    rows, depth = attn_out.shape
    cols, part = w_cols.shape[0], depth // 4
    return pl.pallas_call(
        pack_kernel,
        out_shape=[jax.ShapeDtypeStruct((64, rows, part), BF16)]
        + [jax.ShapeDtypeStruct((cols, part // 2), BF16)] * 3
        + [jax.ShapeDtypeStruct((cols, part), BF16)],
        in_specs=[
            pl.BlockSpec(memory_space=pltpu.SMEM),
            pl.BlockSpec(memory_space=pltpu.VMEM),
            pl.BlockSpec(memory_space=pl.ANY),
        ],
        out_specs=[pl.BlockSpec(memory_space=pl.ANY)] * 5,
        scratch_shapes=[pltpu.VMEM((16, rows, part), BF16), pltpu.SemaphoreType.DMA((8,))],
        compiler_params=pltpu.CompilerParams(vmem_limit_bytes=58 << 20),
        name="pack",
    )(where, attn_out, w_cols)


def partial_kernel(where, tokens, own, *refs):
    mine, other, (out_ref, wide, sems) = refs[:3], refs[3:6], refs[6:]
    cols, half = mine[0].shape
    me, core = where[0], where[1]
    copies = []

    def bring(src, d, lane, width):
        row = pl.multiple_of((me ^ d) * cols, 16)
        copies.append(
            pltpu.make_async_copy(
                src, wide.at[pl.ds(row, cols), pl.ds(lane, width)], sems.at[len(copies)]
            )
        )
        copies[-1].start()

    bring(own, 0, 0, 2 * half)
    for d in range(1, 4):
        bring(mine[d - 1], d, pl.multiple_of(core * half, half), half)
        bring(other[d - 1], d, pl.multiple_of((1 - core) * half, half), half)
    for copy in copies:
        copy.wait()
    step = 128
    for i in range(tokens.shape[0] // step):
        at = pl.ds(i * step, step)
        out_ref[at, :] = lax.dot_general(
            tokens[at, :], wide[...], (((1,), (1,)), ((), ())), preferred_element_type=F32
        ).astype(BF16)


def partial_sums(where, tokens, own, mine, other):
    cols = own.shape[0]
    return pl.pallas_call(
        partial_kernel,
        out_shape=jax.ShapeDtypeStruct((tokens.shape[0], 4 * cols), BF16),
        in_specs=[
            pl.BlockSpec(memory_space=pltpu.SMEM),
            pl.BlockSpec(memory_space=pltpu.VMEM),
            pl.BlockSpec(memory_space=pl.ANY),
        ]
        + [pl.BlockSpec(memory_space=pl.ANY)] * 6,
        out_specs=pl.BlockSpec(memory_space=pltpu.VMEM),
        scratch_shapes=[
            pltpu.VMEM((4 * cols, tokens.shape[1]), BF16),
            pltpu.SemaphoreType.DMA((7,)),
        ],
        compiler_params=pltpu.CompilerParams(vmem_limit_bytes=8 << 20),
        name="partial_sums",
    )(where, tokens, own, *mine, *other)


def project(attn_out, w_proj):
    rows = attn_out.shape[0]
    cols = w_proj.shape[1]
    w_cols = w_proj.T
    where = jnp.stack([lax.axis_index(("yl", "xl")), lax.axis_index("core")]).astype(jnp.int32)
    sent, *pieces, own = pack(where, attn_out, w_cols)
    tokens = lax.all_to_all(sent, EXPERT, split_axis=0, concat_axis=0, tiled=True)
    mine = [
        lax.ppermute(pieces[d - 1], ("yl", "xl"), [(i, i ^ d) for i in range(4)])
        for d in range(1, 4)
    ]
    other = [lax.ppermute(piece, "core", [(0, 1), (1, 0)]) for piece in mine]
    partial = partial_sums(where, tokens.reshape(64 * rows, -1), own, mine, other)
    got = lax.all_to_all(
        partial.reshape(64, rows, 4 * cols), TURNED, split_axis=0, concat_axis=0, tiled=True
    )
    got = got.reshape(4, 2, 4, 2, rows, 4 * cols).astype(F32)
    total = jnp.sum(got, axis=(0, 1, 3)).astype(BF16)
    total = total.reshape(4, rows, 2, 2, cols).transpose(1, 2, 0, 3, 4).reshape(rows, 16 * cols)
    return lax.ppermute(
        total, ("yh", "tensor"), [(a * 4 + b, b * 4 + a) for a in range(4) for b in range(4)]
    )


def per_device(attn_out, w_proj, w_in, w_out, expert_ids, slots, gates):
    groups = lax.axis_size(EXPERT)
    width_block = w_in.shape[1]
    slice_units = w_in.shape[3]
    row = jnp.arange(groups * CAP, dtype=jnp.int32)
    matches = (expert_ids[:, :, None] == row // (HSPLIT * CAP)) & (slots[:, :, None] == row % CAP)
    dispatch_w = jnp.sum(matches.astype(F32), axis=1).astype(BF16)
    combine_w = jnp.sum(jnp.where(matches, gates[:, :, None], F32(0.0)), axis=1)
    combine_hi = lax.reduce_precision(combine_w, 8, 7)
    combine_w = jnp.concatenate([combine_hi, combine_w - combine_hi], axis=0).astype(BF16)
    projected = project(attn_out, w_proj)
    outgoing = jnp.einsum(
        "tgc,td->gcd",
        dispatch_w.reshape(-1, groups, CAP),
        projected,
        preferred_element_type=F32,
    ).astype(BF16)
    gate_up_w = w_in.reshape(width_block, 2 * slice_units)
    down_w = w_out.reshape(slice_units, width_block)
    received = lax.all_to_all(outgoing, EXPERT, split_axis=0, concat_axis=0, tiled=True)
    flat_rows = received.reshape(groups * CAP, width_block)
    gate_up = jnp.dot(flat_rows, gate_up_w, preferred_element_type=F32).astype(BF16)
    quarter = groups * CAP // 4
    gate_up = lax.all_to_all(
        gate_up.reshape(4, quarter, 2 * slice_units), "tensor", split_axis=0, concat_axis=0, tiled=True
    )
    gate_up = jnp.sum(gate_up.astype(F32), axis=0)
    hidden = (jax.nn.silu(gate_up[:, :slice_units]) * gate_up[:, slice_units:]).astype(BF16)
    hidden = lax.all_to_all(
        jnp.broadcast_to(hidden[None], (4, quarter, slice_units)),
        "tensor",
        split_axis=0,
        concat_axis=0,
        tiled=True,
    ).reshape(groups * CAP, slice_units)
    result = jnp.dot(hidden, down_w, preferred_element_type=F32)
    returned = lax.all_to_all(
        result.reshape(groups, CAP, width_block).astype(BF16),
        EXPERT,
        split_axis=0,
        concat_axis=0,
        tiled=True,
    ).reshape(groups * CAP, width_block)
    moe_out = jnp.dot(combine_w, returned, preferred_element_type=F32)
    moe_out = jnp.sum(moe_out.reshape(2, -1, width_block), axis=0)
    return (projected, moe_out.astype(BF16))


def solution(mesh):
    split = Mesh(
        mesh.devices.reshape(2, 2, 4, 2, 4, 2, 4),
        ("plane", "core", "yh", "yl", "xh", "xl", "tensor"),
    )
    rows = ("plane", "core") + EXPERT
    placed = (
        P(rows, "tensor"),
        P("tensor", EXPERT),
        P(EXPERT, "tensor", None, None),
        P(EXPERT, None, "tensor"),
        P(rows, None),
        P(rows, None),
        P(rows, None),
    )
    return jax.shard_map(
        per_device,
        mesh=split,
        in_specs=placed,
        out_specs=(P(rows, "tensor"), P(rows, "tensor")),
        check_vma=False,
    )
```

time: 187 us -> 209 us (1.12)
  Pallas kernels: 0 us -> 22.5 us
  blocking collectives: 44.5 us -> 24.3 us
  waiting for transfers between devices: 46.6 us -> 62.1 us
  starting transfers between devices: 69.4 us -> 81.8 us
  local copies, waits for them, and re-layouts: 18.6 us -> 11.8 us
    pallas_call x0 -> x2, Pallas kernels: none -> 22.5 us  [the longest x1 19.4 us: pack(): pl.pallas_call(pack_kernel, out_shape=[jax.ShapeDtypeStruct((64, rows, pa...]
    all_to_all x1 -> x0, blocking collectives: 20.5 us -> none  [per_device(): lax.all_to_all(result.reshape(groups, CAP, width_block).astype(BF16), EXP...]
    all_to_all x1 -> x2, waiting for transfers between devices: 0.01 us -> 14.9 us  [the longest x1 14.9 us: per_device(): lax.all_to_all(result.reshape(groups, CAP, width_block).astype(BF16), EXP...]
    ppermute x3 -> x6, starting transfers between devices: 9.2 us -> 15.4 us  [the longest x3 9.21 us: project(): lax.ppermute(pieces[d - 1], ('yl', 'xl'), [(i, i ^ d) for i in range(4)])]
    all_to_all x1 -> x2, starting transfers between devices: 17.3 us -> 22.1 us  [the longest x1 17.3 us: project(): lax.all_to_all(sent, EXPERT, split_axis=0, concat_axis=0, tiled=True)]
    dynamic_update_slice x4 -> x0, local copies, waits for them, and re-layouts: 4.72 us -> none  [project(): wide = lax.dynamic_update_slice(wide, blocks[d][None], (me ^ d, 0, 0))]
    broadcast_in_dim x4 -> x0, local copies, waits for them, and re-layouts: 4.25 us -> none  [the longest x1 2.07 us: project(): sent = jnp.broadcast_to(sent[None, :, None, :], (4, 2, 4, 2, rows, part))]
    unnamed x10 -> x18, local copies, waits for them, and re-layouts: 5.46 us -> 8.55 us
  transfers between devices with their start and end apart: 7 -> 11, of which waited for: 4 -> 6; matrix products, arithmetic and copies ran while one was open for 7% -> 2% of each run, Pallas kernels for 0% -> 0%
where the time goes in v2:
time: 209 us; the launch traced here: 208 us
  starting transfers between devices  81.8 us (39%)
  waiting for transfers between devices  62.1 us (30%)
  blocking collectives  24.3 us (12%)
  Pallas kernels  22.5 us (11%)
  local copies, waits for them, and re-layouts  11.8 us (6%)
  matrix products  4.15 us (2%)
    all_to_all x1, starting transfers between devices, per_device(): lax.all_to_all(outgoing, EXPERT, split_axis=0, concat_axis=0, tiled=True)  22.4 us
    all_to_all x1, starting transfers between devices, project(): lax.all_to_all(partial.reshape(64, rows, 4 * cols), TURNED, split_axis=0,...  21.2 us
    all_to_all x1, waiting for transfers between devices, project(): lax.all_to_all(partial.reshape(64, rows, 4 * cols), TURNED, split_axis=0,...  20.2 us
    pallas_call x1, Pallas kernels, pack(): pl.pallas_call(pack_kernel, out_shape=[jax.ShapeDtypeStruct((64, rows, pa...  19.4 us
    all_to_all x1, starting transfers between devices, project(): lax.all_to_all(sent, EXPERT, split_axis=0, concat_axis=0, tiled=True)  17.3 us
    ppermute x3, waiting for transfers between devices, project(): lax.ppermute(pieces[d - 1], ('yl', 'xl'), [(i, i ^ d) for i in range(4)])  15 us
    all_to_all x1, waiting for transfers between devices, per_device(): lax.all_to_all(result.reshape(groups, CAP, width_block).astype(BF16), EXP...  14.9 us
    all_to_all x1, blocking collectives, per_device(): lax.all_to_all(gate_up.reshape(4, quarter, 2 * slice_units), 'tensor', sp...  12.9 us
  transfers between devices with their start and end apart: 11, of which 6 were waited for; matrix products, arithmetic and copies ran while one was open for 2% of the time, Pallas kernels for 0%

profile of v2, /device:TPU:2, one launch (start us, length us, event | category | flops | bytes accessed | tf_op | source)
XLA Modules:
  0.0 208.5 jit_solution(1794875118121840937)
XLA Ops:
  0.7 0.6 pad_add_fusion.where
  1.3 19.4 %pack.1 = (bf16[64,8,1024]{2,1,0:T(8,128)(2,1)}, bf16[112,512]{1,0:T(8,128)(2,1)}, bf16[112,512]{1,0:T(8,128)(2,1)}, bf16[112,512]{1,0:T(8,128)(2,1)}, bf16[112,1024]{1,0:T(8,128)(2,1)}) custom-call(s32[2]{0:T(128)} %pad_add_fusion.where, bf16[8,4096]{1,0:T(8,128)(2,1)} %attn_ref.1, bf16[112,4096]{1,0:T(8,128)(2,1)} %bitcast.30), custom_call_target="tpu_custom_call" | custom-call | tf_op jit(solution)/shard_map/pack/pallas_call | solution.py:47
  20.7 17.3 %all-to-all-start = ((bf16[64,8,1024]{2,1,0:T(8,128)(2,1)}), bf16[64,8,1024]{2,1,0:T(8,128)(2,1)S(1)}, u32[]{:S(2)}, u32[]{:S(2)}) async-start(bf16[64,8,1024]{2,1,0:T(8,128)(2,1)} %get-tuple-element.7), calls=%async_computation | async-start | bytes 2097152 | tf_op jit(solution)/shard_map/all_to_all | solution.py:120
  38.0 2.5 %collective-permute-start = (bf16[112,512]{1,0:T(8,128)(2,1)}, bf16[112,512]{1,0:T(8,128)(2,1)S(1)}, u32[]{:S(2)}, u32[]{:S(2)}) collective-permute-start(bf16[112,512]{1,0:T(8,128)(2,1)} %get-tuple-element.9), channel_id=1, source_target_pairs={{0,4},{4,0},{32,36},{36,32},{1,5},{5,1},{33,37},{37,33},{2,6},{6,2... | collective-permute-start | bytes 344072 | tf_op jit(solution)/shard_map/ppermute | solution.py:122
  40.5 3.4 %collective-permute-start.1 = (bf16[112,512]{1,0:T(8,128)(2,1)}, bf16[112,512]{1,0:T(8,128)(2,1)S(1)}, u32[]{:S(2)}, u32[]{:S(2)}) collective-permute-start(bf16[112,512]{1,0:T(8,128)(2,1)} %get-tuple-element.10), channel_id=1, source_target_pairs={{0,32},{4,36},{32,0},{36,4},{1,33},{5,37},{33,1},{37,5},{2,34},{6,... | collective-permute-start | bytes 344072 | tf_op jit(solution)/shard_map/ppermute | solution.py:122
  43.9 3.3 %collective-permute-start.2 = (bf16[112,512]{1,0:T(8,128)(2,1)}, bf16[112,512]{1,0:T(8,128)(2,1)S(1)}, u32[]{:S(2)}, u32[]{:S(2)}) collective-permute-start(bf16[112,512]{1,0:T(8,128)(2,1)} %get-tuple-element.11), channel_id=1, source_target_pairs={{0,36},{4,32},{32,4},{36,0},{1,37},{5,33},{33,5},{37,1},{2,38},{6,... | collective-permute-start | bytes 344072 | tf_op jit(solution)/shard_map/ppermute | solution.py:122
  47.2 13.3 %collective-permute-done.refs_0_ = bf16[112,512]{1,0:T(8,128)(2,1)S(1)} collective-permute-done((bf16[112,512]{1,0:T(8,128)(2,1)}, bf16[112,512]{1,0:T(8,128)(2,1)S(1)}, u32[]{:S(2)}, u32[]{:S(2)}) %collective-permute-start) | collective-permute-done | bytes 114720 | tf_op jit(solution)/shard_map/ppermute | solution.py:122
  60.5 1.9 collective-permute-start.3
  62.4 1.8 collective-permute-done.1.refs_1_
  64.2 1.9 collective-permute-start.4
  66.1 2.4 %collective-permute-start.5 = (bf16[112,512]{1,0:T(8,128)(2,1)S(1)}, bf16[112,512]{1,0:T(8,128)(2,1)S(1)}, u32[]{:S(2)}, u32[]{:S(2)}) collective-permute-start(bf16[112,512]{1,0:T(8,128)(2,1)S(1)} %collective-permute-done.2.refs_2_), channel_id=1, source_target_pairs={{0,256},{256,0},{1,257},{257,1},{2,258},{258,2},{3,259},{259,3},{4... | collective-permute-start | bytes 344072 | tf_op jit(solution)/shard_map/ppermute | solution.py:125
  68.5 0.9 collective-permute-done.5.refs_5_
  69.5 0.6 copy-done.2
  70.1 0.9 copy-done.1
  71.0 0.9 copy-done.3
  71.9 0.6 copy-done.4
  72.5 3.0 %partial_sums.1 = bf16[512,448]{1,0:T(8,128)(2,1)} custom-call(s32[2]{0:T(128)S(1)} %copy-done.4, bf16[512,1024]{1,0:T(8,128)(2,1)S(1)} %bitcast.25, bf16[112,1024]{1,0:T(8,128)(2,1)S(1)} %copy-done.1, bf16[112,512]{1,0:T(8,128)(2,1)S(1)} %collective-permute-done.refs_0_, bf16[112,512]{1,0:T(8,128)(2,1)S(1)} %collective-permute-done.1.refs_1_, ...), custom_call_target="tpu_custom_call" | custom-call | tf_op jit(solution)/shard_map/partial_sums/pallas_call | solution.py:95
  75.6 21.2 %all-to-all-start.1 = ((bf16[64,8,448]{2,1,0:T(8,128)(2,1)}), bf16[64,8,448]{2,1,0:T(8,128)(2,1)S(1)}, u32[]{:S(2)}, u32[]{:S(2)}) async-start(bf16[64,8,448]{2,1,0:T(8,128)(2,1)} %bitcast.4), calls=%async_computation.1 | async-start | bytes 1048576 | tf_op jit(solution)/shard_map/all_to_all | solution.py:127
  96.8 20.2 %all-to-all-done.1 = bf16[64,8,448]{2,1,0:T(8,128)(2,1)S(1)} async-done(((bf16[64,8,448]{2,1,0:T(8,128)(2,1)}), bf16[64,8,448]{2,1,0:T(8,128)(2,1)S(1)}, u32[]{:S(2)}, u32[]{:S(2)}) %all-to-all-start.1) | async-done | bytes 458784 | tf_op jit(solution)/shard_map/all_to_all | solution.py:127
  117.3 0.7 collective-permute-start.6
  118.5 1.2 copy.22
  119.7 22.4 %all-to-all-start.2 = ((bf16[64,2,1792]{2,1,0:T(2,128)(2,1)}), bf16[64,2,1792]{2,1,0:T(2,128)(2,1)S(1)}, u32[]{:S(2)}, u32[]{:S(2)}) async-start(bf16[64,2,1792]{2,1,0:T(2,128)(2,1)} %copy.22), calls=%async_computation.2 | async-start | bytes 917504 | tf_op jit(solution)/shard_map/all_to_all | solution.py:157
  142.2 4.8 %copy.25 = bf16[224,8,2,512]{3,1,2,0:T(8,128)(2,1)} copy(bf16[224,8,2,512]{3,2,1,0:T(2,128)(2,1)} %bitcast.27) | data formatting | bytes 7340032
  147.0 11.0 %all-to-all-done.2 = bf16[64,2,1792]{2,1,0:T(2,128)(2,1)S(1)} async-done(((bf16[64,2,1792]{2,1,0:T(2,128)(2,1)}), bf16[64,2,1792]{2,1,0:T(2,128)(2,1)S(1)}, u32[]{:S(2)}, u32[]{:S(2)}) %all-to-all-start.2) | async-done | bytes 458784 | tf_op jit(solution)/shard_map/all_to_all | solution.py:157
  158.2 2.7 %convolution_convert_fusion.2 = bf16[128,1024]{1,0:T(8,128)(2,1)S(1)} fusion(bf16[128,1792]{1,0:T(8,128)(2,1)S(1)} %reshape.82, bf16[1792,1024]{1,0:T(8,128)(2,1)} %bitcast.26), kind=kOutput, calls=%fused_computation.3 | convolution fusion | flops 469893120 | bytes 4390912 | tf_op jit(solution)/shard_map/dot_general | solution.py:159
  160.9 12.9 %all_to_all.30 = bf16[4,32,1024]{2,1,0:T(8,128)(2,1)S(1)} all-to-all(bf16[4,32,1024]{2,1,0:T(8,128)(2,1)S(1)} %bitcast.29), channel_id=1, replica_groups=mesh['plane'=2,'core'=2,'yh'=4,'yl'=2,'xh'=4,'xl'=2,'tensor'=4] {'tensor'}, dimensions={0} | all-to-all | bytes 524288 | tf_op jit(solution)/shard_map/all_to_all | solution.py:161
  173.9 11.5 %all_to_all.31 = bf16[4,32,512]{2,1,0:T(8,128)(2,1)S(1)} all-to-all(bf16[4,32,512]{2,1,0:T(8,128)(2,1)S(1)} %broadcast_in_dim.16), channel_id=1, replica_groups=mesh['plane'=2,'core'=2,'yh'=4,'yl'=2,'xh'=4,'xl'=2,'tensor'=4] {'tensor'}, dimensions={0} | all-to-all | bytes 262144 | tf_op jit(solution)/shard_map/all_to_all | solution.py:166
  185.8 1.3 copy.24
  187.1 4.8 %all-to-all-start.5 = ((bf16[64,2,1792]{2,1,0:T(2,128)(2,1)}), bf16[64,2,1792]{2,1,0:T(2,128)(2,1)S(1)}, u32[]{:S(2)}, u32[]{:S(2)}) async-start(bf16[64,2,1792]{2,1,0:T(2,128)(2,1)} %copy.24), calls=%async_computation.5 | async-start | bytes 917504 | tf_op jit(solution)/shard_map/all_to_all | solution.py:174
  191.9 14.9 %all-to-all-done.5 = bf16[64,2,1792]{2,1,0:T(2,128)(2,1)S(1)} async-done(((bf16[64,2,1792]{2,1,0:T(2,128)(2,1)}), bf16[64,2,1792]{2,1,0:T(2,128)(2,1)S(1)}, u32[]{:S(2)}, u32[]{:S(2)}) %all-to-all-start.5) | async-done | bytes 458784 | tf_op jit(solution)/shard_map/all_to_all | solution.py:174
  207.1 0.8 convolution_reduce_fusion
  207.9 0.6 copy.31
  (33 shorter events, 1.7 us)
Async XLA Ops:
  0.6 184.8 %copy-start = (bf16[1,512,1792]{2,1,0:T(8,128)(2,1)S(1)}, bf16[1,512,1792]{2,1,0:T(8,128)(2,1)}, u32[]{:S(2)}) copy-start(bf16[1,512,1792]{2,1,0:T(8,128)(2,1)} %param.10) | copy-start | bytes 5505028
  1.2 116.7 %copy-start.5 = (f32[8,8]{1,0:T(8,128)S(1)}, f32[8,8]{1,0:T(8,128)}, u32[]{:S(2)}) copy-start(f32[8,8]{1,0:T(8,128)} %param.13) | copy-start | bytes 772
  1.2 116.8 %copy-start.6 = (s32[8,8]{1,0:T(8,128)S(1)}, s32[8,8]{1,0:T(8,128)}, u32[]{:S(2)}) copy-start(s32[8,8]{1,0:T(8,128)} %param.12) | copy-start | bytes 772
  1.2 116.8 %copy-start.7 = (s32[8,8]{1,0:T(8,128)S(1)}, s32[8,8]{1,0:T(8,128)}, u32[]{:S(2)}) copy-start(s32[8,8]{1,0:T(8,128)} %param.11) | copy-start | bytes 772
  20.7 49.4 %all-to-all-start = ((bf16[64,8,1024]{2,1,0:T(8,128)(2,1)}), bf16[64,8,1024]{2,1,0:T(8,128)(2,1)S(1)}, u32[]{:S(2)}, u32[]{:S(2)}) async-start(bf16[64,8,1024]{2,1,0:T(8,128)(2,1)} %get-tuple-element.7), calls=%async_computation | async-start | bytes 2097152 | tf_op jit(solution)/shard_map/all_to_all | solution.py:120
  38.0 22.5 %collective-permute-start = (bf16[112,512]{1,0:T(8,128)(2,1)}, bf16[112,512]{1,0:T(8,128)(2,1)S(1)}, u32[]{:S(2)}, u32[]{:S(2)}) collective-permute-start(bf16[112,512]{1,0:T(8,128)(2,1)} %get-tuple-element.9), channel_id=1, source_target_pairs={{0,4},{4,0},{32,36},{36,32},{1,5},{5,1},{33,37},{37,33},{2,6},{6,2... | collective-permute-start | bytes 344072 | tf_op jit(solution)/shard_map/ppermute | solution.py:122
  40.5 23.7 %collective-permute-start.1 = (bf16[112,512]{1,0:T(8,128)(2,1)}, bf16[112,512]{1,0:T(8,128)(2,1)S(1)}, u32[]{:S(2)}, u32[]{:S(2)}) collective-permute-start(bf16[112,512]{1,0:T(8,128)(2,1)} %get-tuple-element.10), channel_id=1, source_target_pairs={{0,32},{4,36},{32,0},{36,4},{1,33},{5,37},{33,1},{37,5},{2,34},{6,... | collective-permute-start | bytes 344072 | tf_op jit(solution)/shard_map/ppermute | solution.py:122
  43.9 22.2 %collective-permute-start.2 = (bf16[112,512]{1,0:T(8,128)(2,1)}, bf16[112,512]{1,0:T(8,128)(2,1)S(1)}, u32[]{:S(2)}, u32[]{:S(2)}) collective-permute-start(bf16[112,512]{1,0:T(8,128)(2,1)} %get-tuple-element.11), channel_id=1, source_target_pairs={{0,36},{4,32},{32,4},{36,0},{1,37},{5,33},{33,5},{37,1},{2,38},{6,... | collective-permute-start | bytes 344072 | tf_op jit(solution)/shard_map/ppermute | solution.py:122
  60.5 8.0 %collective-permute-start.3 = (bf16[112,512]{1,0:T(8,128)(2,1)S(1)}, bf16[112,512]{1,0:T(8,128)(2,1)S(1)}, u32[]{:S(2)}, u32[]{:S(2)}) collective-permute-start(bf16[112,512]{1,0:T(8,128)(2,1)S(1)} %collective-permute-done.refs_0_), channel_id=1, source_target_pairs={{0,256},{256,0},{1,257},{257,1},{2,258},{258,2},{3,259},{259,3},{4... | collective-permute-start | bytes 344072 | tf_op jit(solution)/shard_map/ppermute | solution.py:125
  64.2 4.4 %collective-permute-start.4 = (bf16[112,512]{1,0:T(8,128)(2,1)S(1)}, bf16[112,512]{1,0:T(8,128)(2,1)S(1)}, u32[]{:S(2)}, u32[]{:S(2)}) collective-permute-start(bf16[112,512]{1,0:T(8,128)(2,1)S(1)} %collective-permute-done.1.refs_1_), channel_id=1, source_target_pairs={{0,256},{256,0},{1,257},{257,1},{2,258},{258,2},{3,259},{259,3},{4... | collective-permute-start | bytes 344072 | tf_op jit(solution)/shard_map/ppermute | solution.py:125
  66.1 3.4 %collective-permute-start.5 = (bf16[112,512]{1,0:T(8,128)(2,1)S(1)}, bf16[112,512]{1,0:T(8,128)(2,1)S(1)}, u32[]{:S(2)}, u32[]{:S(2)}) collective-permute-start(bf16[112,512]{1,0:T(8,128)(2,1)S(1)} %collective-permute-done.2.refs_2_), channel_id=1, source_target_pairs={{0,256},{256,0},{1,257},{257,1},{2,258},{258,2},{3,259},{259,3},{4... | collective-permute-start | bytes 344072 | tf_op jit(solution)/shard_map/ppermute | solution.py:125
  69.5 0.6 copy-start.2
  70.1 0.9 copy-start.1
  71.0 0.9 copy-start.3
  71.9 0.6 copy-start.4
  75.6 41.4 %all-to-all-start.1 = ((bf16[64,8,448]{2,1,0:T(8,128)(2,1)}), bf16[64,8,448]{2,1,0:T(8,128)(2,1)S(1)}, u32[]{:S(2)}, u32[]{:S(2)}) async-start(bf16[64,8,448]{2,1,0:T(8,128)(2,1)} %bitcast.4), calls=%async_computation.1 | async-start | bytes 1048576 | tf_op jit(solution)/shard_map/all_to_all | solution.py:127
  117.3 0.9 collective-permute-start.6
  119.7 38.3 %all-to-all-start.2 = ((bf16[64,2,1792]{2,1,0:T(2,128)(2,1)}), bf16[64,2,1792]{2,1,0:T(2,128)(2,1)S(1)}, u32[]{:S(2)}, u32[]{:S(2)}) async-start(bf16[64,2,1792]{2,1,0:T(2,128)(2,1)} %copy.22), calls=%async_computation.2 | async-start | bytes 917504 | tf_op jit(solution)/shard_map/all_to_all | solution.py:157
  187.1 19.8 %all-to-all-start.5 = ((bf16[64,2,1792]{2,1,0:T(2,128)(2,1)}), bf16[64,2,1792]{2,1,0:T(2,128)(2,1)S(1)}, u32[]{:S(2)}, u32[]{:S(2)}) async-start(bf16[64,2,1792]{2,1,0:T(2,128)(2,1)} %copy.24), calls=%async_computation.5 | async-start | bytes 917504 | tf_op jit(solution)/shard_map/all_to_all | solution.py:174

commit v3 on v1

v3 whole, which is shorter than its diff:
```python
import jax
import jax.numpy as jnp
from jax import lax
from jax.experimental import pallas as pl
from jax.experimental.pallas import tpu as pltpu
from jax.sharding import Mesh, PartitionSpec as P

HSPLIT = 4
CAP = 2
EXPERT = ("yh", "yl", "xh", "xl")
TURNED = ("tensor", "yl", "xh", "xl")
BF16 = jnp.bfloat16
F32 = jnp.float32


def pack_kernel(attn_ref, w_ref, sent_ref, pieces_ref, staged, sems):
    part = attn_ref.shape[1] // 4
    for m in range(4):
        block = attn_ref[:, m * part : (m + 1) * part]
        for x in range(4):
            staged[(m // 2) * 8 + x * 2 + m % 2] = block
    copies = [
        pltpu.make_async_copy(staged, sent_ref.at[pl.ds(yh * 16, 16)], sems.at[yh])
        for yh in range(4)
    ]
    for copy in copies:
        copy.start()
    for m in range(4):
        pieces_ref[m] = w_ref[:, m * part : (m + 1) * part]
    for copy in copies:
        copy.wait()


def pack(attn_out, w_cols):
    rows, depth = attn_out.shape
    cols, part = w_cols.shape[0], depth // 4
    vmem = pl.BlockSpec(memory_space=pltpu.VMEM)
    return pl.pallas_call(
        pack_kernel,
        out_shape=[
            jax.ShapeDtypeStruct((64, rows, part), BF16),
            jax.ShapeDtypeStruct((4, cols, part), BF16),
        ],
        in_specs=[vmem, vmem],
        out_specs=[pl.BlockSpec(memory_space=pl.ANY), vmem],
        scratch_shapes=[pltpu.VMEM((16, rows, part), BF16), pltpu.SemaphoreType.DMA((4,))],
        compiler_params=pltpu.CompilerParams(vmem_limit_bytes=16 << 20),
        name="pack",
    )(attn_out, w_cols)


def partial_kernel(tokens, wide, out_ref):
    out_ref[...] = lax.dot_general(
        tokens[...], wide[...], (((1,), (1,)), ((), ())), preferred_element_type=F32
    ).astype(BF16)


def partial_sums(tokens, wide):
    vmem = pl.BlockSpec(memory_space=pltpu.VMEM)
    return pl.pallas_call(
        partial_kernel,
        out_shape=jax.ShapeDtypeStruct((tokens.shape[0], wide.shape[0]), BF16),
        in_specs=[vmem, vmem],
        out_specs=vmem,
        compiler_params=pltpu.CompilerParams(vmem_limit_bytes=16 << 20),
        name="partial_sums",
    )(tokens, wide)


def project(attn_out, w_proj, gate_up_w):
    rows, cols = attn_out.shape[0], w_proj.shape[1]
    sent, pieces = pack(attn_out, w_proj.T)
    wide = lax.all_to_all(pieces, ("yl", "xl"), split_axis=0, concat_axis=0, tiled=True)
    sent, wide = lax.optimization_barrier((sent, wide))
    tokens = lax.all_to_all(sent, EXPERT, split_axis=0, concat_axis=0, tiled=True)
    tokens, gate_up_w = lax.optimization_barrier((tokens, gate_up_w))
    partial = partial_sums(tokens.reshape(64 * rows, -1), wide.reshape(4 * cols, -1))
    got = lax.all_to_all(
        partial.reshape(64, rows, 4 * cols), TURNED, split_axis=0, concat_axis=0, tiled=True
    )
    got = got.reshape(4, 2, 4, 2, rows, 4 * cols).astype(F32)
    total = jnp.sum(got, axis=(0, 1, 3)).astype(BF16)
    total = total.reshape(4, rows, 2, 2, cols).transpose(1, 2, 0, 3, 4).reshape(rows, 16 * cols)
    turned = lax.ppermute(
        total, ("yh", "tensor"), [(a * 4 + b, b * 4 + a) for a in range(4) for b in range(4)]
    )
    return turned, gate_up_w


def per_device(attn_out, w_proj, w_in, w_out, expert_ids, slots, gates):
    groups = lax.axis_size(EXPERT)
    width_block = w_in.shape[1]
    slice_units = w_in.shape[3]
    row = jnp.arange(groups * CAP, dtype=jnp.int32)
    matches = (expert_ids[:, :, None] == row // (HSPLIT * CAP)) & (slots[:, :, None] == row % CAP)
    dispatch_w = jnp.sum(matches.astype(F32), axis=1).astype(BF16)
    combine_w = jnp.sum(jnp.where(matches, gates[:, :, None], F32(0.0)), axis=1)
    projected, gate_up_w = project(attn_out, w_proj, w_in.reshape(width_block, 2 * slice_units))
    outgoing = jnp.einsum(
        "tgc,td->gcd",
        dispatch_w.reshape(-1, groups, CAP),
        projected,
        preferred_element_type=F32,
    ).astype(BF16)
    down_w = w_out.reshape(slice_units, width_block)
    received = lax.all_to_all(outgoing, EXPERT, split_axis=0, concat_axis=0, tiled=True)
    flat_rows = received.reshape(groups * CAP, width_block)
    gate_up = jnp.dot(flat_rows, gate_up_w, preferred_element_type=F32).astype(BF16)
    quarter = groups * CAP // 4
    gate_up = lax.all_to_all(
        gate_up.reshape(4, quarter, 2 * slice_units), "tensor", split_axis=0, concat_axis=0, tiled=True
    )
    gate_up = jnp.sum(gate_up.astype(F32), axis=0)
    hidden = (jax.nn.silu(gate_up[:, :slice_units]) * gate_up[:, slice_units:]).astype(BF16)
    hidden = lax.all_to_all(
        jnp.broadcast_to(hidden[None], (4, quarter, slice_units)),
        "tensor",
        split_axis=0,
        concat_axis=0,
        tiled=True,
    ).reshape(groups * CAP, slice_units)
    result = jnp.dot(hidden, down_w, preferred_element_type=F32)
    returned = lax.all_to_all(
        result.reshape(groups, CAP, width_block).astype(BF16),
        EXPERT,
        split_axis=0,
        concat_axis=0,
        tiled=True,
    ).reshape(groups * CAP, width_block)
    moe_out = jnp.dot(
        combine_w, returned.astype(F32), precision=lax.Precision.HIGHEST, preferred_element_type=F32
    )
    return (projected, moe_out.astype(BF16))


def solution(mesh):
    split = Mesh(
        mesh.devices.reshape(2, 2, 4, 2, 4, 2, 4),
        ("plane", "core", "yh", "yl", "xh", "xl", "tensor"),
    )
    rows = ("plane", "core") + EXPERT
    placed = (
        P(rows, "tensor"),
        P("tensor", EXPERT),
        P(EXPERT, "tensor", None, None),
        P(EXPERT, None, "tensor"),
        P(rows, None),
        P(rows, None),
        P(rows, None),
    )
    return jax.shard_map(
        per_device,
        mesh=split,
        in_specs=placed,
        out_specs=(P(rows, "tensor"), P(rows, "tensor")),
        check_vma=False,
    )
```

time: 187 us -> 187 us (level)
  blocking collectives: 44.5 us -> 103 us
  starting transfers between devices: 69.4 us -> 26.1 us
  local copies, waits for them, and re-layouts: 18.6 us -> 10.5 us
  waiting for transfers between devices: 46.6 us -> 40 us
    all_to_all x0 -> x2, blocking collectives: none -> 58.8 us  [the longest x1 34.4 us: per_device(): lax.all_to_all(outgoing, EXPERT, split_axis=0, concat_axis=0, tiled=True)]
    all_to_all x2 -> x1, starting transfers between devices: 39.1 us -> 5.27 us  [project(): lax.all_to_all(sent, EXPERT, split_axis=0, concat_axis=0, tiled=True)]
    ppermute x3 -> x0, waiting for transfers between devices: 16.9 us -> none  [project(): piece = lax.ppermute(piece, ('yl', 'xl'), [(i, i ^ d) for i in range(4)])]
    all_to_all x2 -> x1, waiting for transfers between devices: 10.6 us -> 23.5 us  [project(): lax.all_to_all(sent, EXPERT, split_axis=0, concat_axis=0, tiled=True)]
    ppermute x3 -> x0, starting transfers between devices: 9.2 us -> none  [project(): piece = lax.ppermute(piece, ('yl', 'xl'), [(i, i ^ d) for i in range(4)])]
    dynamic_update_slice x4 -> x0, local copies, waits for them, and re-layouts: 4.72 us -> none  [project(): wide = lax.dynamic_update_slice(wide, blocks[d][None], (me ^ d, 0, 0))]
    broadcast_in_dim x4 -> x0, local copies, waits for them, and re-layouts: 4.25 us -> none  [the longest x1 2.07 us: project(): sent = jnp.broadcast_to(sent[None, :, None, :], (4, 2, 4, 2, rows, part))]
    unnamed x10 -> x18, local copies, waits for them, and re-layouts: 5.46 us -> 8.8 us
  transfers between devices with their start and end apart: 7 -> 3, of which waited for: 4 -> 2; matrix products, arithmetic and copies ran while one was open for 7% -> 3% of each run, Pallas kernels for 0% -> 0%
where the time goes in v3:
time: 187 us; the launch traced here: 186 us
  blocking collectives  103 us (55%)
  waiting for transfers between devices  40 us (21%)
  starting transfers between devices  26.1 us (14%)
  local copies, waits for them, and re-layouts  10.5 us (6%)
  matrix products  4.26 us (2%)
    all_to_all x1, blocking collectives, per_device(): lax.all_to_all(outgoing, EXPERT, split_axis=0, concat_axis=0, tiled=True)  34.4 us
    all_to_all x1, blocking collectives, project(): lax.all_to_all(pieces, ('yl', 'xl'), split_axis=0, concat_axis=0, tiled=T...  24.4 us
    all_to_all x1, waiting for transfers between devices, project(): lax.all_to_all(sent, EXPERT, split_axis=0, concat_axis=0, tiled=True)  23.5 us
    all_to_all x1, starting transfers between devices, project(): lax.all_to_all(partial.reshape(64, rows, 4 * cols), TURNED, split_axis=0,...  20.2 us
    all_to_all x1, blocking collectives, per_device(): lax.all_to_all(result.reshape(groups, CAP, width_block).astype(BF16), EXP...  19.7 us
    all_to_all x1, waiting for transfers between devices, project(): lax.all_to_all(partial.reshape(64, rows, 4 * cols), TURNED, split_axis=0,...  16.6 us
    all_to_all x1, blocking collectives, per_device(): lax.all_to_all(gate_up.reshape(4, quarter, 2 * slice_units), 'tensor', sp...  12.9 us
    all_to_all x1, blocking collectives, per_device(): lax.all_to_all(jnp.broadcast_to(hidden[None], (4, quarter, slice_units)),...  11.4 us
  transfers between devices with their start and end apart: 3, of which 2 were waited for; matrix products, arithmetic and copies ran while one was open for 3% of the time, Pallas kernels for 0%

profile of v3, /device:TPU:2, one launch (start us, length us, event | category | flops | bytes accessed | tf_op | source)
XLA Modules:
  0.0 186.4 jit_solution(18179135983994889629)
XLA Ops:
  0.6 0.0 copy-start
  0.7 1.3 copy-done.3
  2.0 0.8 copy-done.4
  2.8 0.2 pack.1
  3.0 24.4 %all_to_all.35 = bf16[4,112,1024]{2,1,0:T(8,128)(2,1)} all-to-all(bf16[4,112,1024]{2,1,0:T(8,128)(2,1)S(1)} %get-tuple-element.9), channel_id=1, replica_groups=mesh['plane'=2,'core'=2,'yh'=4,'yl'=2,'xh'=4,'xl'=2,'tensor'=4] {'yl','xl'}, dimensions={0} | all-to-all | bytes 1835008 | tf_op jit(solution)/shard_map/all_to_all | solution.py:73
  27.4 5.3 %all-to-all-start.1 = ((bf16[64,8,1024]{2,1,0:T(8,128)(2,1)}), bf16[64,8,1024]{2,1,0:T(8,128)(2,1)S(1)}, u32[]{:S(2)}, u32[]{:S(2)}) async-start(bf16[64,8,1024]{2,1,0:T(8,128)(2,1)} %copy-done.2), calls=%async_computation.1 | async-start | bytes 2097152 | tf_op jit(solution)/shard_map/all_to_all | solution.py:75
  32.7 4.8 %copy.25 = bf16[224,8,2,512]{3,1,2,0:T(8,128)(2,1)} copy(bf16[224,8,2,512]{3,2,1,0:T(2,128)(2,1)} %bitcast.26) | data formatting | bytes 7340032
  37.6 23.5 %all-to-all-done.1 = bf16[64,8,1024]{2,1,0:T(8,128)(2,1)S(1)} async-done(((bf16[64,8,1024]{2,1,0:T(8,128)(2,1)}), bf16[64,8,1024]{2,1,0:T(8,128)(2,1)S(1)}, u32[]{:S(2)}, u32[]{:S(2)}) %all-to-all-start.1) | async-done | bytes 1048608 | tf_op jit(solution)/shard_map/all_to_all | solution.py:75
  61.1 1.2 copy-done.1
  62.2 1.5 partial_sums.1
  63.8 20.2 %all-to-all-start.2 = ((bf16[64,8,448]{2,1,0:T(8,128)(2,1)}), bf16[64,8,448]{2,1,0:T(8,128)(2,1)S(1)}, u32[]{:S(2)}, u32[]{:S(2)}) async-start(bf16[64,8,448]{2,1,0:T(8,128)(2,1)} %bitcast.3), calls=%async_computation.2 | async-start | bytes 1048576 | tf_op jit(solution)/shard_map/all_to_all | solution.py:78
  83.9 16.6 %all-to-all-done.2 = bf16[64,8,448]{2,1,0:T(8,128)(2,1)S(1)} async-done(((bf16[64,8,448]{2,1,0:T(8,128)(2,1)}), bf16[64,8,448]{2,1,0:T(8,128)(2,1)S(1)}, u32[]{:S(2)}, u32[]{:S(2)}) %all-to-all-start.2) | async-done | bytes 458784 | tf_op jit(solution)/shard_map/all_to_all | solution.py:78
  100.5 0.1 reduce_sum.39
  100.6 0.1 reshape.75
  100.7 0.1 reshape.76
  100.8 0.7 collective-permute-start
  101.5 0.1 convert_reduce_fusion.1
  101.6 0.1 copy.20
  101.8 0.2 convolution_convert_fusion.1
  102.0 0.5 copy.22
  102.5 34.4 %all_to_all.36 = bf16[64,2,1792]{2,1,0:T(2,128)(2,1)S(1)} all-to-all(bf16[64,2,1792]{2,1,0:T(2,128)(2,1)S(1)} %copy.22), channel_id=1, replica_groups=mesh['plane'=2,'core'=2,'yh'=4,'yl'=2,'xh'=4,'xl'=2,'tensor'=4] {'yh','y..., dimensions={0} | all-to-all | bytes 917504 | tf_op jit(solution)/shard_map/all_to_all | solution.py:106
  136.9 0.2 reshape.77
  137.1 2.7 %convolution_convert_fusion.3 = bf16[128,1024]{1,0:T(8,128)(2,1)S(1)} fusion(bf16[128,1792]{1,0:T(8,128)(2,1)S(1)} %reshape.77, bf16[1792,1024]{1,0:T(8,128)(2,1)} %bitcast.25), kind=kOutput, calls=%fused_computation.4 | convolution fusion | flops 469893120 | bytes 4390912 | tf_op jit(solution)/shard_map/dot_general | solution.py:108
  139.8 12.9 %all_to_all.37 = bf16[4,32,1024]{2,1,0:T(8,128)(2,1)S(1)} all-to-all(bf16[4,32,1024]{2,1,0:T(8,128)(2,1)S(1)} %bitcast.28), channel_id=1, replica_groups=mesh['plane'=2,'core'=2,'yh'=4,'yl'=2,'xh'=4,'xl'=2,'tensor'=4] {'tensor'}, dimensions={0} | all-to-all | bytes 524288 | tf_op jit(solution)/shard_map/all_to_all | solution.py:110
  152.7 11.4 %all_to_all.38 = bf16[4,32,512]{2,1,0:T(8,128)(2,1)S(1)} all-to-all(bf16[4,32,512]{2,1,0:T(8,128)(2,1)S(1)} %broadcast_in_dim.16), channel_id=1, replica_groups=mesh['plane'=2,'core'=2,'yh'=4,'yl'=2,'xh'=4,'xl'=2,'tensor'=4] {'tensor'}, dimensions={0} | all-to-all | bytes 262144 | tf_op jit(solution)/shard_map/all_to_all | solution.py:115
  164.1 0.1 dot_general.16
  164.2 0.4 convolution_convert_fusion
  164.6 0.5 copy.24
  165.1 19.7 %all_to_all.39 = bf16[64,2,1792]{2,1,0:T(2,128)(2,1)S(1)} all-to-all(bf16[64,2,1792]{2,1,0:T(2,128)(2,1)S(1)} %copy.24), channel_id=1, replica_groups=mesh['plane'=2,'core'=2,'yh'=4,'yl'=2,'xh'=4,'xl'=2,'tensor'=4] {'yh','y..., dimensions={0} | all-to-all | bytes 917504 | tf_op jit(solution)/shard_map/all_to_all | solution.py:123
  184.7 0.2 reshape.80
  184.9 0.9 convolution_convert_fusion.2
  185.8 0.6 copy.31
  (18 shorter events, 0.1 us)
Async XLA Ops:
  0.6 163.5 %copy-start = (bf16[1,512,1792]{2,1,0:T(8,128)(2,1)S(1)}, bf16[1,512,1792]{2,1,0:T(8,128)(2,1)}, u32[]{:S(2)}) copy-start(bf16[1,512,1792]{2,1,0:T(8,128)(2,1)} %param.10) | copy-start | bytes 5505028
  0.6 1.3 copy-start.3
  2.0 0.8 copy-start.4
  3.0 24.4 %copy-start.2 = (bf16[64,8,1024]{2,1,0:T(8,128)(2,1)}, bf16[64,8,1024]{2,1,0:T(8,128)(2,1)S(1)}, u32[]{:S(2)}) copy-start(bf16[64,8,1024]{2,1,0:T(8,128)(2,1)S(1)} %get-tuple-element.10) | copy-start | bytes 3145732
  27.4 33.6 %all-to-all-start.1 = ((bf16[64,8,1024]{2,1,0:T(8,128)(2,1)}), bf16[64,8,1024]{2,1,0:T(8,128)(2,1)S(1)}, u32[]{:S(2)}, u32[]{:S(2)}) async-start(bf16[64,8,1024]{2,1,0:T(8,128)(2,1)} %copy-done.2), calls=%async_computation.1 | async-start | bytes 2097152 | tf_op jit(solution)/shard_map/all_to_all | solution.py:75
  32.7 68.8 %copy-start.6 = (s32[8,8]{1,0:T(8,128)S(1)}, s32[8,8]{1,0:T(8,128)}, u32[]{:S(2)}) copy-start(s32[8,8]{1,0:T(8,128)} %param.11) | copy-start | bytes 772
  32.7 68.8 %copy-start.7 = (f32[8,8]{1,0:T(8,128)S(1)}, f32[8,8]{1,0:T(8,128)}, u32[]{:S(2)}) copy-start(f32[8,8]{1,0:T(8,128)} %param.13) | copy-start | bytes 772
  37.6 63.9 %copy-start.5 = (s32[8,8]{1,0:T(8,128)S(1)}, s32[8,8]{1,0:T(8,128)}, u32[]{:S(2)}) copy-start(s32[8,8]{1,0:T(8,128)} %param.12) | copy-start | bytes 772
  61.1 1.2 copy-start.1
  63.8 36.7 %all-to-all-start.2 = ((bf16[64,8,448]{2,1,0:T(8,128)(2,1)}), bf16[64,8,448]{2,1,0:T(8,128)(2,1)S(1)}, u32[]{:S(2)}, u32[]{:S(2)}) async-start(bf16[64,8,448]{2,1,0:T(8,128)(2,1)} %bitcast.3), calls=%async_computation.2 | async-start | bytes 1048576 | tf_op jit(solution)/shard_map/all_to_all | solution.py:78
  100.8 0.9 collective-permute-start

commit v4 on v3

--- a/solution.py
+++ b/solution.py
@@ -13,68 +13,104 @@
 F32 = jnp.float32
 
 
-def pack_kernel(attn_ref, w_ref, sent_ref, pieces_ref, staged, sems):
+VMEM = pl.BlockSpec(memory_space=pltpu.VMEM)
+SMEM = pl.BlockSpec(memory_space=pltpu.SMEM)
+ANY = pl.BlockSpec(memory_space=pl.ANY)
+
+
+def address_kernel(attn_ref, sent_ref, staged, in_sems, out_sems):
     part = attn_ref.shape[1] // 4
+    copies = []
     for m in range(4):
-        block = attn_ref[:, m * part : (m + 1) * part]
         for x in range(4):
-            staged[(m // 2) * 8 + x * 2 + m % 2] = block
+            at = (m // 2) * 8 + x * 2 + m % 2
+            copies.append(
+                pltpu.make_async_copy(
+                    attn_ref.at[:, pl.ds(m * part, part)], staged.at[at], in_sems.at[at]
+                )
+            )
+    for copy in copies:
+        copy.start()
+    for copy in copies:
+        copy.wait()
     copies = [
-        pltpu.make_async_copy(staged, sent_ref.at[pl.ds(yh * 16, 16)], sems.at[yh])
+        pltpu.make_async_copy(staged, sent_ref.at[pl.ds(yh * 16, 16)], out_sems.at[yh])
         for yh in range(4)
     ]
     for copy in copies:
         copy.start()
-    for m in range(4):
-        pieces_ref[m] = w_ref[:, m * part : (m + 1) * part]
     for copy in copies:
         copy.wait()
 
 
-def pack(attn_out, w_cols):
-    rows, depth = attn_out.shape
-    cols, part = w_cols.shape[0], depth // 4
-    vmem = pl.BlockSpec(memory_space=pltpu.VMEM)
+def address(attn_out):
+    rows, part = attn_out.shape[0], attn_out.shape[1] // 4
     return pl.pallas_call(
-        pack_kernel,
-        out_shape=[
-            jax.ShapeDtypeStruct((64, rows, part), BF16),
-            jax.ShapeDtypeStruct((4, cols, part), BF16),
+        address_kernel,
+        out_shape=jax.ShapeDtypeStruct((64, rows, part), BF16),
+        in_specs=[ANY],
+        out_specs=ANY,
+        scratch_shapes=[
+            pltpu.VMEM((16, rows, part), BF16),
+            pltpu.SemaphoreType.DMA((16,)),
+            pltpu.SemaphoreType.DMA((4,)),
         ],
-        in_specs=[vmem, vmem],
-        out_specs=[pl.BlockSpec(memory_space=pl.ANY), vmem],
-        scratch_shapes=[pltpu.VMEM((16, rows, part), BF16), pltpu.SemaphoreType.DMA((4,))],
-        compiler_params=pltpu.CompilerParams(vmem_limit_bytes=16 << 20),
-        name="pack",
-    )(attn_out, w_cols)
+        compiler_params=pltpu.CompilerParams(vmem_limit_bytes=58 << 20),
+        name="address",
+    )(attn_out)
 
 
-def partial_kernel(tokens, wide, out_ref):
+def cut_kernel(me, w_ref, *pieces):
+    part = pieces[0].shape[1]
+    for d in range(4):
+        start = pl.multiple_of((me[0] ^ d) * part, part)
+        pieces[d][...] = w_ref[:, pl.ds(start, part)]
+
+
+def cut(me, w_cols):
+    cols, part = w_cols.shape[0], w_cols.shape[1] // 4
+    return pl.pallas_call(
+        cut_kernel,
+        out_shape=[jax.ShapeDtypeStruct((cols, part), BF16)] * 4,
+        in_specs=[SMEM, VMEM],
+        out_specs=[VMEM] * 4,
+        compiler_params=pltpu.CompilerParams(vmem_limit_bytes=8 << 20),
+        name="cut",
+    )(me, w_cols)
+
+
+def partial_kernel(me, tokens, *refs):
+    blocks, (out_ref, wide) = refs[:4], refs[4:]
+    cols = blocks[0].shape[0]
+    for d in range(4):
+        wide[pl.ds(pl.multiple_of((me[0] ^ d) * cols, 16), cols), :] = blocks[d][...]
     out_ref[...] = lax.dot_general(
         tokens[...], wide[...], (((1,), (1,)), ((), ())), preferred_element_type=F32
     ).astype(BF16)
 
 
-def partial_sums(tokens, wide):
-    vmem = pl.BlockSpec(memory_space=pltpu.VMEM)
+def partial_sums(me, tokens, blocks):
+    cols, part = blocks[0].shape
     return pl.pallas_call(
         partial_kernel,
-        out_shape=jax.ShapeDtypeStruct((tokens.shape[0], wide.shape[0]), BF16),
-        in_specs=[vmem, vmem],
-        out_specs=vmem,
+        out_shape=jax.ShapeDtypeStruct((tokens.shape[0], 4 * cols), BF16),
+        in_specs=[SMEM] + [VMEM] * 5,
+        out_specs=VMEM,
+        scratch_shapes=[pltpu.VMEM((4 * cols, part), BF16)],
         compiler_params=pltpu.CompilerParams(vmem_limit_bytes=16 << 20),
         name="partial_sums",
-    )(tokens, wide)
+    )(me, tokens, *blocks)
 
 
 def project(attn_out, w_proj, gate_up_w):
     rows, cols = attn_out.shape[0], w_proj.shape[1]
-    sent, pieces = pack(attn_out, w_proj.T)
-    wide = lax.all_to_all(pieces, ("yl", "xl"), split_axis=0, concat_axis=0, tiled=True)
-    sent, wide = lax.optimization_barrier((sent, wide))
-    tokens = lax.all_to_all(sent, EXPERT, split_axis=0, concat_axis=0, tiled=True)
+    me = lax.axis_index(("yl", "xl")).reshape(1).astype(jnp.int32)
+    tokens = lax.all_to_all(address(attn_out), EXPERT, split_axis=0, concat_axis=0, tiled=True)
+    blocks = list(cut(me, w_proj.T))
+    for d in range(1, 4):
+        blocks[d] = lax.ppermute(blocks[d], ("yl", "xl"), [(i, i ^ d) for i in range(4)])
     tokens, gate_up_w = lax.optimization_barrier((tokens, gate_up_w))
-    partial = partial_sums(tokens.reshape(64 * rows, -1), wide.reshape(4 * cols, -1))
+    partial = partial_sums(me, tokens.reshape(64 * rows, -1), blocks)
     got = lax.all_to_all(
         partial.reshape(64, rows, 4 * cols), TURNED, split_axis=0, concat_axis=0, tiled=True
     )

time: 187 us -> 185 us (0.989)
  starting transfers between devices: 26.1 us -> 47.6 us
  blocking collectives: 103 us -> 82.4 us
  waiting for transfers between devices: 40 us -> 34.9 us
  Pallas kernels: 1.71 us -> 5.68 us
  local copies, waits for them, and re-layouts: 10.5 us -> 8.35 us
    all_to_all x1 -> x0, blocking collectives: 24.4 us -> none  [project(): lax.all_to_all(pieces, ('yl', 'xl'), split_axis=0, concat_axis=0, tiled=T...]
    all_to_all x1, starting transfers between devices: 5.27 us -> 17.3 us  [project(): lax.all_to_all(address(attn_out), EXPERT, split_axis=0, concat_axis=0, ti...]
    all_to_all x1, waiting for transfers between devices: 23.5 us -> 12.3 us  [project(): lax.all_to_all(address(attn_out), EXPERT, split_axis=0, concat_axis=0, ti...]
    ppermute x0 -> x3, starting transfers between devices: none -> 9.2 us  [project(): lax.ppermute(blocks[d], ('yl', 'xl'), [(i, i ^ d) for i in range(4)])]
    all_to_all x1, blocking collectives: 34.4 us -> 38.4 us  [per_device(): lax.all_to_all(outgoing, EXPERT, split_axis=0, concat_axis=0, tiled=True)]
    ppermute x0 -> x3, waiting for transfers between devices: none -> 3.2 us  [project(): lax.ppermute(blocks[d], ('yl', 'xl'), [(i, i ^ d) for i in range(4)])]
    pallas_call x1 -> x2, Pallas kernels: 0.19 us -> 3.05 us  [the longest x1 2.15 us: address(): pl.pallas_call(address_kernel, out_shape=jax.ShapeDtypeStruct((64, rows,...]
    all_to_all x1, waiting for transfers between devices: 16.6 us -> 19.4 us  [project(): lax.all_to_all(partial.reshape(64, rows, 4 * cols), TURNED, split_axis=0,...]
  transfers between devices with their start and end apart: 3 -> 6, of which waited for: 2 -> 3; matrix products, arithmetic and copies ran while one was open for 3% -> 3% of each run, Pallas kernels for 0% -> 0%
where the time goes in v4:
time: 185 us; the launch traced here: 184 us
  blocking collectives  82.4 us (45%)
  starting transfers between devices  47.6 us (26%)
  waiting for transfers between devices  34.9 us (19%)
  local copies, waits for them, and re-layouts  8.35 us (5%)
  Pallas kernels  5.68 us (3%)
  matrix products  4.26 us (2%)
    all_to_all x1, blocking collectives, per_device(): lax.all_to_all(outgoing, EXPERT, split_axis=0, concat_axis=0, tiled=True)  38.4 us
    all_to_all x1, starting transfers between devices, project(): lax.all_to_all(partial.reshape(64, rows, 4 * cols), TURNED, split_axis=0,...  20.4 us
    all_to_all x1, blocking collectives, per_device(): lax.all_to_all(result.reshape(groups, CAP, width_block).astype(BF16), EXP...  19.7 us
    all_to_all x1, waiting for transfers between devices, project(): lax.all_to_all(partial.reshape(64, rows, 4 * cols), TURNED, split_axis=0,...  19.4 us
    all_to_all x1, starting transfers between devices, project(): lax.all_to_all(address(attn_out), EXPERT, split_axis=0, concat_axis=0, ti...  17.3 us
    all_to_all x1, blocking collectives, per_device(): lax.all_to_all(gate_up.reshape(4, quarter, 2 * slice_units), 'tensor', sp...  12.9 us
    all_to_all x1, waiting for transfers between devices, project(): lax.all_to_all(address(attn_out), EXPERT, split_axis=0, concat_axis=0, ti...  12.3 us
    all_to_all x1, blocking collectives, per_device(): lax.all_to_all(jnp.broadcast_to(hidden[None], (4, quarter, slice_units)),...  11.5 us
  transfers between devices with their start and end apart: 6, of which 3 were waited for; matrix products, arithmetic and copies ran while one was open for 3% of the time, Pallas kernels for 0%

profile of v4, /device:TPU:2, one launch (start us, length us, event | category | flops | bytes accessed | tf_op | source)
XLA Modules:
  0.0 184.2 jit_solution(7627547450194216372)
XLA Ops:
  0.6 2.2 %address.1 = bf16[64,8,1024]{2,1,0:T(8,128)(2,1)} custom-call(bf16[8,4096]{1,0:T(8,128)(2,1)} %attn_ref.1), custom_call_target="tpu_custom_call" | custom-call | tf_op jit(solution)/shard_map/address/pallas_call | solution.py:48
  2.8 17.3 %all-to-all-start = ((bf16[64,8,1024]{2,1,0:T(8,128)(2,1)}), bf16[64,8,1024]{2,1,0:T(8,128)(2,1)S(1)}, u32[]{:S(2)}, u32[]{:S(2)}) async-start(bf16[64,8,1024]{2,1,0:T(8,128)(2,1)} %address.1), calls=%async_computation | async-start | bytes 2097152 | tf_op jit(solution)/shard_map/all_to_all | solution.py:108
  20.1 1.2 copy-done.1
  21.3 0.9 cut.1
  22.2 2.5 %collective-permute-start = (bf16[112,1024]{1,0:T(8,128)(2,1)}, bf16[112,1024]{1,0:T(8,128)(2,1)S(1)}, u32[]{:S(2)}, u32[]{:S(2)}) collective-permute-start(bf16[112,1024]{1,0:T(8,128)(2,1)} %get-tuple-element.10), channel_id=1, source_target_pairs={{0,4},{4,0},{32,36},{36,32},{1,5},{5,1},{33,37},{37,33},{2,6},{6,2... | collective-permute-start | bytes 688136 | tf_op jit(solution)/shard_map/ppermute | solution.py:111
  24.7 3.4 %collective-permute-start.1 = (bf16[112,1024]{1,0:T(8,128)(2,1)}, bf16[112,1024]{1,0:T(8,128)(2,1)}, u32[]{:S(2)}, u32[]{:S(2)}) collective-permute-start(bf16[112,1024]{1,0:T(8,128)(2,1)} %get-tuple-element.11), channel_id=1, source_target_pairs={{0,32},{4,36},{32,0},{36,4},{1,33},{5,37},{33,1},{37,5},{2,34},{6,... | collective-permute-start | bytes 688136 | tf_op jit(solution)/shard_map/ppermute | solution.py:111
  28.1 3.3 %collective-permute-start.2 = (bf16[112,1024]{1,0:T(8,128)(2,1)}, bf16[112,1024]{1,0:T(8,128)(2,1)}, u32[]{:S(2)}, u32[]{:S(2)}) collective-permute-start(bf16[112,1024]{1,0:T(8,128)(2,1)} %get-tuple-element.12), channel_id=1, source_target_pairs={{0,36},{4,32},{32,4},{36,0},{1,37},{5,33},{33,5},{37,1},{2,38},{6,... | collective-permute-start | bytes 688136 | tf_op jit(solution)/shard_map/ppermute | solution.py:111
  31.4 4.8 %copy.25 = bf16[224,8,2,512]{3,1,2,0:T(8,128)(2,1)} copy(bf16[224,8,2,512]{3,2,1,0:T(2,128)(2,1)} %bitcast.25) | data formatting | bytes 7340032
  36.2 12.3 %all-to-all-done = bf16[64,8,1024]{2,1,0:T(8,128)(2,1)S(1)} async-done(((bf16[64,8,1024]{2,1,0:T(8,128)(2,1)}), bf16[64,8,1024]{2,1,0:T(8,128)(2,1)S(1)}, u32[]{:S(2)}, u32[]{:S(2)}) %all-to-all-start) | async-done | bytes 1048608 | tf_op jit(solution)/shard_map/all_to_all | solution.py:108
  48.6 3.2 %collective-permute-done.1.refs_2_ = bf16[112,1024]{1,0:T(8,128)(2,1)} collective-permute-done((bf16[112,1024]{1,0:T(8,128)(2,1)}, bf16[112,1024]{1,0:T(8,128)(2,1)}, u32[]{:S(2)}, u32[]{:S(2)}) %collective-permute-start.1) | collective-permute-done | bytes 229408 | tf_op jit(solution)/shard_map/ppermute | solution.py:111
  51.8 2.6 %partial_sums.1 = bf16[512,448]{1,0:T(8,128)(2,1)} custom-call(s32[1]{0:T(128)} %bitcast.me, bf16[512,1024]{1,0:T(8,128)(2,1)S(1)} %bitcast.22, bf16[112,1024]{1,0:T(8,128)(2,1)S(1)} %get-tuple-element.9.refs_0_, bf16[112,1024]{1,0:T(8,128)(2,1)S(1)} %collective-permute-done.refs_1_, bf16[112,1024]{1,0:T(8,128)(2,1)} %collective-permute-done.1.refs_2_, ...), custom_call_target="tpu_custom_call" | custom-call | tf_op jit(solution)/shard_map/partial_sums/pallas_call | solution.py:94
  54.4 20.4 %all-to-all-start.1 = ((bf16[64,8,448]{2,1,0:T(8,128)(2,1)}), bf16[64,8,448]{2,1,0:T(8,128)(2,1)S(1)}, u32[]{:S(2)}, u32[]{:S(2)}) async-start(bf16[64,8,448]{2,1,0:T(8,128)(2,1)} %bitcast.3), calls=%async_computation.1 | async-start | bytes 1048576 | tf_op jit(solution)/shard_map/all_to_all | solution.py:114
  74.8 19.4 %all-to-all-done.1 = bf16[64,8,448]{2,1,0:T(8,128)(2,1)S(1)} async-done(((bf16[64,8,448]{2,1,0:T(8,128)(2,1)}), bf16[64,8,448]{2,1,0:T(8,128)(2,1)S(1)}, u32[]{:S(2)}, u32[]{:S(2)}) %all-to-all-start.1) | async-done | bytes 458784 | tf_op jit(solution)/shard_map/all_to_all | solution.py:114
  94.2 0.1 reduce_sum.39
  94.3 0.1 reshape.75
  94.4 0.1 reshape.76
  94.6 0.7 collective-permute-start.3
  95.3 0.1 convert_reduce_fusion.1
  95.4 0.1 copy.20
  95.5 0.2 convolution_convert_fusion.1
  95.7 0.5 copy.22
  96.2 38.4 %all_to_all.30 = bf16[64,2,1792]{2,1,0:T(2,128)(2,1)S(1)} all-to-all(bf16[64,2,1792]{2,1,0:T(2,128)(2,1)S(1)} %copy.22), channel_id=1, replica_groups=mesh['plane'=2,'core'=2,'yh'=4,'yl'=2,'xh'=4,'xl'=2,'tensor'=4] {'yh','y..., dimensions={0} | all-to-all | bytes 917504 | tf_op jit(solution)/shard_map/all_to_all | solution.py:142
  134.6 0.2 reshape.77
  134.8 2.7 %convolution_convert_fusion.3 = bf16[128,1024]{1,0:T(8,128)(2,1)S(1)} fusion(bf16[128,1792]{1,0:T(8,128)(2,1)S(1)} %reshape.77, bf16[1792,1024]{1,0:T(8,128)(2,1)} %bitcast.24), kind=kOutput, calls=%fused_computation.4 | convolution fusion | flops 469893120 | bytes 4390912 | tf_op jit(solution)/shard_map/dot_general | solution.py:144
  137.5 12.9 %all_to_all.31 = bf16[4,32,1024]{2,1,0:T(8,128)(2,1)S(1)} all-to-all(bf16[4,32,1024]{2,1,0:T(8,128)(2,1)S(1)} %bitcast.27), channel_id=1, replica_groups=mesh['plane'=2,'core'=2,'yh'=4,'yl'=2,'xh'=4,'xl'=2,'tensor'=4] {'tensor'}, dimensions={0} | all-to-all | bytes 524288 | tf_op jit(solution)/shard_map/all_to_all | solution.py:146
  150.4 11.5 %all_to_all.32 = bf16[4,32,512]{2,1,0:T(8,128)(2,1)S(1)} all-to-all(bf16[4,32,512]{2,1,0:T(8,128)(2,1)S(1)} %broadcast_in_dim.16), channel_id=1, replica_groups=mesh['plane'=2,'core'=2,'yh'=4,'yl'=2,'xh'=4,'xl'=2,'tensor'=4] {'tensor'}, dimensions={0} | all-to-all | bytes 262144 | tf_op jit(solution)/shard_map/all_to_all | solution.py:151
  162.0 0.4 convolution_convert_fusion
  162.4 0.5 copy.24
  162.9 19.7 %all_to_all.33 = bf16[64,2,1792]{2,1,0:T(2,128)(2,1)S(1)} all-to-all(bf16[64,2,1792]{2,1,0:T(2,128)(2,1)S(1)} %copy.24), channel_id=1, replica_groups=mesh['plane'=2,'core'=2,'yh'=4,'yl'=2,'xh'=4,'xl'=2,'tensor'=4] {'yh','y..., dimensions={0} | all-to-all | bytes 917504 | tf_op jit(solution)/shard_map/all_to_all | solution.py:159
  182.6 0.2 reshape.80
  182.7 0.9 convolution_convert_fusion.2
  183.6 0.6 copy.31
  (18 shorter events, 0.2 us)
Async XLA Ops:
  0.6 161.3 %copy-start = (bf16[1,512,1792]{2,1,0:T(8,128)(2,1)S(1)}, bf16[1,512,1792]{2,1,0:T(8,128)(2,1)}, u32[]{:S(2)}) copy-start(bf16[1,512,1792]{2,1,0:T(8,128)(2,1)} %param.10) | copy-start | bytes 5505028
  2.8 45.8 %all-to-all-start = ((bf16[64,8,1024]{2,1,0:T(8,128)(2,1)}), bf16[64,8,1024]{2,1,0:T(8,128)(2,1)S(1)}, u32[]{:S(2)}, u32[]{:S(2)}) async-start(bf16[64,8,1024]{2,1,0:T(8,128)(2,1)} %address.1), calls=%async_computation | async-start | bytes 2097152 | tf_op jit(solution)/shard_map/all_to_all | solution.py:108
  20.1 1.2 copy-start.1
  22.2 26.4 %collective-permute-start = (bf16[112,1024]{1,0:T(8,128)(2,1)}, bf16[112,1024]{1,0:T(8,128)(2,1)S(1)}, u32[]{:S(2)}, u32[]{:S(2)}) collective-permute-start(bf16[112,1024]{1,0:T(8,128)(2,1)} %get-tuple-element.10), channel_id=1, source_target_pairs={{0,4},{4,0},{32,36},{36,32},{1,5},{5,1},{33,37},{37,33},{2,6},{6,2... | collective-permute-start | bytes 688136 | tf_op jit(solution)/shard_map/ppermute | solution.py:111
  24.7 27.1 %collective-permute-start.1 = (bf16[112,1024]{1,0:T(8,128)(2,1)}, bf16[112,1024]{1,0:T(8,128)(2,1)}, u32[]{:S(2)}, u32[]{:S(2)}) collective-permute-start(bf16[112,1024]{1,0:T(8,128)(2,1)} %get-tuple-element.11), channel_id=1, source_target_pairs={{0,32},{4,36},{32,0},{36,4},{1,33},{5,37},{33,1},{37,5},{2,34},{6,... | collective-permute-start | bytes 688136 | tf_op jit(solution)/shard_map/ppermute | solution.py:111
  28.1 23.7 %collective-permute-start.2 = (bf16[112,1024]{1,0:T(8,128)(2,1)}, bf16[112,1024]{1,0:T(8,128)(2,1)}, u32[]{:S(2)}, u32[]{:S(2)}) collective-permute-start(bf16[112,1024]{1,0:T(8,128)(2,1)} %get-tuple-element.12), channel_id=1, source_target_pairs={{0,36},{4,32},{32,4},{36,0},{1,37},{5,33},{33,5},{37,1},{2,38},{6,... | collective-permute-start | bytes 688136 | tf_op jit(solution)/shard_map/ppermute | solution.py:111
  36.2 59.0 %copy-start.2 = (s32[8,8]{1,0:T(8,128)S(1)}, s32[8,8]{1,0:T(8,128)}, u32[]{:S(2)}) copy-start(s32[8,8]{1,0:T(8,128)} %param.12) | copy-start | bytes 772
  36.2 59.0 %copy-start.3 = (s32[8,8]{1,0:T(8,128)S(1)}, s32[8,8]{1,0:T(8,128)}, u32[]{:S(2)}) copy-start(s32[8,8]{1,0:T(8,128)} %param.11) | copy-start | bytes 772
  36.2 59.0 %copy-start.4 = (f32[8,8]{1,0:T(8,128)S(1)}, f32[8,8]{1,0:T(8,128)}, u32[]{:S(2)}) copy-start(f32[8,8]{1,0:T(8,128)} %param.13) | copy-start | bytes 772
  54.4 39.8 %all-to-all-start.1 = ((bf16[64,8,448]{2,1,0:T(8,128)(2,1)}), bf16[64,8,448]{2,1,0:T(8,128)(2,1)S(1)}, u32[]{:S(2)}, u32[]{:S(2)}) async-start(bf16[64,8,448]{2,1,0:T(8,128)(2,1)} %bitcast.3), calls=%async_computation.1 | async-start | bytes 1048576 | tf_op jit(solution)/shard_map/all_to_all | solution.py:114
  94.6 0.9 collective-permute-start.3

commit v5 on v4

--- a/solution.py
+++ b/solution.py
@@ -8,7 +8,8 @@
 HSPLIT = 4
 CAP = 2
 EXPERT = ("yh", "yl", "xh", "xl")
-TURNED = ("tensor", "yl", "xh", "xl")
+NEAR = ("yl", "xh", "xl")
+FAR = ("yh", "tensor")
 BF16 = jnp.bfloat16
 F32 = jnp.float32
 
@@ -22,8 +23,8 @@
     part = attn_ref.shape[1] // 4
     copies = []
     for m in range(4):
-        for x in range(4):
-            at = (m // 2) * 8 + x * 2 + m % 2
+        for yh in range(4):
+            at = m * 4 + yh
             copies.append(
                 pltpu.make_async_copy(
                     attn_ref.at[:, pl.ds(m * part, part)], staged.at[at], in_sems.at[at]
@@ -34,8 +35,10 @@
     for copy in copies:
         copy.wait()
     copies = [
-        pltpu.make_async_copy(staged, sent_ref.at[pl.ds(yh * 16, 16)], out_sems.at[yh])
-        for yh in range(4)
+        pltpu.make_async_copy(
+            staged.at[pl.ds(i // 4 * 8, 8)], sent_ref.at[pl.ds(i * 8, 8)], out_sems.at[i]
+        )
+        for i in range(8)
     ]
     for copy in copies:
         copy.start()
@@ -53,7 +56,7 @@
         scratch_shapes=[
             pltpu.VMEM((16, rows, part), BF16),
             pltpu.SemaphoreType.DMA((16,)),
-            pltpu.SemaphoreType.DMA((4,)),
+            pltpu.SemaphoreType.DMA((8,)),
         ],
         compiler_params=pltpu.CompilerParams(vmem_limit_bytes=58 << 20),
         name="address",
@@ -105,22 +108,25 @@
 def project(attn_out, w_proj, gate_up_w):
     rows, cols = attn_out.shape[0], w_proj.shape[1]
     me = lax.axis_index(("yl", "xl")).reshape(1).astype(jnp.int32)
-    tokens = lax.all_to_all(address(attn_out), EXPERT, split_axis=0, concat_axis=0, tiled=True)
+    tokens = lax.all_to_all(address(attn_out), NEAR + ("yh",), split_axis=0, concat_axis=0, tiled=True)
     blocks = list(cut(me, w_proj.T))
     for d in range(1, 4):
         blocks[d] = lax.ppermute(blocks[d], ("yl", "xl"), [(i, i ^ d) for i in range(4)])
     tokens, gate_up_w = lax.optimization_barrier((tokens, gate_up_w))
     partial = partial_sums(me, tokens.reshape(64 * rows, -1), blocks)
     got = lax.all_to_all(
-        partial.reshape(64, rows, 4 * cols), TURNED, split_axis=0, concat_axis=0, tiled=True
+        partial.reshape(16, 4 * rows, 4 * cols), NEAR, split_axis=0, concat_axis=0, tiled=True
     )
-    got = got.reshape(4, 2, 4, 2, rows, 4 * cols).astype(F32)
-    total = jnp.sum(got, axis=(0, 1, 3)).astype(BF16)
+    got = jnp.sum(got.reshape(2, 4, 2, 4 * rows, 4 * cols).astype(F32), axis=(0, 2))
+    got = got.astype(BF16).reshape(4, 4, rows, 4 * cols).transpose(1, 0, 2, 3)
+    real = jnp.arange(4, dtype=jnp.int32) == lax.axis_index("yh")
+    got = jnp.where(real[None, :, None, None, None], got[:, None], BF16(0))
+    got = lax.all_to_all(
+        got.reshape(16, 4, rows, 4 * cols), FAR, split_axis=0, concat_axis=0, tiled=True
+    )
+    total = jnp.sum(got.astype(F32), axis=0).astype(BF16)
     total = total.reshape(4, rows, 2, 2, cols).transpose(1, 2, 0, 3, 4).reshape(rows, 16 * cols)
-    turned = lax.ppermute(
-        total, ("yh", "tensor"), [(a * 4 + b, b * 4 + a) for a in range(4) for b in range(4)]
-    )
-    return turned, gate_up_w
+    return total, gate_up_w
 
 
 def per_device(attn_out, w_proj, w_in, w_out, expert_ids, slots, gates):

time: 185 us -> 195 us (1.054)
  blocking collectives: 82.4 us -> 53.5 us
  waiting for transfers between devices: 34.9 us -> 61 us
  starting transfers between devices: 47.6 us -> 58.2 us
    all_to_all x2 -> x4, waiting for transfers between devices: 31.7 us -> 56.7 us  [the longest x1 15.4 us: project(): lax.all_to_all(got.reshape(16, 4, rows, 4 * cols), FAR, split_axis=0, con...]
    all_to_all x1 -> x0, blocking collectives: 19.7 us -> none  [per_device(): lax.all_to_all(result.reshape(groups, CAP, width_block).astype(BF16), EXP...]
    all_to_all x2 -> x4, starting transfers between devices: 37.7 us -> 49 us  [the longest x1 19.2 us: project(): lax.all_to_all(got.reshape(16, 4, rows, 4 * cols), FAR, split_axis=0, con...]
    all_to_all x1, blocking collectives: 38.4 us -> 30.2 us  [per_device(): lax.all_to_all(outgoing, EXPERT, split_axis=0, concat_axis=0, tiled=True)]
    unnamed x12 -> x11, local copies, waits for them, and re-layouts: 6.64 us -> 6.03 us
  transfers between devices with their start and end apart: 6 -> 7, of which waited for: 3 -> 5; matrix products, arithmetic and copies ran while one was open for 3% -> 3% of each run, Pallas kernels for 0% -> 0%
where the time goes in v5:
time: 195 us; the launch traced here: 194 us
  waiting for transfers between devices  61 us (31%)
  starting transfers between devices  58.2 us (30%)
  blocking collectives  53.5 us (27%)
  local copies, waits for them, and re-layouts  9.31 us (5%)
  Pallas kernels  5.72 us (3%)
  matrix products  4.26 us (2%)
    all_to_all x1, blocking collectives, per_device(): lax.all_to_all(outgoing, EXPERT, split_axis=0, concat_axis=0, tiled=True)  30.2 us
    all_to_all x1, starting transfers between devices, project(): lax.all_to_all(got.reshape(16, 4, rows, 4 * cols), FAR, split_axis=0, con...  19.2 us
    all_to_all x1, starting transfers between devices, project(): lax.all_to_all(address(attn_out), NEAR + ('yh',), split_axis=0, concat_ax...  17.3 us
    all_to_all x1, waiting for transfers between devices, project(): lax.all_to_all(got.reshape(16, 4, rows, 4 * cols), FAR, split_axis=0, con...  15.4 us
    all_to_all x1, waiting for transfers between devices, per_device(): lax.all_to_all(result.reshape(groups, CAP, width_block).astype(BF16), EXP...  15.3 us
    all_to_all x1, waiting for transfers between devices, project(): lax.all_to_all(partial.reshape(16, 4 * rows, 4 * cols), NEAR, split_axis=...  14.8 us
    all_to_all x1, blocking collectives, per_device(): lax.all_to_all(gate_up.reshape(4, quarter, 2 * slice_units), 'tensor', sp...  12.2 us
    all_to_all x1, waiting for transfers between devices, project(): lax.all_to_all(address(attn_out), NEAR + ('yh',), split_axis=0, concat_ax...  11.2 us
  transfers between devices with their start and end apart: 7, of which 5 were waited for; matrix products, arithmetic and copies ran while one was open for 3% of the time, Pallas kernels for 0%

profile of v5, /device:TPU:2, one launch (start us, length us, event | category | flops | bytes accessed | tf_op | source)
XLA Modules:
  0.0 194.0 jit_solution(15204833477219503652)
XLA Ops:
  0.6 2.2 %address.1 = bf16[64,8,1024]{2,1,0:T(8,128)(2,1)} custom-call(bf16[8,4096]{1,0:T(8,128)(2,1)} %attn_ref.1), custom_call_target="tpu_custom_call" | custom-call | tf_op jit(solution)/shard_map/address/pallas_call | solution.py:51
  2.8 17.3 %all-to-all-start = ((bf16[64,8,1024]{2,1,0:T(8,128)(2,1)}), bf16[64,8,1024]{2,1,0:T(8,128)(2,1)S(1)}, u32[]{:S(2)}, u32[]{:S(2)}) async-start(bf16[64,8,1024]{2,1,0:T(8,128)(2,1)} %address.1), calls=%async_computation | async-start | bytes 2097152 | tf_op jit(solution)/shard_map/all_to_all | solution.py:111
  20.2 1.2 copy-done.1
  21.3 0.9 cut.1
  22.2 2.4 %collective-permute-start = (bf16[112,1024]{1,0:T(8,128)(2,1)}, bf16[112,1024]{1,0:T(8,128)(2,1)S(1)}, u32[]{:S(2)}, u32[]{:S(2)}) collective-permute-start(bf16[112,1024]{1,0:T(8,128)(2,1)} %get-tuple-element.10), channel_id=1, source_target_pairs={{0,4},{4,0},{32,36},{36,32},{1,5},{5,1},{33,37},{37,33},{2,6},{6,2... | collective-permute-start | bytes 688136 | tf_op jit(solution)/shard_map/ppermute | solution.py:114
  24.7 3.6 %collective-permute-start.1 = (bf16[112,1024]{1,0:T(8,128)(2,1)}, bf16[112,1024]{1,0:T(8,128)(2,1)}, u32[]{:S(2)}, u32[]{:S(2)}) collective-permute-start(bf16[112,1024]{1,0:T(8,128)(2,1)} %get-tuple-element.11), channel_id=1, source_target_pairs={{0,32},{4,36},{32,0},{36,4},{1,33},{5,37},{33,1},{37,5},{2,34},{6,... | collective-permute-start | bytes 688136 | tf_op jit(solution)/shard_map/ppermute | solution.py:114
  28.3 3.2 %collective-permute-start.2 = (bf16[112,1024]{1,0:T(8,128)(2,1)}, bf16[112,1024]{1,0:T(8,128)(2,1)}, u32[]{:S(2)}, u32[]{:S(2)}) collective-permute-start(bf16[112,1024]{1,0:T(8,128)(2,1)} %get-tuple-element.12), channel_id=1, source_target_pairs={{0,36},{4,32},{32,4},{36,0},{1,37},{5,33},{33,5},{37,1},{2,38},{6,... | collective-permute-start | bytes 688136 | tf_op jit(solution)/shard_map/ppermute | solution.py:114
  31.5 4.8 %copy.33 = bf16[224,8,2,512]{3,1,2,0:T(8,128)(2,1)} copy(bf16[224,8,2,512]{3,2,1,0:T(2,128)(2,1)} %bitcast.31) | data formatting | bytes 7340032
  36.3 11.2 %all-to-all-done = bf16[64,8,1024]{2,1,0:T(8,128)(2,1)S(1)} async-done(((bf16[64,8,1024]{2,1,0:T(8,128)(2,1)}), bf16[64,8,1024]{2,1,0:T(8,128)(2,1)S(1)}, u32[]{:S(2)}, u32[]{:S(2)}) %all-to-all-start) | async-done | bytes 1048608 | tf_op jit(solution)/shard_map/all_to_all | solution.py:111
  47.5 4.2 %collective-permute-done.1.refs_2_ = bf16[112,1024]{1,0:T(8,128)(2,1)} collective-permute-done((bf16[112,1024]{1,0:T(8,128)(2,1)}, bf16[112,1024]{1,0:T(8,128)(2,1)}, u32[]{:S(2)}, u32[]{:S(2)}) %collective-permute-start.1) | collective-permute-done | bytes 229408 | tf_op jit(solution)/shard_map/ppermute | solution.py:114
  51.8 2.6 %partial_sums.1 = bf16[512,448]{1,0:T(8,128)(2,1)} custom-call(s32[1]{0:T(128)} %bitcast.me, bf16[512,1024]{1,0:T(8,128)(2,1)S(1)} %bitcast.28, bf16[112,1024]{1,0:T(8,128)(2,1)S(1)} %get-tuple-element.9.refs_0_, bf16[112,1024]{1,0:T(8,128)(2,1)S(1)} %collective-permute-done.refs_1_, bf16[112,1024]{1,0:T(8,128)(2,1)} %collective-permute-done.1.refs_2_, ...), custom_call_target="tpu_custom_call" | custom-call | tf_op jit(solution)/shard_map/partial_sums/pallas_call | solution.py:97
  54.4 6.8 %all-to-all-start.1 = ((bf16[16,32,448]{2,1,0:T(8,128)(2,1)}), bf16[16,32,448]{2,1,0:T(8,128)(2,1)S(1)}, u32[]{:S(2)}, u32[]{:S(2)}) async-start(bf16[16,32,448]{2,1,0:T(8,128)(2,1)} %bitcast.3), calls=%async_computation.1 | async-start | bytes 1048576 | tf_op jit(solution)/shard_map/all_to_all | solution.py:117
  61.3 14.8 %all-to-all-done.1 = bf16[16,32,448]{2,1,0:T(8,128)(2,1)S(1)} async-done(((bf16[16,32,448]{2,1,0:T(8,128)(2,1)}), bf16[16,32,448]{2,1,0:T(8,128)(2,1)S(1)}, u32[]{:S(2)}, u32[]{:S(2)}) %all-to-all-start.1) | async-done | bytes 458784 | tf_op jit(solution)/shard_map/all_to_all | solution.py:117
  76.3 0.9 bitcast_select_fusion
  77.2 19.2 %all-to-all-start.2 = ((bf16[16,4,8,448]{3,2,1,0:T(8,128)(2,1)}), bf16[16,4,8,448]{3,2,1,0:T(8,128)(2,1)S(1)}, u32[]{:S(2)}, u32[]{:S(2)}) async-start(bf16[16,4,8,448]{3,2,1,0:T(8,128)(2,1)} %bitcast_select_fusion), calls=%async_computation.2 | async-start | bytes 1048576 | tf_op jit(solution)/shard_map/all_to_all | solution.py:124
  96.6 0.1 copy.28
  96.7 15.4 %all-to-all-done.2 = bf16[16,4,8,448]{3,2,1,0:T(8,128)(2,1)S(1)} async-done(((bf16[16,4,8,448]{3,2,1,0:T(8,128)(2,1)}), bf16[16,4,8,448]{3,2,1,0:T(8,128)(2,1)S(1)}, u32[]{:S(2)}, u32[]{:S(2)}) %all-to-all-start.2) | async-done | bytes 458784 | tf_op jit(solution)/shard_map/all_to_all | solution.py:124
  112.3 0.1 reshape.99
  112.4 0.2 convolution_convert_fusion.1
  112.7 0.5 copy.30
  113.2 30.2 %all_to_all.35 = bf16[64,2,1792]{2,1,0:T(2,128)(2,1)S(1)} all-to-all(bf16[64,2,1792]{2,1,0:T(2,128)(2,1)S(1)} %copy.30), channel_id=1, replica_groups=mesh['plane'=2,'core'=2,'yh'=4,'yl'=2,'xh'=4,'xl'=2,'tensor'=4] {'yh','y..., dimensions={0} | all-to-all | bytes 917504 | tf_op jit(solution)/shard_map/all_to_all | solution.py:148
  143.3 0.2 reshape.95
  143.5 2.7 %convolution_convert_fusion.3 = bf16[128,1024]{1,0:T(8,128)(2,1)S(1)} fusion(bf16[128,1792]{1,0:T(8,128)(2,1)S(1)} %reshape.95, bf16[1792,1024]{1,0:T(8,128)(2,1)} %bitcast.30), kind=kOutput, calls=%fused_computation.4 | convolution fusion | flops 469893120 | bytes 4390912 | tf_op jit(solution)/shard_map/dot_general | solution.py:150
  146.2 12.2 %all_to_all.36 = bf16[4,32,1024]{2,1,0:T(8,128)(2,1)S(1)} all-to-all(bf16[4,32,1024]{2,1,0:T(8,128)(2,1)S(1)} %bitcast.33), channel_id=1, replica_groups=mesh['plane'=2,'core'=2,'yh'=4,'yl'=2,'xh'=4,'xl'=2,'tensor'=4] {'tensor'}, dimensions={0} | all-to-all | bytes 524288 | tf_op jit(solution)/shard_map/all_to_all | solution.py:152
  158.5 11.1 %all_to_all.37 = bf16[4,32,512]{2,1,0:T(8,128)(2,1)S(1)} all-to-all(bf16[4,32,512]{2,1,0:T(8,128)(2,1)S(1)} %broadcast_in_dim.59), channel_id=1, replica_groups=mesh['plane'=2,'core'=2,'yh'=4,'yl'=2,'xh'=4,'xl'=2,'tensor'=4] {'tensor'}, dimensions={0} | all-to-all | bytes 262144 | tf_op jit(solution)/shard_map/all_to_all | solution.py:157
  169.7 0.4 convolution_convert_fusion
  170.1 1.2 copy.32
  171.4 5.6 %all-to-all-start.6 = ((bf16[64,2,1792]{2,1,0:T(2,128)(2,1)}), bf16[64,2,1792]{2,1,0:T(2,128)(2,1)S(1)}, u32[]{:S(2)}, u32[]{:S(2)}) async-start(bf16[64,2,1792]{2,1,0:T(2,128)(2,1)} %copy.32), calls=%async_computation.6 | async-start | bytes 917504 | tf_op jit(solution)/shard_map/all_to_all | solution.py:165
  177.0 0.7 reshape.94
  177.7 15.3 %all-to-all-done.6 = bf16[64,2,1792]{2,1,0:T(2,128)(2,1)S(1)} async-done(((bf16[64,2,1792]{2,1,0:T(2,128)(2,1)}), bf16[64,2,1792]{2,1,0:T(2,128)(2,1)S(1)}, u32[]{:S(2)}, u32[]{:S(2)}) %all-to-all-start.6) | async-done | bytes 458784 | tf_op jit(solution)/shard_map/all_to_all | solution.py:165
  193.0 0.2 reshape.98
  193.1 0.9 convolution_convert_fusion.2
  (24 shorter events, 0.7 us)
Async XLA Ops:
  0.6 169.1 %copy-start = (bf16[1,512,1792]{2,1,0:T(8,128)(2,1)S(1)}, bf16[1,512,1792]{2,1,0:T(8,128)(2,1)}, u32[]{:S(2)}) copy-start(bf16[1,512,1792]{2,1,0:T(8,128)(2,1)} %param.10) | copy-start | bytes 5505028
  2.8 44.7 %all-to-all-start = ((bf16[64,8,1024]{2,1,0:T(8,128)(2,1)}), bf16[64,8,1024]{2,1,0:T(8,128)(2,1)S(1)}, u32[]{:S(2)}, u32[]{:S(2)}) async-start(bf16[64,8,1024]{2,1,0:T(8,128)(2,1)} %address.1), calls=%async_computation | async-start | bytes 2097152 | tf_op jit(solution)/shard_map/all_to_all | solution.py:111
  20.2 1.2 copy-start.1
  22.2 25.3 %collective-permute-start = (bf16[112,1024]{1,0:T(8,128)(2,1)}, bf16[112,1024]{1,0:T(8,128)(2,1)S(1)}, u32[]{:S(2)}, u32[]{:S(2)}) collective-permute-start(bf16[112,1024]{1,0:T(8,128)(2,1)} %get-tuple-element.10), channel_id=1, source_target_pairs={{0,4},{4,0},{32,36},{36,32},{1,5},{5,1},{33,37},{37,33},{2,6},{6,2... | collective-permute-start | bytes 688136 | tf_op jit(solution)/shard_map/ppermute | solution.py:114
  24.7 27.1 %collective-permute-start.1 = (bf16[112,1024]{1,0:T(8,128)(2,1)}, bf16[112,1024]{1,0:T(8,128)(2,1)}, u32[]{:S(2)}, u32[]{:S(2)}) collective-permute-start(bf16[112,1024]{1,0:T(8,128)(2,1)} %get-tuple-element.11), channel_id=1, source_target_pairs={{0,32},{4,36},{32,0},{36,4},{1,33},{5,37},{33,1},{37,5},{2,34},{6,... | collective-permute-start | bytes 688136 | tf_op jit(solution)/shard_map/ppermute | solution.py:114
  28.3 23.5 %collective-permute-start.2 = (bf16[112,1024]{1,0:T(8,128)(2,1)}, bf16[112,1024]{1,0:T(8,128)(2,1)}, u32[]{:S(2)}, u32[]{:S(2)}) collective-permute-start(bf16[112,1024]{1,0:T(8,128)(2,1)} %get-tuple-element.12), channel_id=1, source_target_pairs={{0,36},{4,32},{32,4},{36,0},{1,37},{5,33},{33,5},{37,1},{2,38},{6,... | collective-permute-start | bytes 688136 | tf_op jit(solution)/shard_map/ppermute | solution.py:114
  36.3 60.1 %copy-start.2 = (s32[8,8]{1,0:T(8,128)S(1)}, s32[8,8]{1,0:T(8,128)}, u32[]{:S(2)}) copy-start(s32[8,8]{1,0:T(8,128)} %param.12) | copy-start | bytes 772
  36.3 60.1 %copy-start.3 = (s32[8,8]{1,0:T(8,128)S(1)}, s32[8,8]{1,0:T(8,128)}, u32[]{:S(2)}) copy-start(s32[8,8]{1,0:T(8,128)} %param.11) | copy-start | bytes 772
  36.3 60.1 %copy-start.4 = (f32[8,8]{1,0:T(8,128)S(1)}, f32[8,8]{1,0:T(8,128)}, u32[]{:S(2)}) copy-start(f32[8,8]{1,0:T(8,128)} %param.13) | copy-start | bytes 772
  54.4 21.8 %all-to-all-start.1 = ((bf16[16,32,448]{2,1,0:T(8,128)(2,1)}), bf16[16,32,448]{2,1,0:T(8,128)(2,1)S(1)}, u32[]{:S(2)}, u32[]{:S(2)}) async-start(bf16[16,32,448]{2,1,0:T(8,128)(2,1)} %bitcast.3), calls=%async_computation.1 | async-start | bytes 1048576 | tf_op jit(solution)/shard_map/all_to_all | solution.py:117
  77.2 34.9 %all-to-all-start.2 = ((bf16[16,4,8,448]{3,2,1,0:T(8,128)(2,1)}), bf16[16,4,8,448]{3,2,1,0:T(8,128)(2,1)S(1)}, u32[]{:S(2)}, u32[]{:S(2)}) async-start(bf16[16,4,8,448]{3,2,1,0:T(8,128)(2,1)} %bitcast_select_fusion), calls=%async_computation.2 | async-start | bytes 1048576 | tf_op jit(solution)/shard_map/all_to_all | solution.py:124
  171.4 21.6 %all-to-all-start.6 = ((bf16[64,2,1792]{2,1,0:T(2,128)(2,1)}), bf16[64,2,1792]{2,1,0:T(2,128)(2,1)S(1)}, u32[]{:S(2)}, u32[]{:S(2)}) async-start(bf16[64,2,1792]{2,1,0:T(2,128)(2,1)} %copy.32), calls=%async_computation.6 | async-start | bytes 917504 | tf_op jit(solution)/shard_map/all_to_all | solution.py:165

commit v6 on v4

--- a/solution.py
+++ b/solution.py
@@ -8,7 +8,6 @@
 HSPLIT = 4
 CAP = 2
 EXPERT = ("yh", "yl", "xh", "xl")
-TURNED = ("tensor", "yl", "xh", "xl")
 BF16 = jnp.bfloat16
 F32 = jnp.float32
 
@@ -82,6 +81,8 @@
 def partial_kernel(me, tokens, *refs):
     blocks, (out_ref, wide) = refs[:4], refs[4:]
     cols = blocks[0].shape[0]
+    spare = wide.shape[0] - 4 * cols
+    wide[pl.ds(4 * cols, spare), :] = jnp.zeros((spare, wide.shape[1]), BF16)
     for d in range(4):
         wide[pl.ds(pl.multiple_of((me[0] ^ d) * cols, 16), cols), :] = blocks[d][...]
     out_ref[...] = lax.dot_general(
@@ -91,12 +92,13 @@
 
 def partial_sums(me, tokens, blocks):
     cols, part = blocks[0].shape
+    padded = -(-4 * cols // 128) * 128
     return pl.pallas_call(
         partial_kernel,
-        out_shape=jax.ShapeDtypeStruct((tokens.shape[0], 4 * cols), BF16),
+        out_shape=jax.ShapeDtypeStruct((tokens.shape[0], padded), BF16),
         in_specs=[SMEM] + [VMEM] * 5,
         out_specs=VMEM,
-        scratch_shapes=[pltpu.VMEM((4 * cols, part), BF16)],
+        scratch_shapes=[pltpu.VMEM((padded, part), BF16)],
         compiler_params=pltpu.CompilerParams(vmem_limit_bytes=16 << 20),
         name="partial_sums",
     )(me, tokens, *blocks)
@@ -112,15 +114,14 @@
     tokens, gate_up_w = lax.optimization_barrier((tokens, gate_up_w))
     partial = partial_sums(me, tokens.reshape(64 * rows, -1), blocks)
     got = lax.all_to_all(
-        partial.reshape(64, rows, 4 * cols), TURNED, split_axis=0, concat_axis=0, tiled=True
+        partial.reshape(64, rows, -1), EXPERT, split_axis=0, concat_axis=0, tiled=True
     )
-    got = got.reshape(4, 2, 4, 2, rows, 4 * cols).astype(F32)
-    total = jnp.sum(got, axis=(0, 1, 3)).astype(BF16)
+    got = got.reshape(4, 2, 4, 2, rows, -1)[..., : 4 * cols].astype(F32)
+    got = jnp.sum(got, axis=(1, 3)).astype(BF16)
+    got = lax.all_to_all(got, "tensor", split_axis=0, concat_axis=0, tiled=True)
+    total = jnp.sum(got.astype(F32), axis=0).astype(BF16)
     total = total.reshape(4, rows, 2, 2, cols).transpose(1, 2, 0, 3, 4).reshape(rows, 16 * cols)
-    turned = lax.ppermute(
-        total, ("yh", "tensor"), [(a * 4 + b, b * 4 + a) for a in range(4) for b in range(4)]
-    )
-    return turned, gate_up_w
+    return total, gate_up_w
 
 
 def per_device(attn_out, w_proj, w_in, w_out, expert_ids, slots, gates):

time: 185 us -> 180 us (0.973)
  blocking collectives: 82.4 us -> 73.2 us
  waiting for transfers between devices: 34.9 us -> 37.9 us
    all_to_all x1, blocking collectives: 38.4 us -> 20.8 us  [per_device(): lax.all_to_all(outgoing, EXPERT, split_axis=0, concat_axis=0, tiled=True)]
    all_to_all x1, blocking collectives: 19.7 us -> 27.9 us  [project(): lax.all_to_all(partial.reshape(64, rows, -1), EXPERT, split_axis=0, conca...]
    all_to_all x1 -> x2, waiting for transfers between devices: 19.4 us -> 22.3 us  [the longest x1 14.2 us: per_device(): lax.all_to_all(result.reshape(groups, CAP, width_block).astype(BF16), EXP...]
    all_to_all x1 -> x2, starting transfers between devices: 20.4 us -> 21.9 us  [the longest x1 17.1 us: project(): got = lax.all_to_all(got, 'tensor', split_axis=0, concat_axis=0, tiled=True)]
    unnamed x12 -> x11, local copies, waits for them, and re-layouts: 6.64 us -> 6.03 us
  transfers between devices with their start and end apart: 6 -> 6, of which waited for: 3 -> 4; matrix products, arithmetic and copies ran while one was open for 3% -> 3% of each run, Pallas kernels for 0% -> 1%
where the time goes in v6:
time: 180 us
  blocking collectives  73.2 us (41%)
  starting transfers between devices  48.4 us (27%)
  waiting for transfers between devices  37.9 us (21%)
  local copies, waits for them, and re-layouts  9.23 us (5%)
  Pallas kernels  4.92 us (3%)
  matrix products  4.26 us (2%)
    all_to_all x1, blocking collectives, project(): lax.all_to_all(partial.reshape(64, rows, -1), EXPERT, split_axis=0, conca...  27.9 us
    all_to_all x1, blocking collectives, per_device(): lax.all_to_all(outgoing, EXPERT, split_axis=0, concat_axis=0, tiled=True)  20.8 us
    all_to_all x1, starting transfers between devices, project(): lax.all_to_all(address(attn_out), EXPERT, split_axis=0, concat_axis=0, ti...  17.3 us
    all_to_all x1, starting transfers between devices, project(): got = lax.all_to_all(got, 'tensor', split_axis=0, concat_axis=0, tiled=True)  17.1 us
    all_to_all x1, waiting for transfers between devices, per_device(): lax.all_to_all(result.reshape(groups, CAP, width_block).astype(BF16), EXP...  14.2 us
    all_to_all x1, blocking collectives, per_device(): lax.all_to_all(gate_up.reshape(4, quarter, 2 * slice_units), 'tensor', sp...  12.9 us
    all_to_all x1, waiting for transfers between devices, project(): lax.all_to_all(address(attn_out), EXPERT, split_axis=0, concat_axis=0, ti...  12.3 us
    all_to_all x1, blocking collectives, per_device(): lax.all_to_all(jnp.broadcast_to(hidden[None], (4, quarter, slice_units)),...  11.5 us
  transfers between devices with their start and end apart: 6, of which 4 were waited for; matrix products, arithmetic and copies ran while one was open for 3% of the time, Pallas kernels for 1%

profile of v6, /device:TPU:2, one launch (start us, length us, event | category | flops | bytes accessed | tf_op | source)
XLA Modules:
  0.0 179.6 jit_solution(5740344597792075307)
XLA Ops:
  0.6 2.2 %address.1 = bf16[64,8,1024]{2,1,0:T(8,128)(2,1)} custom-call(bf16[8,4096]{1,0:T(8,128)(2,1)} %attn_ref.1), custom_call_target="tpu_custom_call" | custom-call | tf_op jit(solution)/shard_map/address/pallas_call | solution.py:47
  2.8 17.3 %all-to-all-start = ((bf16[64,8,1024]{2,1,0:T(8,128)(2,1)}), bf16[64,8,1024]{2,1,0:T(8,128)(2,1)S(1)}, u32[]{:S(2)}, u32[]{:S(2)}) async-start(bf16[64,8,1024]{2,1,0:T(8,128)(2,1)} %address.1), calls=%async_computation | async-start | bytes 2097152 | tf_op jit(solution)/shard_map/all_to_all | solution.py:110
  20.1 1.2 copy-done.1
  21.3 0.9 cut.1
  22.2 2.5 %collective-permute-start = (bf16[112,1024]{1,0:T(8,128)(2,1)}, bf16[112,1024]{1,0:T(8,128)(2,1)S(1)}, u32[]{:S(2)}, u32[]{:S(2)}) collective-permute-start(bf16[112,1024]{1,0:T(8,128)(2,1)} %get-tuple-element.10), channel_id=1, source_target_pairs={{0,4},{4,0},{32,36},{36,32},{1,5},{5,1},{33,37},{37,33},{2,6},{6,2... | collective-permute-start | bytes 688136 | tf_op jit(solution)/shard_map/ppermute | solution.py:113
  24.7 3.4 %collective-permute-start.1 = (bf16[112,1024]{1,0:T(8,128)(2,1)}, bf16[112,1024]{1,0:T(8,128)(2,1)}, u32[]{:S(2)}, u32[]{:S(2)}) collective-permute-start(bf16[112,1024]{1,0:T(8,128)(2,1)} %get-tuple-element.11), channel_id=1, source_target_pairs={{0,32},{4,36},{32,0},{36,4},{1,33},{5,37},{33,1},{37,5},{2,34},{6,... | collective-permute-start | bytes 688136 | tf_op jit(solution)/shard_map/ppermute | solution.py:113
  28.1 3.3 %collective-permute-start.2 = (bf16[112,1024]{1,0:T(8,128)(2,1)}, bf16[112,1024]{1,0:T(8,128)(2,1)}, u32[]{:S(2)}, u32[]{:S(2)}) collective-permute-start(bf16[112,1024]{1,0:T(8,128)(2,1)} %get-tuple-element.12), channel_id=1, source_target_pairs={{0,36},{4,32},{32,4},{36,0},{1,37},{5,33},{33,5},{37,1},{2,38},{6,... | collective-permute-start | bytes 688136 | tf_op jit(solution)/shard_map/ppermute | solution.py:113
  31.4 4.8 %copy.29 = bf16[224,8,2,512]{3,1,2,0:T(8,128)(2,1)} copy(bf16[224,8,2,512]{3,2,1,0:T(2,128)(2,1)} %bitcast.24) | data formatting | bytes 7340032
  36.3 12.3 %all-to-all-done = bf16[64,8,1024]{2,1,0:T(8,128)(2,1)S(1)} async-done(((bf16[64,8,1024]{2,1,0:T(8,128)(2,1)}), bf16[64,8,1024]{2,1,0:T(8,128)(2,1)S(1)}, u32[]{:S(2)}, u32[]{:S(2)}) %all-to-all-start) | async-done | bytes 1048608 | tf_op jit(solution)/shard_map/all_to_all | solution.py:110
  48.6 3.2 %collective-permute-done.1.refs_2_ = bf16[112,1024]{1,0:T(8,128)(2,1)} collective-permute-done((bf16[112,1024]{1,0:T(8,128)(2,1)}, bf16[112,1024]{1,0:T(8,128)(2,1)}, u32[]{:S(2)}, u32[]{:S(2)}) %collective-permute-start.1) | collective-permute-done | bytes 229408 | tf_op jit(solution)/shard_map/ppermute | solution.py:113
  51.8 1.9 %partial_sums.1 = bf16[512,512]{1,0:T(8,128)(2,1)S(1)} custom-call(s32[1]{0:T(128)} %bitcast.me, bf16[512,1024]{1,0:T(8,128)(2,1)S(1)} %bitcast.20, bf16[112,1024]{1,0:T(8,128)(2,1)S(1)} %get-tuple-element.9.refs_0_, bf16[112,1024]{1,0:T(8,128)(2,1)S(1)} %collective-permute-done.refs_1_, bf16[112,1024]{1,0:T(8,128)(2,1)} %collective-permute-done.1.refs_2_, ...), custom_call_target="tpu_custom_call" | custom-call | tf_op jit(solution)/shard_map/partial_sums/pallas_call | solution.py:96
  53.6 27.9 %all_to_all.35 = bf16[64,8,512]{2,1,0:T(8,128)(2,1)S(1)} all-to-all(bf16[64,8,512]{2,1,0:T(8,128)(2,1)S(1)} %bitcast.21), channel_id=1, replica_groups=mesh['plane'=2,'core'=2,'yh'=4,'yl'=2,'xh'=4,'xl'=2,'tensor'=4] {'yh','y..., dimensions={0} | all-to-all | bytes 1048576 | tf_op jit(solution)/shard_map/all_to_all | solution.py:116
  81.5 0.7 slice_reduce_fusion
  82.3 17.1 %all-to-all-start.2 = ((bf16[4,4,8,448]{3,2,1,0:T(8,128)(2,1)}), bf16[4,4,8,448]{3,2,1,0:T(8,128)(2,1)S(1)}, u32[]{:S(2)}, u32[]{:S(2)}) async-start(bf16[4,4,8,448]{3,2,1,0:T(8,128)(2,1)} %slice_reduce_fusion), calls=%async_computation.2 | async-start | bytes 262144 | tf_op jit(solution)/shard_map/all_to_all | solution.py:121
  99.4 0.1 convert_reduce_fusion.1
  99.5 0.1 copy.24
  99.6 8.1 %all-to-all-done.2 = bf16[4,4,8,448]{3,2,1,0:T(8,128)(2,1)S(1)} async-done(((bf16[4,4,8,448]{3,2,1,0:T(8,128)(2,1)}), bf16[4,4,8,448]{3,2,1,0:T(8,128)(2,1)S(1)}, u32[]{:S(2)}, u32[]{:S(2)}) %all-to-all-start.2) | async-done | bytes 114720 | tf_op jit(solution)/shard_map/all_to_all | solution.py:121
  107.9 0.1 reshape.87
  108.0 0.2 convolution_convert_fusion.1
  108.3 0.5 copy.26
  108.7 20.8 %all_to_all.36 = bf16[64,2,1792]{2,1,0:T(2,128)(2,1)S(1)} all-to-all(bf16[64,2,1792]{2,1,0:T(2,128)(2,1)S(1)} %copy.26), channel_id=1, replica_groups=mesh['plane'=2,'core'=2,'yh'=4,'yl'=2,'xh'=4,'xl'=2,'tensor'=4] {'yh','y..., dimensions={0} | all-to-all | bytes 917504 | tf_op jit(solution)/shard_map/all_to_all | solution.py:143
  129.6 0.2 reshape.83
  129.7 2.7 %convolution_convert_fusion.3 = bf16[128,1024]{1,0:T(8,128)(2,1)S(1)} fusion(bf16[128,1792]{1,0:T(8,128)(2,1)S(1)} %reshape.83, bf16[1792,1024]{1,0:T(8,128)(2,1)} %bitcast.23), kind=kOutput, calls=%fused_computation.4 | convolution fusion | flops 469893120 | bytes 4390912 | tf_op jit(solution)/shard_map/dot_general | solution.py:145
  132.4 12.9 %all_to_all.37 = bf16[4,32,1024]{2,1,0:T(8,128)(2,1)S(1)} all-to-all(bf16[4,32,1024]{2,1,0:T(8,128)(2,1)S(1)} %bitcast.26), channel_id=1, replica_groups=mesh['plane'=2,'core'=2,'yh'=4,'yl'=2,'xh'=4,'xl'=2,'tensor'=4] {'tensor'}, dimensions={0} | all-to-all | bytes 524288 | tf_op jit(solution)/shard_map/all_to_all | solution.py:147
  145.5 11.5 %all_to_all.38 = bf16[4,32,512]{2,1,0:T(8,128)(2,1)S(1)} all-to-all(bf16[4,32,512]{2,1,0:T(8,128)(2,1)S(1)} %broadcast_in_dim.16), channel_id=1, replica_groups=mesh['plane'=2,'core'=2,'yh'=4,'yl'=2,'xh'=4,'xl'=2,'tensor'=4] {'tensor'}, dimensions={0} | all-to-all | bytes 262144 | tf_op jit(solution)/shard_map/all_to_all | solution.py:152
  157.0 0.4 convolution_convert_fusion
  157.4 1.2 copy.28
  158.7 4.9 %all-to-all-start.6 = ((bf16[64,2,1792]{2,1,0:T(2,128)(2,1)}), bf16[64,2,1792]{2,1,0:T(2,128)(2,1)S(1)}, u32[]{:S(2)}, u32[]{:S(2)}) async-start(bf16[64,2,1792]{2,1,0:T(2,128)(2,1)} %copy.28), calls=%async_computation.6 | async-start | bytes 917504 | tf_op jit(solution)/shard_map/all_to_all | solution.py:160
  163.5 0.7 reshape.82
  164.3 14.2 %all-to-all-done.6 = bf16[64,2,1792]{2,1,0:T(2,128)(2,1)S(1)} async-done(((bf16[64,2,1792]{2,1,0:T(2,128)(2,1)}), bf16[64,2,1792]{2,1,0:T(2,128)(2,1)S(1)}, u32[]{:S(2)}, u32[]{:S(2)}) %all-to-all-start.6) | async-done | bytes 458784 | tf_op jit(solution)/shard_map/all_to_all | solution.py:160
  178.5 0.2 reshape.86
  178.7 0.9 convolution_convert_fusion.2
  (19 shorter events, 0.3 us)
Async XLA Ops:
  0.6 156.4 %copy-start = (bf16[1,512,1792]{2,1,0:T(8,128)(2,1)S(1)}, bf16[1,512,1792]{2,1,0:T(8,128)(2,1)}, u32[]{:S(2)}) copy-start(bf16[1,512,1792]{2,1,0:T(8,128)(2,1)} %param.10) | copy-start | bytes 5505028
  2.8 45.8 %all-to-all-start = ((bf16[64,8,1024]{2,1,0:T(8,128)(2,1)}), bf16[64,8,1024]{2,1,0:T(8,128)(2,1)S(1)}, u32[]{:S(2)}, u32[]{:S(2)}) async-start(bf16[64,8,1024]{2,1,0:T(8,128)(2,1)} %address.1), calls=%async_computation | async-start | bytes 2097152 | tf_op jit(solution)/shard_map/all_to_all | solution.py:110
  20.1 1.2 copy-start.1
  22.2 26.4 %collective-permute-start = (bf16[112,1024]{1,0:T(8,128)(2,1)}, bf16[112,1024]{1,0:T(8,128)(2,1)S(1)}, u32[]{:S(2)}, u32[]{:S(2)}) collective-permute-start(bf16[112,1024]{1,0:T(8,128)(2,1)} %get-tuple-element.10), channel_id=1, source_target_pairs={{0,4},{4,0},{32,36},{36,32},{1,5},{5,1},{33,37},{37,33},{2,6},{6,2... | collective-permute-start | bytes 688136 | tf_op jit(solution)/shard_map/ppermute | solution.py:113
  24.7 27.1 %collective-permute-start.1 = (bf16[112,1024]{1,0:T(8,128)(2,1)}, bf16[112,1024]{1,0:T(8,128)(2,1)}, u32[]{:S(2)}, u32[]{:S(2)}) collective-permute-start(bf16[112,1024]{1,0:T(8,128)(2,1)} %get-tuple-element.11), channel_id=1, source_target_pairs={{0,32},{4,36},{32,0},{36,4},{1,33},{5,37},{33,1},{37,5},{2,34},{6,... | collective-permute-start | bytes 688136 | tf_op jit(solution)/shard_map/ppermute | solution.py:113
  28.1 23.7 %collective-permute-start.2 = (bf16[112,1024]{1,0:T(8,128)(2,1)}, bf16[112,1024]{1,0:T(8,128)(2,1)}, u32[]{:S(2)}, u32[]{:S(2)}) collective-permute-start(bf16[112,1024]{1,0:T(8,128)(2,1)} %get-tuple-element.12), channel_id=1, source_target_pairs={{0,36},{4,32},{32,4},{36,0},{1,37},{5,33},{33,5},{37,1},{2,38},{6,... | collective-permute-start | bytes 688136 | tf_op jit(solution)/shard_map/ppermute | solution.py:113
  36.3 63.1 %copy-start.2 = (s32[8,8]{1,0:T(8,128)S(1)}, s32[8,8]{1,0:T(8,128)}, u32[]{:S(2)}) copy-start(s32[8,8]{1,0:T(8,128)} %param.12) | copy-start | bytes 772
  36.3 63.1 %copy-start.3 = (s32[8,8]{1,0:T(8,128)S(1)}, s32[8,8]{1,0:T(8,128)}, u32[]{:S(2)}) copy-start(s32[8,8]{1,0:T(8,128)} %param.11) | copy-start | bytes 772
  36.3 63.1 %copy-start.4 = (f32[8,8]{1,0:T(8,128)S(1)}, f32[8,8]{1,0:T(8,128)}, u32[]{:S(2)}) copy-start(f32[8,8]{1,0:T(8,128)} %param.13) | copy-start | bytes 772
  82.3 25.4 %all-to-all-start.2 = ((bf16[4,4,8,448]{3,2,1,0:T(8,128)(2,1)}), bf16[4,4,8,448]{3,2,1,0:T(8,128)(2,1)S(1)}, u32[]{:S(2)}, u32[]{:S(2)}) async-start(bf16[4,4,8,448]{3,2,1,0:T(8,128)(2,1)} %slice_reduce_fusion), calls=%async_computation.2 | async-start | bytes 262144 | tf_op jit(solution)/shard_map/all_to_all | solution.py:121
  158.7 19.8 %all-to-all-start.6 = ((bf16[64,2,1792]{2,1,0:T(2,128)(2,1)}), bf16[64,2,1792]{2,1,0:T(2,128)(2,1)S(1)}, u32[]{:S(2)}, u32[]{:S(2)}) async-start(bf16[64,2,1792]{2,1,0:T(2,128)(2,1)} %copy.28), calls=%async_computation.6 | async-start | bytes 917504 | tf_op jit(solution)/shard_map/all_to_all | solution.py:160

commit v7 on v6

--- a/solution.py
+++ b/solution.py
@@ -104,24 +104,46 @@
     )(me, tokens, *blocks)
 
 
+CHIPS = ("core",) + EXPERT
+PLACES = [
+    [64 * core + (y + core) % 8 * 8 + (x + core) % 8 for y in range(8) for x in range(8)]
+    for core in range(2)
+]
+
+
+def trade(block, d):
+    flip = (d // 2) * 8 + d % 2
+    pairs = [(places[p], places[p ^ flip]) for places in PLACES for p in range(64)]
+    return lax.ppermute(block, CHIPS, pairs)
+
+
+def spread(pieces):
+    return lax.all_to_all(
+        pieces, CHIPS, split_axis=0, concat_axis=0, tiled=True, axis_index_groups=PLACES
+    )
+
+
 def project(attn_out, w_proj, gate_up_w):
     rows, cols = attn_out.shape[0], w_proj.shape[1]
-    me = lax.axis_index(("yl", "xl")).reshape(1).astype(jnp.int32)
-    tokens = lax.all_to_all(address(attn_out), EXPERT, split_axis=0, concat_axis=0, tiled=True)
+    core = lax.axis_index("core")
+    me = (lax.axis_index(("yl", "xl")) ^ (core * 3)).reshape(1).astype(jnp.int32)
+    tokens = spread(address(attn_out))
     blocks = list(cut(me, w_proj.T))
     for d in range(1, 4):
-        blocks[d] = lax.ppermute(blocks[d], ("yl", "xl"), [(i, i ^ d) for i in range(4)])
-    tokens, gate_up_w = lax.optimization_barrier((tokens, gate_up_w))
+        blocks[d] = trade(blocks[d], d)
+    lane = jnp.arange(4 * cols, dtype=jnp.int32)
+    moves = jnp.broadcast_to((lane >= 2 * cols) & (core == 1), (rows, 4 * cols))
+    tokens, gate_up_w, moves = lax.optimization_barrier((tokens, gate_up_w, moves))
     partial = partial_sums(me, tokens.reshape(64 * rows, -1), blocks)
-    got = lax.all_to_all(
-        partial.reshape(64, rows, -1), EXPERT, split_axis=0, concat_axis=0, tiled=True
-    )
+    got = spread(partial.reshape(64, rows, -1))
     got = got.reshape(4, 2, 4, 2, rows, -1)[..., : 4 * cols].astype(F32)
     got = jnp.sum(got, axis=(1, 3)).astype(BF16)
+    got = jnp.where(moves, jnp.roll(got, 1, axis=0), got)
     got = lax.all_to_all(got, "tensor", split_axis=0, concat_axis=0, tiled=True)
     total = jnp.sum(got.astype(F32), axis=0).astype(BF16)
-    total = total.reshape(4, rows, 2, 2, cols).transpose(1, 2, 0, 3, 4).reshape(rows, 16 * cols)
-    return total, gate_up_w
+    total = total.reshape(4, rows, 2, 2, cols).transpose(1, 2, 0, 3, 4).reshape(rows, 2, 8, cols)
+    total = jnp.where(core == 1, jnp.roll(total[:, ::-1], 1, axis=2), total)
+    return total.reshape(rows, 16 * cols), gate_up_w
 
 
 def per_device(attn_out, w_proj, w_in, w_out, expert_ids, slots, gates):

time: 180 us -> 176 us (0.978)
  waiting for transfers between devices: 37.9 us -> 34.8 us
    ppermute x3, waiting for transfers between devices: 3.2 us -> 0.01 us  [trade(): return lax.ppermute(block, CHIPS, pairs)]
  transfers between devices with their start and end apart: 6 -> 6, of which waited for: 4 -> 3; matrix products, arithmetic and copies ran while one was open for 3% -> 3% of each run, Pallas kernels for 1% -> 1%
where the time goes in v7:
time: 176 us
  blocking collectives  72.1 us (41%)
  starting transfers between devices  48.2 us (27%)
  waiting for transfers between devices  34.8 us (20%)
  local copies, waits for them, and re-layouts  8.78 us (5%)
  Pallas kernels  4.91 us (3%)
  matrix products  4.26 us (2%)
    all_to_all x1, blocking collectives, spread(): lax.all_to_all(pieces, CHIPS, split_axis=0, concat_axis=0, tiled=True, ax...  26.8 us
    all_to_all x1, blocking collectives, per_device(): lax.all_to_all(outgoing, EXPERT, split_axis=0, concat_axis=0, tiled=True)  22 us
    all_to_all x1, starting transfers between devices, spread(): lax.all_to_all(pieces, CHIPS, split_axis=0, concat_axis=0, tiled=True, ax...  17.3 us
    all_to_all x1, starting transfers between devices, project(): got = lax.all_to_all(got, 'tensor', split_axis=0, concat_axis=0, tiled=True)  15.8 us
    all_to_all x1, waiting for transfers between devices, per_device(): lax.all_to_all(result.reshape(groups, CAP, width_block).astype(BF16), EXP...  14.1 us
    all_to_all x1, blocking collectives, per_device(): lax.all_to_all(gate_up.reshape(4, quarter, 2 * slice_units), 'tensor', sp...  12.6 us
    all_to_all x1, waiting for transfers between devices, spread(): lax.all_to_all(pieces, CHIPS, split_axis=0, concat_axis=0, tiled=True, ax...  12.5 us
    all_to_all x1, blocking collectives, per_device(): lax.all_to_all(jnp.broadcast_to(hidden[None], (4, quarter, slice_units)),...  10.8 us
  transfers between devices with their start and end apart: 6, of which 3 were waited for; matrix products, arithmetic and copies ran while one was open for 3% of the time, Pallas kernels for 1%

profile of v7, /device:TPU:2, one launch (start us, length us, event | category | flops | bytes accessed | tf_op | source)
XLA Modules:
  0.0 175.6 jit_solution(13730784406526874256)
XLA Ops:
  0.6 2.2 %address.1 = bf16[64,8,1024]{2,1,0:T(8,128)(2,1)} custom-call(bf16[8,4096]{1,0:T(8,128)(2,1)} %attn_ref.1), custom_call_target="tpu_custom_call" | custom-call | tf_op jit(solution)/shard_map/address/pallas_call | solution.py:47
  2.8 17.3 %all-to-all-start = ((bf16[64,8,1024]{2,1,0:T(8,128)(2,1)}), bf16[64,8,1024]{2,1,0:T(8,128)(2,1)S(1)}, u32[]{:S(2)}, u32[]{:S(2)}) async-start(bf16[64,8,1024]{2,1,0:T(8,128)(2,1)} %address.1), calls=%async_computation | async-start | bytes 2097152 | tf_op jit(solution)/shard_map/all_to_all | solution.py:121
  20.1 1.2 copy-done.1
  21.3 0.9 cut.1
  22.2 2.5 %collective-permute-start = (bf16[112,1024]{1,0:T(8,128)(2,1)}, bf16[112,1024]{1,0:T(8,128)(2,1)S(1)}, u32[]{:S(2)}, u32[]{:S(2)}) collective-permute-start(bf16[112,1024]{1,0:T(8,128)(2,1)} %get-tuple-element.12), channel_id=1, source_target_pairs={{0,4},{4,0},{8,12},{12,8},{16,20},{20,16},{24,28},{28,24},{32,36},... | collective-permute-start | bytes 688136 | tf_op jit(solution)/shard_map/ppermute | solution.py:117
  24.7 3.4 %collective-permute-start.1 = (bf16[112,1024]{1,0:T(8,128)(2,1)}, bf16[112,1024]{1,0:T(8,128)(2,1)}, u32[]{:S(2)}, u32[]{:S(2)}) collective-permute-start(bf16[112,1024]{1,0:T(8,128)(2,1)} %get-tuple-element.13), channel_id=1, source_target_pairs={{0,32},{4,36},{8,40},{12,44},{16,48},{20,52},{24,56},{28,60},{32,0... | collective-permute-start | bytes 688136 | tf_op jit(solution)/shard_map/ppermute | solution.py:117
  28.1 3.3 %collective-permute-start.2 = (bf16[112,1024]{1,0:T(8,128)(2,1)}, bf16[112,1024]{1,0:T(8,128)(2,1)}, u32[]{:S(2)}, u32[]{:S(2)}) collective-permute-start(bf16[112,1024]{1,0:T(8,128)(2,1)} %get-tuple-element.14), channel_id=1, source_target_pairs={{0,36},{4,32},{8,44},{12,40},{16,52},{20,48},{24,60},{28,56},{32,4... | collective-permute-start | bytes 688136 | tf_op jit(solution)/shard_map/ppermute | solution.py:117
  31.4 4.8 %copy.44 = bf16[224,8,2,512]{3,1,2,0:T(8,128)(2,1)} copy(bf16[224,8,2,512]{3,2,1,0:T(2,128)(2,1)} %bitcast.29) | data formatting | bytes 7340032
  36.3 12.5 %all-to-all-done = bf16[64,8,1024]{2,1,0:T(8,128)(2,1)S(1)} async-done(((bf16[64,8,1024]{2,1,0:T(8,128)(2,1)}), bf16[64,8,1024]{2,1,0:T(8,128)(2,1)S(1)}, u32[]{:S(2)}, u32[]{:S(2)}) %all-to-all-start) | async-done | bytes 1048608 | tf_op jit(solution)/shard_map/all_to_all | solution.py:121
  48.8 1.9 %partial_sums.1 = bf16[512,512]{1,0:T(8,128)(2,1)S(1)} custom-call(s32[1]{0:T(128)} %bitcast.me, bf16[512,1024]{1,0:T(8,128)(2,1)S(1)} %bitcast.25, bf16[112,1024]{1,0:T(8,128)(2,1)S(1)} %get-tuple-element.11.refs_0_, bf16[112,1024]{1,0:T(8,128)(2,1)S(1)} %collective-permute-done.refs_1_, bf16[112,1024]{1,0:T(8,128)(2,1)} %collective-permute-done.1.refs_2_, ...), custom_call_target="tpu_custom_call" | custom-call | tf_op jit(solution)/shard_map/partial_sums/pallas_call | solution.py:96
  50.7 26.8 %all_to_all.35 = bf16[64,8,512]{2,1,0:T(8,128)(2,1)S(1)} all-to-all(bf16[64,8,512]{2,1,0:T(8,128)(2,1)S(1)} %bitcast.26), channel_id=1, replica_groups={{0,4,8,12,16,20,24,28,32,36,40,44,48,52,56,60,64,68,72,76,80,84,88,92,9..., dimensions={0} | all-to-all | bytes 1048576 | tf_op jit(solution)/shard_map/all_to_all | solution.py:121
  77.5 0.7 maximum_select_fusion
  78.2 15.8 %all-to-all-start.2 = ((bf16[4,4,8,448]{3,2,1,0:T(8,128)(2,1)}), bf16[4,4,8,448]{3,2,1,0:T(8,128)(2,1)S(1)}, u32[]{:S(2)}, u32[]{:S(2)}) async-start(bf16[4,4,8,448]{3,2,1,0:T(8,128)(2,1)} %maximum_select_fusion), calls=%async_computation.2 | async-start | bytes 262144 | tf_op jit(solution)/shard_map/all_to_all | solution.py:142
  94.1 0.1 copy.38
  94.2 8.2 %all-to-all-done.2 = bf16[4,4,8,448]{3,2,1,0:T(8,128)(2,1)S(1)} async-done(((bf16[4,4,8,448]{3,2,1,0:T(8,128)(2,1)}), bf16[4,4,8,448]{3,2,1,0:T(8,128)(2,1)S(1)}, u32[]{:S(2)}, u32[]{:S(2)}) %all-to-all-start.2) | async-done | bytes 114720 | tf_op jit(solution)/shard_map/all_to_all | solution.py:142
  102.7 0.1 reshape.107
  102.8 0.2 convolution_convert_fusion.1
  103.0 0.5 copy.41
  103.5 22.0 %all_to_all.36 = bf16[64,2,1792]{2,1,0:T(2,128)(2,1)S(1)} all-to-all(bf16[64,2,1792]{2,1,0:T(2,128)(2,1)S(1)} %copy.41), channel_id=1, replica_groups=mesh['plane'=2,'core'=2,'yh'=4,'yl'=2,'xh'=4,'xl'=2,'tensor'=4] {'yh','y..., dimensions={0} | all-to-all | bytes 917504 | tf_op jit(solution)/shard_map/all_to_all | solution.py:165
  125.5 0.2 reshape.103
  125.7 2.7 %convolution_convert_fusion.3 = bf16[128,1024]{1,0:T(8,128)(2,1)S(1)} fusion(bf16[128,1792]{1,0:T(8,128)(2,1)S(1)} %reshape.103, bf16[1792,1024]{1,0:T(8,128)(2,1)} %bitcast.28), kind=kOutput, calls=%fused_computation.4 | convolution fusion | flops 469893120 | bytes 4390912 | tf_op jit(solution)/shard_map/dot_general | solution.py:167
  128.4 12.6 %all_to_all.37 = bf16[4,32,1024]{2,1,0:T(8,128)(2,1)S(1)} all-to-all(bf16[4,32,1024]{2,1,0:T(8,128)(2,1)S(1)} %bitcast.31), channel_id=1, replica_groups=mesh['plane'=2,'core'=2,'yh'=4,'yl'=2,'xh'=4,'xl'=2,'tensor'=4] {'tensor'}, dimensions={0} | all-to-all | bytes 524288 | tf_op jit(solution)/shard_map/all_to_all | solution.py:169
  141.1 10.8 %all_to_all.38 = bf16[4,32,512]{2,1,0:T(8,128)(2,1)S(1)} all-to-all(bf16[4,32,512]{2,1,0:T(8,128)(2,1)S(1)} %broadcast_in_dim.34), channel_id=1, replica_groups=mesh['plane'=2,'core'=2,'yh'=4,'yl'=2,'xh'=4,'xl'=2,'tensor'=4] {'tensor'}, dimensions={0} | all-to-all | bytes 262144 | tf_op jit(solution)/shard_map/all_to_all | solution.py:174
  151.9 0.4 convolution_convert_fusion
  152.4 1.2 copy.43
  153.6 6.0 %all-to-all-start.6 = ((bf16[64,2,1792]{2,1,0:T(2,128)(2,1)}), bf16[64,2,1792]{2,1,0:T(2,128)(2,1)S(1)}, u32[]{:S(2)}, u32[]{:S(2)}) async-start(bf16[64,2,1792]{2,1,0:T(2,128)(2,1)} %copy.43), calls=%async_computation.6 | async-start | bytes 917504 | tf_op jit(solution)/shard_map/all_to_all | solution.py:182
  159.6 0.1 concatenate.12
  159.7 0.1 reshape.102
  159.8 0.6 broadcast_select_fusion.1
  160.5 14.1 %all-to-all-done.6 = bf16[64,2,1792]{2,1,0:T(2,128)(2,1)S(1)} async-done(((bf16[64,2,1792]{2,1,0:T(2,128)(2,1)}), bf16[64,2,1792]{2,1,0:T(2,128)(2,1)S(1)}, u32[]{:S(2)}, u32[]{:S(2)}) %all-to-all-start.6) | async-done | bytes 458784 | tf_op jit(solution)/shard_map/all_to_all | solution.py:182
  174.5 0.2 reshape.106
  174.7 0.9 convolution_convert_fusion.2
  (34 shorter events, 0.6 us)
Async XLA Ops:
  0.6 151.3 %copy-start = (bf16[1,512,1792]{2,1,0:T(8,128)(2,1)S(1)}, bf16[1,512,1792]{2,1,0:T(8,128)(2,1)}, u32[]{:S(2)}) copy-start(bf16[1,512,1792]{2,1,0:T(8,128)(2,1)} %param.10) | copy-start | bytes 5505028
  2.8 46.0 %all-to-all-start = ((bf16[64,8,1024]{2,1,0:T(8,128)(2,1)}), bf16[64,8,1024]{2,1,0:T(8,128)(2,1)S(1)}, u32[]{:S(2)}, u32[]{:S(2)}) async-start(bf16[64,8,1024]{2,1,0:T(8,128)(2,1)} %address.1), calls=%async_computation | async-start | bytes 2097152 | tf_op jit(solution)/shard_map/all_to_all | solution.py:121
  20.1 1.2 copy-start.1
  22.2 26.6 %collective-permute-start = (bf16[112,1024]{1,0:T(8,128)(2,1)}, bf16[112,1024]{1,0:T(8,128)(2,1)S(1)}, u32[]{:S(2)}, u32[]{:S(2)}) collective-permute-start(bf16[112,1024]{1,0:T(8,128)(2,1)} %get-tuple-element.12), channel_id=1, source_target_pairs={{0,4},{4,0},{8,12},{12,8},{16,20},{20,16},{24,28},{28,24},{32,36},... | collective-permute-start | bytes 688136 | tf_op jit(solution)/shard_map/ppermute | solution.py:117
  24.7 24.1 %collective-permute-start.1 = (bf16[112,1024]{1,0:T(8,128)(2,1)}, bf16[112,1024]{1,0:T(8,128)(2,1)}, u32[]{:S(2)}, u32[]{:S(2)}) collective-permute-start(bf16[112,1024]{1,0:T(8,128)(2,1)} %get-tuple-element.13), channel_id=1, source_target_pairs={{0,32},{4,36},{8,40},{12,44},{16,48},{20,52},{24,56},{28,60},{32,0... | collective-permute-start | bytes 688136 | tf_op jit(solution)/shard_map/ppermute | solution.py:117
  28.1 20.7 %collective-permute-start.2 = (bf16[112,1024]{1,0:T(8,128)(2,1)}, bf16[112,1024]{1,0:T(8,128)(2,1)}, u32[]{:S(2)}, u32[]{:S(2)}) collective-permute-start(bf16[112,1024]{1,0:T(8,128)(2,1)} %get-tuple-element.14), channel_id=1, source_target_pairs={{0,36},{4,32},{8,44},{12,40},{16,52},{20,48},{24,60},{28,56},{32,4... | collective-permute-start | bytes 688136 | tf_op jit(solution)/shard_map/ppermute | solution.py:117
  36.2 57.7 %copy-start.2 = (s32[8,8]{1,0:T(8,128)S(1)}, s32[8,8]{1,0:T(8,128)}, u32[]{:S(2)}) copy-start(s32[8,8]{1,0:T(8,128)} %param.12) | copy-start | bytes 772
  36.2 57.7 %copy-start.3 = (s32[8,8]{1,0:T(8,128)S(1)}, s32[8,8]{1,0:T(8,128)}, u32[]{:S(2)}) copy-start(s32[8,8]{1,0:T(8,128)} %param.11) | copy-start | bytes 772
  36.2 57.7 %copy-start.4 = (f32[8,8]{1,0:T(8,128)S(1)}, f32[8,8]{1,0:T(8,128)}, u32[]{:S(2)}) copy-start(f32[8,8]{1,0:T(8,128)} %param.13) | copy-start | bytes 772
  78.2 24.2 %all-to-all-start.2 = ((bf16[4,4,8,448]{3,2,1,0:T(8,128)(2,1)}), bf16[4,4,8,448]{3,2,1,0:T(8,128)(2,1)S(1)}, u32[]{:S(2)}, u32[]{:S(2)}) async-start(bf16[4,4,8,448]{3,2,1,0:T(8,128)(2,1)} %maximum_select_fusion), calls=%async_computation.2 | async-start | bytes 262144 | tf_op jit(solution)/shard_map/all_to_all | solution.py:142
  153.6 20.9 %all-to-all-start.6 = ((bf16[64,2,1792]{2,1,0:T(2,128)(2,1)}), bf16[64,2,1792]{2,1,0:T(2,128)(2,1)S(1)}, u32[]{:S(2)}, u32[]{:S(2)}) async-start(bf16[64,2,1792]{2,1,0:T(2,128)(2,1)} %copy.43), calls=%async_computation.6 | async-start | bytes 917504 | tf_op jit(solution)/shard_map/all_to_all | solution.py:182

commit v8 on v7

--- a/solution.py
+++ b/solution.py
@@ -17,65 +17,74 @@
 ANY = pl.BlockSpec(memory_space=pl.ANY)
 
 
-def address_kernel(attn_ref, sent_ref, staged, in_sems, out_sems):
+def prepare_kernel(me, attn_ref, w_ref, sent_ref, *refs):
+    pieces, (staged, w_held, in_sems, out_sems) = refs[:4], refs[4:]
     part = attn_ref.shape[1] // 4
-    copies = []
+    arrivals = []
     for m in range(4):
         for x in range(4):
             at = (m // 2) * 8 + x * 2 + m % 2
-            copies.append(
+            arrivals.append(
                 pltpu.make_async_copy(
                     attn_ref.at[:, pl.ds(m * part, part)], staged.at[at], in_sems.at[at]
                 )
             )
-    for copy in copies:
+    weights = pltpu.make_async_copy(w_ref, w_held, in_sems.at[16])
+    for copy in arrivals:
         copy.start()
-    for copy in copies:
+    weights.start()
+    for copy in arrivals:
         copy.wait()
-    copies = [
+    leaving = [
         pltpu.make_async_copy(staged, sent_ref.at[pl.ds(yh * 16, 16)], out_sems.at[yh])
         for yh in range(4)
     ]
-    for copy in copies:
+    for copy in leaving:
         copy.start()
-    for copy in copies:
+    weights.wait()
+    for d in range(4):
+        start = pl.multiple_of((me[0] ^ d) * part, part)
+        leaving.append(
+            pltpu.make_async_copy(w_held.at[:, pl.ds(start, part)], pieces[d], out_sems.at[4 + d])
+        )
+        leaving[-1].start()
+    for copy in leaving:
         copy.wait()
 
 
-def address(attn_out):
-    rows, part = attn_out.shape[0], attn_out.shape[1] // 4
+def prepare(me, attn_out, w_cols):
+    rows, cols = attn_out.shape[0], w_cols.shape[0]
+    part = attn_out.shape[1] // 4
     return pl.pallas_call(
-        address_kernel,
-        out_shape=jax.ShapeDtypeStruct((64, rows, part), BF16),
-        in_specs=[ANY],
-        out_specs=ANY,
+        prepare_kernel,
+        out_shape=[jax.ShapeDtypeStruct((64, rows, part), BF16)]
+        + [jax.ShapeDtypeStruct((cols, part), BF16)] * 4,
+        in_specs=[SMEM, ANY, ANY],
+        out_specs=[ANY] * 5,
         scratch_shapes=[
             pltpu.VMEM((16, rows, part), BF16),
-            pltpu.SemaphoreType.DMA((16,)),
-            pltpu.SemaphoreType.DMA((4,)),
+            pltpu.VMEM(w_cols.shape, BF16),
+            pltpu.SemaphoreType.DMA((17,)),
+            pltpu.SemaphoreType.DMA((8,)),
         ],
         compiler_params=pltpu.CompilerParams(vmem_limit_bytes=58 << 20),
-        name="address",
-    )(attn_out)
-
-
-def cut_kernel(me, w_ref, *pieces):
-    part = pieces[0].shape[1]
-    for d in range(4):
-        start = pl.multiple_of((me[0] ^ d) * part, part)
-        pieces[d][...] = w_ref[:, pl.ds(start, part)]
-
-
-def cut(me, w_cols):
-    cols, part = w_cols.shape[0], w_cols.shape[1] // 4
+        name="prepare",
+    )(me, attn_out, w_cols)
+
+
+def gate_up_kernel(routed, weights, out_ref):
+    out_ref[...] = jnp.dot(routed[...], weights[...], preferred_element_type=F32).astype(BF16)
+
+
+def gate_up_product(routed, weights):
     return pl.pallas_call(
-        cut_kernel,
-        out_shape=[jax.ShapeDtypeStruct((cols, part), BF16)] * 4,
-        in_specs=[SMEM, VMEM],
-        out_specs=[VMEM] * 4,
-        compiler_params=pltpu.CompilerParams(vmem_limit_bytes=8 << 20),
-        name="cut",
-    )(me, w_cols)
+        gate_up_kernel,
+        out_shape=jax.ShapeDtypeStruct((routed.shape[0], weights.shape[1]), BF16),
+        in_specs=[VMEM] * 2,
+        out_specs=VMEM,
+        compiler_params=pltpu.CompilerParams(vmem_limit_bytes=16 << 20),
+        name="gate_up_product",
+    )(routed, weights)
 
 
 def partial_kernel(me, tokens, *refs):
@@ -127,8 +136,8 @@
     rows, cols = attn_out.shape[0], w_proj.shape[1]
     core = lax.axis_index("core")
     me = (lax.axis_index(("yl", "xl")) ^ (core * 3)).reshape(1).astype(jnp.int32)
-    tokens = spread(address(attn_out))
-    blocks = list(cut(me, w_proj.T))
+    sent, *blocks = prepare(me, attn_out, w_proj.T)
+    tokens = spread(sent)
     for d in range(1, 4):
         blocks[d] = trade(blocks[d], d)
     lane = jnp.arange(4 * cols, dtype=jnp.int32)
@@ -164,7 +173,7 @@
     down_w = w_out.reshape(slice_units, width_block)
     received = lax.all_to_all(outgoing, EXPERT, split_axis=0, concat_axis=0, tiled=True)
     flat_rows = received.reshape(groups * CAP, width_block)
-    gate_up = jnp.dot(flat_rows, gate_up_w, preferred_element_type=F32).astype(BF16)
+    gate_up = gate_up_product(flat_rows, gate_up_w)
     quarter = groups * CAP // 4
     gate_up = lax.all_to_all(
         gate_up.reshape(4, quarter, 2 * slice_units), "tensor", split_axis=0, concat_axis=0, tiled=True

time: 176 us -> 177 us (level)
  matrix products: 4.26 us -> 1.57 us
  waiting for transfers between devices: 34.8 us -> 36.8 us
    dot_general x1 -> x0, matrix products: 2.69 us -> none  [per_device(): jnp.dot(flat_rows, gate_up_w, preferred_element_type=F32).astype(BF16)]
    all_to_all x1, waiting for transfers between devices: 12.5 us -> 14.5 us  [spread(): lax.all_to_all(pieces, CHIPS, split_axis=0, concat_axis=0, tiled=True, ax...]
    unnamed x11 -> x13, local copies, waits for them, and re-layouts: 6.02 us -> 6.94 us
  transfers between devices with their start and end apart: 6 -> 6, of which waited for: 3 -> 3; matrix products, arithmetic and copies ran while one was open for 3% -> 3% of each run, Pallas kernels for 1% -> 0%
where the time goes in v8:
time: 177 us; the launch traced here: 176 us
  blocking collectives  72.3 us (41%)
  starting transfers between devices  48.2 us (27%)
  waiting for transfers between devices  36.8 us (21%)
  local copies, waits for them, and re-layouts  9.69 us (5%)
  Pallas kernels  5.19 us (3%)
    all_to_all x1, blocking collectives, spread(): lax.all_to_all(pieces, CHIPS, split_axis=0, concat_axis=0, tiled=True, ax...  26.9 us
    all_to_all x1, blocking collectives, per_device(): lax.all_to_all(outgoing, EXPERT, split_axis=0, concat_axis=0, tiled=True)  22 us
    all_to_all x1, starting transfers between devices, spread(): lax.all_to_all(pieces, CHIPS, split_axis=0, concat_axis=0, tiled=True, ax...  17.3 us
    all_to_all x1, starting transfers between devices, project(): got = lax.all_to_all(got, 'tensor', split_axis=0, concat_axis=0, tiled=True)  15.8 us
    all_to_all x1, waiting for transfers between devices, spread(): lax.all_to_all(pieces, CHIPS, split_axis=0, concat_axis=0, tiled=True, ax...  14.5 us
    all_to_all x1, waiting for transfers between devices, per_device(): lax.all_to_all(result.reshape(groups, CAP, width_block).astype(BF16), EXP...  14.1 us
    all_to_all x1, blocking collectives, per_device(): lax.all_to_all(gate_up.reshape(4, quarter, 2 * slice_units), 'tensor', sp...  12.6 us
    all_to_all x1, blocking collectives, per_device(): lax.all_to_all(jnp.broadcast_to(hidden[None], (4, quarter, slice_units)),...  10.8 us
  transfers between devices with their start and end apart: 6, of which 3 were waited for; matrix products, arithmetic and copies ran while one was open for 3% of the time, Pallas kernels for 0%

profile of v8, /device:TPU:2, one launch (start us, length us, event | category | flops | bytes accessed | tf_op | source)
XLA Modules:
  0.0 176.3 jit_solution(4170409455103456515)
XLA Ops:
  0.7 2.7 %prepare.1 = (bf16[64,8,1024]{2,1,0:T(8,128)(2,1)}, bf16[112,1024]{1,0:T(8,128)(2,1)}, bf16[112,1024]{1,0:T(8,128)(2,1)}, bf16[112,1024]{1,0:T(8,128)(2,1)}, bf16[112,1024]{1,0:T(8,128)(2,1)}) custom-call(s32[1]{0:T(128)} %bitcast.me, bf16[8,4096]{1,0:T(8,128)(2,1)} %attn_ref.1, bf16[112,4096]{1,0:T(8,128)(2,1)} %bitcast.29), custom_call_target="tpu_custom_call" | custom-call | tf_op jit(solution)/shard_map/prepare/pallas_call | solution.py:58
  3.4 17.3 %all-to-all-start = ((bf16[64,8,1024]{2,1,0:T(8,128)(2,1)}), bf16[64,8,1024]{2,1,0:T(8,128)(2,1)S(1)}, u32[]{:S(2)}, u32[]{:S(2)}) async-start(bf16[64,8,1024]{2,1,0:T(8,128)(2,1)} %get-tuple-element.10), calls=%async_computation | async-start | bytes 2097152 | tf_op jit(solution)/shard_map/all_to_all | solution.py:130
  20.6 2.5 %collective-permute-start = (bf16[112,1024]{1,0:T(8,128)(2,1)}, bf16[112,1024]{1,0:T(8,128)(2,1)S(1)}, u32[]{:S(2)}, u32[]{:S(2)}) collective-permute-start(bf16[112,1024]{1,0:T(8,128)(2,1)} %get-tuple-element.14), channel_id=1, source_target_pairs={{0,4},{4,0},{8,12},{12,8},{16,20},{20,16},{24,28},{28,24},{32,36},... | collective-permute-start | bytes 688136 | tf_op jit(solution)/shard_map/ppermute | solution.py:126
  23.1 3.4 %collective-permute-start.1 = (bf16[112,1024]{1,0:T(8,128)(2,1)}, bf16[112,1024]{1,0:T(8,128)(2,1)}, u32[]{:S(2)}, u32[]{:S(2)}) collective-permute-start(bf16[112,1024]{1,0:T(8,128)(2,1)} %get-tuple-element.15), channel_id=1, source_target_pairs={{0,32},{4,36},{8,40},{12,44},{16,48},{20,52},{24,56},{28,60},{32,0... | collective-permute-start | bytes 688136 | tf_op jit(solution)/shard_map/ppermute | solution.py:126
  26.5 3.3 %collective-permute-start.2 = (bf16[112,1024]{1,0:T(8,128)(2,1)}, bf16[112,1024]{1,0:T(8,128)(2,1)}, u32[]{:S(2)}, u32[]{:S(2)}) collective-permute-start(bf16[112,1024]{1,0:T(8,128)(2,1)} %get-tuple-element.16), channel_id=1, source_target_pairs={{0,36},{4,32},{8,44},{12,40},{16,52},{20,48},{24,60},{28,56},{32,4... | collective-permute-start | bytes 688136 | tf_op jit(solution)/shard_map/ppermute | solution.py:126
  29.9 4.9 %copy.45 = bf16[224,8,2,512]{3,1,2,0:T(8,128)(2,1)} copy(bf16[224,8,2,512]{3,2,1,0:T(2,128)(2,1)} %bitcast.27) | data formatting | bytes 7340032
  34.8 14.5 %all-to-all-done = bf16[64,8,1024]{2,1,0:T(8,128)(2,1)S(1)} async-done(((bf16[64,8,1024]{2,1,0:T(8,128)(2,1)}), bf16[64,8,1024]{2,1,0:T(8,128)(2,1)S(1)}, u32[]{:S(2)}, u32[]{:S(2)}) %all-to-all-start) | async-done | bytes 1048608 | tf_op jit(solution)/shard_map/all_to_all | solution.py:130
  49.4 1.9 %partial_sums.1 = bf16[512,512]{1,0:T(8,128)(2,1)S(1)} custom-call(s32[1]{0:T(128)} %bitcast.me, bf16[512,1024]{1,0:T(8,128)(2,1)S(1)} %bitcast.24, bf16[112,1024]{1,0:T(8,128)(2,1)S(1)} %copy-done.2, bf16[112,1024]{1,0:T(8,128)(2,1)S(1)} %collective-permute-done.refs_1_, bf16[112,1024]{1,0:T(8,128)(2,1)} %collective-permute-done.1.refs_2_, ...), custom_call_target="tpu_custom_call" | custom-call | tf_op jit(solution)/shard_map/partial_sums/pallas_call | solution.py:105
  51.2 26.9 %all_to_all.35 = bf16[64,8,512]{2,1,0:T(8,128)(2,1)S(1)} all-to-all(bf16[64,8,512]{2,1,0:T(8,128)(2,1)S(1)} %bitcast.25), channel_id=1, replica_groups={{0,4,8,12,16,20,24,28,32,36,40,44,48,52,56,60,64,68,72,76,80,84,88,92,9..., dimensions={0} | all-to-all | bytes 1048576 | tf_op jit(solution)/shard_map/all_to_all | solution.py:130
  78.2 0.7 maximum_select_fusion
  78.9 15.8 %all-to-all-start.2 = ((bf16[4,4,8,448]{3,2,1,0:T(8,128)(2,1)}), bf16[4,4,8,448]{3,2,1,0:T(8,128)(2,1)S(1)}, u32[]{:S(2)}, u32[]{:S(2)}) async-start(bf16[4,4,8,448]{3,2,1,0:T(8,128)(2,1)} %maximum_select_fusion), calls=%async_computation.2 | async-start | bytes 262144 | tf_op jit(solution)/shard_map/all_to_all | solution.py:151
  94.7 0.1 convert_reduce_fusion.1
  94.8 0.1 copy.39
  94.9 8.2 %all-to-all-done.2 = bf16[4,4,8,448]{3,2,1,0:T(8,128)(2,1)S(1)} async-done(((bf16[4,4,8,448]{3,2,1,0:T(8,128)(2,1)}), bf16[4,4,8,448]{3,2,1,0:T(8,128)(2,1)S(1)}, u32[]{:S(2)}, u32[]{:S(2)}) %all-to-all-start.2) | async-done | bytes 114720 | tf_op jit(solution)/shard_map/all_to_all | solution.py:151
  103.4 0.1 reshape.107
  103.5 0.2 convolution_convert_fusion.1
  103.8 0.5 copy.42
  104.2 22.0 %all_to_all.36 = bf16[64,2,1792]{2,1,0:T(2,128)(2,1)S(1)} all-to-all(bf16[64,2,1792]{2,1,0:T(2,128)(2,1)S(1)} %copy.42), channel_id=1, replica_groups=mesh['plane'=2,'core'=2,'yh'=4,'yl'=2,'xh'=4,'xl'=2,'tensor'=4] {'yh','y..., dimensions={0} | all-to-all | bytes 917504 | tf_op jit(solution)/shard_map/all_to_all | solution.py:174
  126.2 0.2 reshape.103.routed
  126.4 2.0 %copy-done.1 = bf16[224,8,2,512]{3,1,2,0:T(8,128)(2,1)S(1)} copy-done((bf16[224,8,2,512]{3,1,2,0:T(8,128)(2,1)S(1)}, bf16[224,8,2,512]{3,1,2,0:T(8,128)(2,1)}, u32[]{:S(2)}) %copy-start.1) | copy-done | bytes 3670040
  128.4 0.6 gate_up_product.1
  129.1 12.6 %all_to_all.37 = bf16[4,32,1024]{2,1,0:T(8,128)(2,1)S(1)} all-to-all(bf16[4,32,1024]{2,1,0:T(8,128)(2,1)S(1)} %bitcast.26), channel_id=1, replica_groups=mesh['plane'=2,'core'=2,'yh'=4,'yl'=2,'xh'=4,'xl'=2,'tensor'=4] {'tensor'}, dimensions={0} | all-to-all | bytes 524288 | tf_op jit(solution)/shard_map/all_to_all | solution.py:178
  141.8 10.8 %all_to_all.38 = bf16[4,32,512]{2,1,0:T(8,128)(2,1)S(1)} all-to-all(bf16[4,32,512]{2,1,0:T(8,128)(2,1)S(1)} %broadcast_in_dim.34), channel_id=1, replica_groups=mesh['plane'=2,'core'=2,'yh'=4,'yl'=2,'xh'=4,'xl'=2,'tensor'=4] {'tensor'}, dimensions={0} | all-to-all | bytes 262144 | tf_op jit(solution)/shard_map/all_to_all | solution.py:183
  152.7 0.4 convolution_convert_fusion
  153.1 1.2 copy.44
  154.3 6.0 %all-to-all-start.6 = ((bf16[64,2,1792]{2,1,0:T(2,128)(2,1)}), bf16[64,2,1792]{2,1,0:T(2,128)(2,1)S(1)}, u32[]{:S(2)}, u32[]{:S(2)}) async-start(bf16[64,2,1792]{2,1,0:T(2,128)(2,1)} %copy.44), calls=%async_computation.6 | async-start | bytes 917504 | tf_op jit(solution)/shard_map/all_to_all | solution.py:191
  160.3 0.1 concatenate.12
  160.4 0.1 reshape.102
  160.6 0.6 broadcast_select_fusion.1
  161.2 14.1 %all-to-all-done.6 = bf16[64,2,1792]{2,1,0:T(2,128)(2,1)S(1)} async-done(((bf16[64,2,1792]{2,1,0:T(2,128)(2,1)}), bf16[64,2,1792]{2,1,0:T(2,128)(2,1)S(1)}, u32[]{:S(2)}, u32[]{:S(2)}) %all-to-all-start.6) | async-done | bytes 458784 | tf_op jit(solution)/shard_map/all_to_all | solution.py:191
  175.2 0.2 reshape.106
  175.4 0.9 convolution_convert_fusion.2
  (35 shorter events, 0.5 us)
Async XLA Ops:
  0.6 152.0 %copy-start = (bf16[1,512,1792]{2,1,0:T(8,128)(2,1)S(1)}, bf16[1,512,1792]{2,1,0:T(8,128)(2,1)}, u32[]{:S(2)}) copy-start(bf16[1,512,1792]{2,1,0:T(8,128)(2,1)} %param.10) | copy-start | bytes 5505028
  3.4 46.0 %all-to-all-start = ((bf16[64,8,1024]{2,1,0:T(8,128)(2,1)}), bf16[64,8,1024]{2,1,0:T(8,128)(2,1)S(1)}, u32[]{:S(2)}, u32[]{:S(2)}) async-start(bf16[64,8,1024]{2,1,0:T(8,128)(2,1)} %get-tuple-element.10), calls=%async_computation | async-start | bytes 2097152 | tf_op jit(solution)/shard_map/all_to_all | solution.py:130
  20.6 28.7 %collective-permute-start = (bf16[112,1024]{1,0:T(8,128)(2,1)}, bf16[112,1024]{1,0:T(8,128)(2,1)S(1)}, u32[]{:S(2)}, u32[]{:S(2)}) collective-permute-start(bf16[112,1024]{1,0:T(8,128)(2,1)} %get-tuple-element.14), channel_id=1, source_target_pairs={{0,4},{4,0},{8,12},{12,8},{16,20},{20,16},{24,28},{28,24},{32,36},... | collective-permute-start | bytes 688136 | tf_op jit(solution)/shard_map/ppermute | solution.py:126
  23.1 26.2 %collective-permute-start.1 = (bf16[112,1024]{1,0:T(8,128)(2,1)}, bf16[112,1024]{1,0:T(8,128)(2,1)}, u32[]{:S(2)}, u32[]{:S(2)}) collective-permute-start(bf16[112,1024]{1,0:T(8,128)(2,1)} %get-tuple-element.15), channel_id=1, source_target_pairs={{0,32},{4,36},{8,40},{12,44},{16,48},{20,52},{24,56},{28,60},{32,0... | collective-permute-start | bytes 688136 | tf_op jit(solution)/shard_map/ppermute | solution.py:126
  26.5 22.8 %collective-permute-start.2 = (bf16[112,1024]{1,0:T(8,128)(2,1)}, bf16[112,1024]{1,0:T(8,128)(2,1)}, u32[]{:S(2)}, u32[]{:S(2)}) collective-permute-start(bf16[112,1024]{1,0:T(8,128)(2,1)} %get-tuple-element.16), channel_id=1, source_target_pairs={{0,36},{4,32},{8,44},{12,40},{16,52},{20,48},{24,60},{28,56},{32,4... | collective-permute-start | bytes 688136 | tf_op jit(solution)/shard_map/ppermute | solution.py:126
  29.9 19.5 %copy-start.2 = (bf16[112,1024]{1,0:T(8,128)(2,1)S(1)}, bf16[112,1024]{1,0:T(8,128)(2,1)}, u32[]{:S(2)}) copy-start(bf16[112,1024]{1,0:T(8,128)(2,1)} %get-tuple-element.13.refs_0_) | copy-start | bytes 688132
  51.2 43.5 %copy-start.3 = (s32[8,8]{1,0:T(8,128)S(1)}, s32[8,8]{1,0:T(8,128)}, u32[]{:S(2)}) copy-start(s32[8,8]{1,0:T(8,128)} %param.12) | copy-start | bytes 772
  51.2 43.5 %copy-start.4 = (s32[8,8]{1,0:T(8,128)S(1)}, s32[8,8]{1,0:T(8,128)}, u32[]{:S(2)}) copy-start(s32[8,8]{1,0:T(8,128)} %param.11) | copy-start | bytes 772
  51.2 43.5 %copy-start.5 = (f32[8,8]{1,0:T(8,128)S(1)}, f32[8,8]{1,0:T(8,128)}, u32[]{:S(2)}) copy-start(f32[8,8]{1,0:T(8,128)} %param.13) | copy-start | bytes 772
  78.9 24.2 %all-to-all-start.2 = ((bf16[4,4,8,448]{3,2,1,0:T(8,128)(2,1)}), bf16[4,4,8,448]{3,2,1,0:T(8,128)(2,1)S(1)}, u32[]{:S(2)}, u32[]{:S(2)}) async-start(bf16[4,4,8,448]{3,2,1,0:T(8,128)(2,1)} %maximum_select_fusion), calls=%async_computation.2 | async-start | bytes 262144 | tf_op jit(solution)/shard_map/all_to_all | solution.py:151
  126.4 2.0 %copy-start.1 = (bf16[224,8,2,512]{3,1,2,0:T(8,128)(2,1)S(1)}, bf16[224,8,2,512]{3,1,2,0:T(8,128)(2,1)}, u32[]{:S(2)}) copy-start(bf16[224,8,2,512]{3,1,2,0:T(8,128)(2,1)} %copy.45) | copy-start | bytes 11010052
  154.3 20.9 %all-to-all-start.6 = ((bf16[64,2,1792]{2,1,0:T(2,128)(2,1)}), bf16[64,2,1792]{2,1,0:T(2,128)(2,1)S(1)}, u32[]{:S(2)}, u32[]{:S(2)}) async-start(bf16[64,2,1792]{2,1,0:T(2,128)(2,1)} %copy.44), calls=%async_computation.6 | async-start | bytes 917504 | tf_op jit(solution)/shard_map/all_to_all | solution.py:191

commit v9 on v7

--- a/solution.py
+++ b/solution.py
@@ -123,7 +123,7 @@
     )
 
 
-def project(attn_out, w_proj, gate_up_w):
+def project(attn_out, w_proj, beside):
     rows, cols = attn_out.shape[0], w_proj.shape[1]
     core = lax.axis_index("core")
     me = (lax.axis_index(("yl", "xl")) ^ (core * 3)).reshape(1).astype(jnp.int32)
@@ -133,7 +133,7 @@
         blocks[d] = trade(blocks[d], d)
     lane = jnp.arange(4 * cols, dtype=jnp.int32)
     moves = jnp.broadcast_to((lane >= 2 * cols) & (core == 1), (rows, 4 * cols))
-    tokens, gate_up_w, moves = lax.optimization_barrier((tokens, gate_up_w, moves))
+    tokens, beside, moves = lax.optimization_barrier((tokens, beside, moves))
     partial = partial_sums(me, tokens.reshape(64 * rows, -1), blocks)
     got = spread(partial.reshape(64, rows, -1))
     got = got.reshape(4, 2, 4, 2, rows, -1)[..., : 4 * cols].astype(F32)
@@ -143,7 +143,7 @@
     total = jnp.sum(got.astype(F32), axis=0).astype(BF16)
     total = total.reshape(4, rows, 2, 2, cols).transpose(1, 2, 0, 3, 4).reshape(rows, 2, 8, cols)
     total = jnp.where(core == 1, jnp.roll(total[:, ::-1], 1, axis=2), total)
-    return total.reshape(rows, 16 * cols), gate_up_w
+    return lax.optimization_barrier(total.reshape(rows, 16 * cols)), beside
 
 
 def per_device(attn_out, w_proj, w_in, w_out, expert_ids, slots, gates):
@@ -154,14 +154,16 @@
     matches = (expert_ids[:, :, None] == row // (HSPLIT * CAP)) & (slots[:, :, None] == row % CAP)
     dispatch_w = jnp.sum(matches.astype(F32), axis=1).astype(BF16)
     combine_w = jnp.sum(jnp.where(matches, gates[:, :, None], F32(0.0)), axis=1)
-    projected, gate_up_w = project(attn_out, w_proj, w_in.reshape(width_block, 2 * slice_units))
+    beside = (w_in.reshape(width_block, 2 * slice_units), dispatch_w.T, combine_w)
+    projected, (gate_up_w, dispatch_w, combine_w) = project(attn_out, w_proj, beside)
     outgoing = jnp.einsum(
-        "tgc,td->gcd",
-        dispatch_w.reshape(-1, groups, CAP),
+        "gct,td->gcd",
+        dispatch_w.reshape(groups, CAP, -1),
         projected,
         preferred_element_type=F32,
     ).astype(BF16)
     down_w = w_out.reshape(slice_units, width_block)
+    projected, outgoing = lax.optimization_barrier((projected, outgoing))
     received = lax.all_to_all(outgoing, EXPERT, split_axis=0, concat_axis=0, tiled=True)
     flat_rows = received.reshape(groups * CAP, width_block)
     gate_up = jnp.dot(flat_rows, gate_up_w, preferred_element_type=F32).astype(BF16)

time: 176 us -> 175 us (level)
  blocking collectives: 72.1 us -> 92.2 us
  waiting for transfers between devices: 34.8 us -> 20.7 us
  starting transfers between devices: 48.2 us -> 42.2 us
    all_to_all x0 -> x1, blocking collectives: none -> 20 us  [per_device(): lax.all_to_all(result.reshape(groups, CAP, width_block).astype(BF16), EXP...]
    all_to_all x1 -> x0, waiting for transfers between devices: 14.1 us -> none  [per_device(): lax.all_to_all(result.reshape(groups, CAP, width_block).astype(BF16), EXP...]
    all_to_all x1 -> x0, starting transfers between devices: 5.96 us -> none  [per_device(): lax.all_to_all(result.reshape(groups, CAP, width_block).astype(BF16), EXP...]
    unnamed x11 -> x13, local copies, waits for them, and re-layouts: 6.02 us -> 6.05 us
  transfers between devices with their start and end apart: 6 -> 5, of which waited for: 3 -> 2; matrix products, arithmetic and copies ran while one was open for 3% -> 3% of each run, Pallas kernels for 1% -> 1%
where the time goes in v9:
time: 175 us; the launch traced here: 174 us
  blocking collectives  92.2 us (53%)
  starting transfers between devices  42.2 us (24%)
  waiting for transfers between devices  20.7 us (12%)
  local copies, waits for them, and re-layouts  7.92 us (5%)
  Pallas kernels  4.91 us (3%)
  matrix products  4.25 us (2%)
    all_to_all x1, blocking collectives, spread(): lax.all_to_all(pieces, CHIPS, split_axis=0, concat_axis=0, tiled=True, ax...  26.8 us
    all_to_all x1, blocking collectives, per_device(): lax.all_to_all(outgoing, EXPERT, split_axis=0, concat_axis=0, tiled=True)  22 us
    all_to_all x1, blocking collectives, per_device(): lax.all_to_all(result.reshape(groups, CAP, width_block).astype(BF16), EXP...  20 us
    all_to_all x1, starting transfers between devices, spread(): lax.all_to_all(pieces, CHIPS, split_axis=0, concat_axis=0, tiled=True, ax...  17.3 us
    all_to_all x1, starting transfers between devices, project(): got = lax.all_to_all(got, 'tensor', split_axis=0, concat_axis=0, tiled=True)  15.8 us
    all_to_all x1, blocking collectives, per_device(): lax.all_to_all(gate_up.reshape(4, quarter, 2 * slice_units), 'tensor', sp...  12.6 us
    all_to_all x1, waiting for transfers between devices, spread(): lax.all_to_all(pieces, CHIPS, split_axis=0, concat_axis=0, tiled=True, ax...  12.3 us
    all_to_all x1, blocking collectives, per_device(): lax.all_to_all(jnp.broadcast_to(hidden[None], (4, quarter, slice_units)),...  10.8 us
  transfers between devices with their start and end apart: 5, of which 2 were waited for; matrix products, arithmetic and copies ran while one was open for 3% of the time, Pallas kernels for 1%

profile of v9, /device:TPU:2, one launch (start us, length us, event | category | flops | bytes accessed | tf_op | source)
XLA Modules:
  0.0 174.1 jit_solution(9325079765943192721)
XLA Ops:
  0.6 2.1 %address.1 = bf16[64,8,1024]{2,1,0:T(8,128)(2,1)} custom-call(bf16[8,4096]{1,0:T(8,128)(2,1)} %attn_ref.1), custom_call_target="tpu_custom_call" | custom-call | tf_op jit(solution)/shard_map/address/pallas_call | solution.py:47
  2.8 17.3 %all-to-all-start = ((bf16[64,8,1024]{2,1,0:T(8,128)(2,1)}), bf16[64,8,1024]{2,1,0:T(8,128)(2,1)S(1)}, u32[]{:S(2)}, u32[]{:S(2)}) async-start(bf16[64,8,1024]{2,1,0:T(8,128)(2,1)} %address.1), calls=%async_computation | async-start | bytes 2097152 | tf_op jit(solution)/shard_map/all_to_all | solution.py:121
  20.1 1.2 copy-done.1
  21.3 0.9 cut.1
  22.2 2.5 %collective-permute-start = (bf16[112,1024]{1,0:T(8,128)(2,1)}, bf16[112,1024]{1,0:T(8,128)(2,1)S(1)}, u32[]{:S(2)}, u32[]{:S(2)}) collective-permute-start(bf16[112,1024]{1,0:T(8,128)(2,1)} %get-tuple-element.16), channel_id=1, source_target_pairs={{0,4},{4,0},{8,12},{12,8},{16,20},{20,16},{24,28},{28,24},{32,36},... | collective-permute-start | bytes 688136 | tf_op jit(solution)/shard_map/ppermute | solution.py:117
  24.7 3.4 %collective-permute-start.1 = (bf16[112,1024]{1,0:T(8,128)(2,1)}, bf16[112,1024]{1,0:T(8,128)(2,1)}, u32[]{:S(2)}, u32[]{:S(2)}) collective-permute-start(bf16[112,1024]{1,0:T(8,128)(2,1)} %get-tuple-element.17), channel_id=1, source_target_pairs={{0,32},{4,36},{8,40},{12,44},{16,48},{20,52},{24,56},{28,60},{32,0... | collective-permute-start | bytes 688136 | tf_op jit(solution)/shard_map/ppermute | solution.py:117
  28.1 3.3 %collective-permute-start.2 = (bf16[112,1024]{1,0:T(8,128)(2,1)}, bf16[112,1024]{1,0:T(8,128)(2,1)}, u32[]{:S(2)}, u32[]{:S(2)}) collective-permute-start(bf16[112,1024]{1,0:T(8,128)(2,1)} %get-tuple-element.18), channel_id=1, source_target_pairs={{0,36},{4,32},{8,44},{12,40},{16,52},{20,48},{24,60},{28,56},{32,4... | collective-permute-start | bytes 688136 | tf_op jit(solution)/shard_map/ppermute | solution.py:117
  31.4 4.8 %copy.41 = bf16[224,8,2,512]{3,1,2,0:T(8,128)(2,1)} copy(bf16[224,8,2,512]{3,2,1,0:T(2,128)(2,1)} %bitcast.32) | data formatting | bytes 7340032
  36.3 0.1 select_reduce_fusion
  36.4 12.3 %all-to-all-done = bf16[64,8,1024]{2,1,0:T(8,128)(2,1)S(1)} async-done(((bf16[64,8,1024]{2,1,0:T(8,128)(2,1)}), bf16[64,8,1024]{2,1,0:T(8,128)(2,1)S(1)}, u32[]{:S(2)}, u32[]{:S(2)}) %all-to-all-start) | async-done | bytes 1048608 | tf_op jit(solution)/shard_map/all_to_all | solution.py:121
  48.8 1.9 %partial_sums.1 = bf16[512,512]{1,0:T(8,128)(2,1)S(1)} custom-call(s32[1]{0:T(128)} %bitcast.1.me, bf16[512,1024]{1,0:T(8,128)(2,1)S(1)} %bitcast.28, bf16[112,1024]{1,0:T(8,128)(2,1)S(1)} %get-tuple-element.15.refs_0_, bf16[112,1024]{1,0:T(8,128)(2,1)S(1)} %collective-permute-done.refs_1_, bf16[112,1024]{1,0:T(8,128)(2,1)} %collective-permute-done.1.refs_2_, ...), custom_call_target="tpu_custom_call" | custom-call | tf_op jit(solution)/shard_map/partial_sums/pallas_call | solution.py:96
  50.6 26.8 %all_to_all.35 = bf16[64,8,512]{2,1,0:T(8,128)(2,1)S(1)} all-to-all(bf16[64,8,512]{2,1,0:T(8,128)(2,1)S(1)} %bitcast.29), channel_id=1, replica_groups={{0,4,8,12,16,20,24,28,32,36,40,44,48,52,56,60,64,68,72,76,80,84,88,92,9..., dimensions={0} | all-to-all | bytes 1048576 | tf_op jit(solution)/shard_map/all_to_all | solution.py:121
  77.4 0.1 slice_reduce_fusion
  77.5 0.7 maximum_select_fusion
  78.2 15.8 %all-to-all-start.2 = ((bf16[4,4,8,448]{3,2,1,0:T(8,128)(2,1)}), bf16[4,4,8,448]{3,2,1,0:T(8,128)(2,1)S(1)}, u32[]{:S(2)}, u32[]{:S(2)}) async-start(bf16[4,4,8,448]{3,2,1,0:T(8,128)(2,1)} %maximum_select_fusion), calls=%async_computation.2 | async-start | bytes 262144 | tf_op jit(solution)/shard_map/all_to_all | solution.py:142
  93.9 0.1 copy.36
  94.1 8.4 %all-to-all-done.2 = bf16[4,4,8,448]{3,2,1,0:T(8,128)(2,1)S(1)} async-done(((bf16[4,4,8,448]{3,2,1,0:T(8,128)(2,1)}), bf16[4,4,8,448]{3,2,1,0:T(8,128)(2,1)S(1)}, u32[]{:S(2)}, u32[]{:S(2)}) %all-to-all-start.2) | async-done | bytes 114720 | tf_op jit(solution)/shard_map/all_to_all | solution.py:142
  102.5 0.1 reshape.80
  102.6 0.1 reshape.82
  102.8 0.1 concatenate.12
  102.9 0.2 convolution_convert_fusion.1
  103.2 0.5 copy.38
  103.6 22.0 %all_to_all.36 = bf16[64,2,1792]{2,1,0:T(2,128)(2,1)S(1)} all-to-all(bf16[64,2,1792]{2,1,0:T(2,128)(2,1)S(1)} %copy.38), channel_id=1, replica_groups=mesh['plane'=2,'core'=2,'yh'=4,'yl'=2,'xh'=4,'xl'=2,'tensor'=4] {'yh','y..., dimensions={0} | all-to-all | bytes 917504 | tf_op jit(solution)/shard_map/all_to_all | solution.py:167
  125.6 0.2 reshape.84
  125.8 2.7 %convolution_convert_fusion.3 = bf16[128,1024]{1,0:T(8,128)(2,1)S(1)} fusion(bf16[128,1792]{1,0:T(8,128)(2,1)S(1)} %reshape.84, bf16[1792,1024]{1,0:T(8,128)(2,1)} %bitcast.31), kind=kOutput, calls=%fused_computation.4 | convolution fusion | flops 469893120 | bytes 4390912 | tf_op jit(solution)/shard_map/dot_general | solution.py:169
  128.5 12.6 %all_to_all.37 = bf16[4,32,1024]{2,1,0:T(8,128)(2,1)S(1)} all-to-all(bf16[4,32,1024]{2,1,0:T(8,128)(2,1)S(1)} %bitcast.34), channel_id=1, replica_groups=mesh['plane'=2,'core'=2,'yh'=4,'yl'=2,'xh'=4,'xl'=2,'tensor'=4] {'tensor'}, dimensions={0} | all-to-all | bytes 524288 | tf_op jit(solution)/shard_map/all_to_all | solution.py:171
  141.3 10.8 %all_to_all.38 = bf16[4,32,512]{2,1,0:T(8,128)(2,1)S(1)} all-to-all(bf16[4,32,512]{2,1,0:T(8,128)(2,1)S(1)} %broadcast_in_dim.34), channel_id=1, replica_groups=mesh['plane'=2,'core'=2,'yh'=4,'yl'=2,'xh'=4,'xl'=2,'tensor'=4] {'tensor'}, dimensions={0} | all-to-all | bytes 262144 | tf_op jit(solution)/shard_map/all_to_all | solution.py:176
  152.1 0.4 convolution_convert_fusion
  152.5 0.5 copy.40
  153.0 20.0 %all_to_all.39 = bf16[64,2,1792]{2,1,0:T(2,128)(2,1)S(1)} all-to-all(bf16[64,2,1792]{2,1,0:T(2,128)(2,1)S(1)} %copy.40), channel_id=1, replica_groups=mesh['plane'=2,'core'=2,'yh'=4,'yl'=2,'xh'=4,'xl'=2,'tensor'=4] {'yh','y..., dimensions={0} | all-to-all | bytes 917504 | tf_op jit(solution)/shard_map/all_to_all | solution.py:184
  173.0 0.2 reshape.87
  173.2 0.9 convolution_convert_fusion.2
  (33 shorter events, 0.3 us)
Async XLA Ops:
  0.6 151.5 %copy-start = (bf16[1,512,1792]{2,1,0:T(8,128)(2,1)S(1)}, bf16[1,512,1792]{2,1,0:T(8,128)(2,1)}, u32[]{:S(2)}) copy-start(bf16[1,512,1792]{2,1,0:T(8,128)(2,1)} %param.10) | copy-start | bytes 5505028
  2.8 45.9 %all-to-all-start = ((bf16[64,8,1024]{2,1,0:T(8,128)(2,1)}), bf16[64,8,1024]{2,1,0:T(8,128)(2,1)S(1)}, u32[]{:S(2)}, u32[]{:S(2)}) async-start(bf16[64,8,1024]{2,1,0:T(8,128)(2,1)} %address.1), calls=%async_computation | async-start | bytes 2097152 | tf_op jit(solution)/shard_map/all_to_all | solution.py:121
  20.1 1.2 copy-start.1
  22.2 26.6 %collective-permute-start = (bf16[112,1024]{1,0:T(8,128)(2,1)}, bf16[112,1024]{1,0:T(8,128)(2,1)S(1)}, u32[]{:S(2)}, u32[]{:S(2)}) collective-permute-start(bf16[112,1024]{1,0:T(8,128)(2,1)} %get-tuple-element.16), channel_id=1, source_target_pairs={{0,4},{4,0},{8,12},{12,8},{16,20},{20,16},{24,28},{28,24},{32,36},... | collective-permute-start | bytes 688136 | tf_op jit(solution)/shard_map/ppermute | solution.py:117
  24.7 24.1 %collective-permute-start.1 = (bf16[112,1024]{1,0:T(8,128)(2,1)}, bf16[112,1024]{1,0:T(8,128)(2,1)}, u32[]{:S(2)}, u32[]{:S(2)}) collective-permute-start(bf16[112,1024]{1,0:T(8,128)(2,1)} %get-tuple-element.17), channel_id=1, source_target_pairs={{0,32},{4,36},{8,40},{12,44},{16,48},{20,52},{24,56},{28,60},{32,0... | collective-permute-start | bytes 688136 | tf_op jit(solution)/shard_map/ppermute | solution.py:117
  28.1 20.7 %collective-permute-start.2 = (bf16[112,1024]{1,0:T(8,128)(2,1)}, bf16[112,1024]{1,0:T(8,128)(2,1)}, u32[]{:S(2)}, u32[]{:S(2)}) collective-permute-start(bf16[112,1024]{1,0:T(8,128)(2,1)} %get-tuple-element.18), channel_id=1, source_target_pairs={{0,36},{4,32},{8,44},{12,40},{16,52},{20,48},{24,60},{28,56},{32,4... | collective-permute-start | bytes 688136 | tf_op jit(solution)/shard_map/ppermute | solution.py:117
  31.4 4.9 %copy-start.3 = (f32[8,8]{1,0:T(8,128)S(1)}, f32[8,8]{1,0:T(8,128)}, u32[]{:S(2)}) copy-start(f32[8,8]{1,0:T(8,128)} %param.13) | copy-start | bytes 772
  31.4 4.9 %copy-start.4 = (s32[8,8]{1,0:T(8,128)S(1)}, s32[8,8]{1,0:T(8,128)}, u32[]{:S(2)}) copy-start(s32[8,8]{1,0:T(8,128)} %param.12) | copy-start | bytes 772
  31.4 4.9 %copy-start.5 = (s32[8,8]{1,0:T(8,128)S(1)}, s32[8,8]{1,0:T(8,128)}, u32[]{:S(2)}) copy-start(s32[8,8]{1,0:T(8,128)} %param.11) | copy-start | bytes 772
  78.2 24.2 %all-to-all-start.2 = ((bf16[4,4,8,448]{3,2,1,0:T(8,128)(2,1)}), bf16[4,4,8,448]{3,2,1,0:T(8,128)(2,1)S(1)}, u32[]{:S(2)}, u32[]{:S(2)}) async-start(bf16[4,4,8,448]{3,2,1,0:T(8,128)(2,1)} %maximum_select_fusion), calls=%async_computation.2 | async-start | bytes 262144 | tf_op jit(solution)/shard_map/all_to_all | solution.py:142
  102.9 25.6 %copy-start.2 = (bf16[8,1792]{1,0:T(8,128)(2,1)}, bf16[8,1792]{1,0:T(8,128)(2,1)S(1)}, u32[]{:S(2)}) copy-start(bf16[8,1792]{1,0:T(8,128)(2,1)S(1)} %broadcast_select_fusion) | copy-start | bytes 86020

commit v10 on v8

--- a/solution.py
+++ b/solution.py
@@ -72,17 +72,33 @@
     )(me, attn_out, w_cols)
 
 
-def gate_up_kernel(routed, weights, out_ref):
-    out_ref[...] = jnp.dot(routed[...], weights[...], preferred_element_type=F32).astype(BF16)
+def gate_up_kernel(routed, weights, out_ref, total):
+    step = pl.program_id(0)
+    depth = weights.shape[0]
+    columns = pl.ds(pl.multiple_of(step * depth, depth), depth)
+
+    @pl.when(step == 0)
+    def _():
+        total[...] = jnp.zeros_like(total)
+
+    total[...] += jnp.dot(routed[:, columns], weights[...], preferred_element_type=F32)
+
+    @pl.when(step == pl.num_programs(0) - 1)
+    def _():
+        out_ref[...] = total[...].astype(BF16)
 
 
 def gate_up_product(routed, weights):
+    rows, depth = routed.shape
+    units, steps = weights.shape[1], 7
     return pl.pallas_call(
         gate_up_kernel,
-        out_shape=jax.ShapeDtypeStruct((routed.shape[0], weights.shape[1]), BF16),
-        in_specs=[VMEM] * 2,
+        grid=(steps,),
+        out_shape=jax.ShapeDtypeStruct((rows, units), BF16),
+        in_specs=[VMEM, pl.BlockSpec((depth // steps, units), lambda k: (k, 0))],
         out_specs=VMEM,
-        compiler_params=pltpu.CompilerParams(vmem_limit_bytes=16 << 20),
+        scratch_shapes=[pltpu.VMEM((rows, units), F32)],
+        compiler_params=pltpu.CompilerParams(vmem_limit_bytes=58 << 20),
         name="gate_up_product",
     )(routed, weights)
 
@@ -132,7 +148,7 @@
     )
 
 
-def project(attn_out, w_proj, gate_up_w):
+def project(attn_out, w_proj, beside):
     rows, cols = attn_out.shape[0], w_proj.shape[1]
     core = lax.axis_index("core")
     me = (lax.axis_index(("yl", "xl")) ^ (core * 3)).reshape(1).astype(jnp.int32)
@@ -142,7 +158,7 @@
         blocks[d] = trade(blocks[d], d)
     lane = jnp.arange(4 * cols, dtype=jnp.int32)
     moves = jnp.broadcast_to((lane >= 2 * cols) & (core == 1), (rows, 4 * cols))
-    tokens, gate_up_w, moves = lax.optimization_barrier((tokens, gate_up_w, moves))
+    tokens, beside, moves = lax.optimization_barrier((tokens, beside, moves))
     partial = partial_sums(me, tokens.reshape(64 * rows, -1), blocks)
     got = spread(partial.reshape(64, rows, -1))
     got = got.reshape(4, 2, 4, 2, rows, -1)[..., : 4 * cols].astype(F32)
@@ -152,7 +168,7 @@
     total = jnp.sum(got.astype(F32), axis=0).astype(BF16)
     total = total.reshape(4, rows, 2, 2, cols).transpose(1, 2, 0, 3, 4).reshape(rows, 2, 8, cols)
     total = jnp.where(core == 1, jnp.roll(total[:, ::-1], 1, axis=2), total)
-    return total.reshape(rows, 16 * cols), gate_up_w
+    return lax.optimization_barrier(total.reshape(rows, 16 * cols)), beside
 
 
 def per_device(attn_out, w_proj, w_in, w_out, expert_ids, slots, gates):
@@ -163,14 +179,16 @@
     matches = (expert_ids[:, :, None] == row // (HSPLIT * CAP)) & (slots[:, :, None] == row % CAP)
     dispatch_w = jnp.sum(matches.astype(F32), axis=1).astype(BF16)
     combine_w = jnp.sum(jnp.where(matches, gates[:, :, None], F32(0.0)), axis=1)
-    projected, gate_up_w = project(attn_out, w_proj, w_in.reshape(width_block, 2 * slice_units))
+    beside = (w_in.reshape(width_block, 2 * slice_units), dispatch_w.T, combine_w)
+    projected, (gate_up_w, dispatch_w, combine_w) = project(attn_out, w_proj, beside)
     outgoing = jnp.einsum(
-        "tgc,td->gcd",
-        dispatch_w.reshape(-1, groups, CAP),
+        "gct,td->gcd",
+        dispatch_w.reshape(groups, CAP, -1),
         projected,
         preferred_element_type=F32,
     ).astype(BF16)
     down_w = w_out.reshape(slice_units, width_block)
+    projected, outgoing = lax.optimization_barrier((projected, outgoing))
     received = lax.all_to_all(outgoing, EXPERT, split_axis=0, concat_axis=0, tiled=True)
     flat_rows = received.reshape(groups * CAP, width_block)
     gate_up = gate_up_product(flat_rows, gate_up_w)

time: 177 us -> 180 us (1.017)
  blocking collectives: 72.3 us -> 92.7 us
  waiting for transfers between devices: 36.8 us -> 22.7 us
  starting transfers between devices: 48.2 us -> 42.3 us
  Pallas kernels: 5.19 us -> 10.6 us
  local copies, waits for them, and re-layouts: 9.69 us -> 7.56 us
    all_to_all x0 -> x1, blocking collectives: none -> 19.7 us  [per_device(): lax.all_to_all(result.reshape(groups, CAP, width_block).astype(BF16), EXP...]
    all_to_all x1 -> x0, waiting for transfers between devices: 14.1 us -> none  [per_device(): lax.all_to_all(result.reshape(groups, CAP, width_block).astype(BF16), EXP...]
    all_to_all x1 -> x0, starting transfers between devices: 5.96 us -> none  [per_device(): lax.all_to_all(result.reshape(groups, CAP, width_block).astype(BF16), EXP...]
    pallas_call x1, Pallas kernels: 0.65 us -> 6.05 us  [gate_up_product(): pl.pallas_call(gate_up_kernel, grid=(steps,), out_shape=jax.ShapeDtypeStr...]
    unnamed x13, local copies, waits for them, and re-layouts: 6.94 us -> 4.91 us
  transfers between devices with their start and end apart: 6 -> 5, of which waited for: 3 -> 2; matrix products, arithmetic and copies ran while one was open for 3% -> 3% of each run, Pallas kernels for 0% -> 0%
where the time goes in v10:
time: 180 us; the launch traced here: 179 us
  blocking collectives  92.7 us (52%)
  starting transfers between devices  42.3 us (24%)
  waiting for transfers between devices  22.7 us (13%)
  Pallas kernels  10.6 us (6%)
  local copies, waits for them, and re-layouts  7.56 us (4%)
    all_to_all x1, blocking collectives, spread(): lax.all_to_all(pieces, CHIPS, split_axis=0, concat_axis=0, tiled=True, ax...  26.7 us
    all_to_all x1, blocking collectives, per_device(): lax.all_to_all(outgoing, EXPERT, split_axis=0, concat_axis=0, tiled=True)  22 us
    all_to_all x1, blocking collectives, per_device(): lax.all_to_all(result.reshape(groups, CAP, width_block).astype(BF16), EXP...  19.7 us
    all_to_all x1, starting transfers between devices, spread(): lax.all_to_all(pieces, CHIPS, split_axis=0, concat_axis=0, tiled=True, ax...  17.3 us
    all_to_all x1, starting transfers between devices, project(): got = lax.all_to_all(got, 'tensor', split_axis=0, concat_axis=0, tiled=True)  15.8 us
    all_to_all x1, waiting for transfers between devices, spread(): lax.all_to_all(pieces, CHIPS, split_axis=0, concat_axis=0, tiled=True, ax...  14.4 us
    all_to_all x1, blocking collectives, per_device(): lax.all_to_all(gate_up.reshape(4, quarter, 2 * slice_units), 'tensor', sp...  13.4 us
    all_to_all x1, blocking collectives, per_device(): lax.all_to_all(jnp.broadcast_to(hidden[None], (4, quarter, slice_units)),...  10.9 us
  transfers between devices with their start and end apart: 5, of which 2 were waited for; matrix products, arithmetic and copies ran while one was open for 3% of the time, Pallas kernels for 0%

profile of v10, /device:TPU:2, one launch (start us, length us, event | category | flops | bytes accessed | tf_op | source)
XLA Modules:
  0.0 179.4 jit_solution(9517517687505174110)
XLA Ops:
  0.6 0.0 copy-start
  0.7 2.7 %prepare.1 = (bf16[64,8,1024]{2,1,0:T(8,128)(2,1)}, bf16[112,1024]{1,0:T(8,128)(2,1)}, bf16[112,1024]{1,0:T(8,128)(2,1)}, bf16[112,1024]{1,0:T(8,128)(2,1)}, bf16[112,1024]{1,0:T(8,128)(2,1)}) custom-call(s32[1]{0:T(128)} %bitcast.me, bf16[8,4096]{1,0:T(8,128)(2,1)} %attn_ref.1, bf16[112,4096]{1,0:T(8,128)(2,1)} %bitcast.32), custom_call_target="tpu_custom_call" | custom-call | tf_op jit(solution)/shard_map/prepare/pallas_call | solution.py:58
  3.4 17.3 %all-to-all-start = ((bf16[64,8,1024]{2,1,0:T(8,128)(2,1)}), bf16[64,8,1024]{2,1,0:T(8,128)(2,1)S(1)}, u32[]{:S(2)}, u32[]{:S(2)}) async-start(bf16[64,8,1024]{2,1,0:T(8,128)(2,1)} %get-tuple-element.14), calls=%async_computation | async-start | bytes 2097152 | tf_op jit(solution)/shard_map/all_to_all | solution.py:146
  20.7 2.5 %collective-permute-start = (bf16[112,1024]{1,0:T(8,128)(2,1)}, bf16[112,1024]{1,0:T(8,128)(2,1)S(1)}, u32[]{:S(2)}, u32[]{:S(2)}) collective-permute-start(bf16[112,1024]{1,0:T(8,128)(2,1)} %get-tuple-element.18), channel_id=1, source_target_pairs={{0,4},{4,0},{8,12},{12,8},{16,20},{20,16},{24,28},{28,24},{32,36},... | collective-permute-start | bytes 688136 | tf_op jit(solution)/shard_map/ppermute | solution.py:142
  23.1 3.4 %collective-permute-start.1 = (bf16[112,1024]{1,0:T(8,128)(2,1)}, bf16[112,1024]{1,0:T(8,128)(2,1)}, u32[]{:S(2)}, u32[]{:S(2)}) collective-permute-start(bf16[112,1024]{1,0:T(8,128)(2,1)} %get-tuple-element.19), channel_id=1, source_target_pairs={{0,32},{4,36},{8,40},{12,44},{16,48},{20,52},{24,56},{28,60},{32,0... | collective-permute-start | bytes 688136 | tf_op jit(solution)/shard_map/ppermute | solution.py:142
  26.6 3.3 %collective-permute-start.2 = (bf16[112,1024]{1,0:T(8,128)(2,1)}, bf16[112,1024]{1,0:T(8,128)(2,1)}, u32[]{:S(2)}, u32[]{:S(2)}) collective-permute-start(bf16[112,1024]{1,0:T(8,128)(2,1)} %get-tuple-element.20), channel_id=1, source_target_pairs={{0,36},{4,32},{8,44},{12,40},{16,52},{20,48},{24,60},{28,56},{32,4... | collective-permute-start | bytes 688136 | tf_op jit(solution)/shard_map/ppermute | solution.py:142
  29.9 4.9 %copy.42 = bf16[224,8,2,512]{3,1,2,0:T(8,128)(2,1)} copy(bf16[224,8,2,512]{3,2,1,0:T(2,128)(2,1)} %bitcast.29) | data formatting | bytes 7340032
  34.9 0.1 select_reduce_fusion
  35.0 14.4 %all-to-all-done = bf16[64,8,1024]{2,1,0:T(8,128)(2,1)S(1)} async-done(((bf16[64,8,1024]{2,1,0:T(8,128)(2,1)}), bf16[64,8,1024]{2,1,0:T(8,128)(2,1)S(1)}, u32[]{:S(2)}, u32[]{:S(2)}) %all-to-all-start) | async-done | bytes 1048608 | tf_op jit(solution)/shard_map/all_to_all | solution.py:146
  49.4 1.9 %partial_sums.1 = bf16[512,512]{1,0:T(8,128)(2,1)S(1)} custom-call(s32[1]{0:T(128)} %bitcast.me, bf16[512,1024]{1,0:T(8,128)(2,1)S(1)} %bitcast.26, bf16[112,1024]{1,0:T(8,128)(2,1)S(1)} %copy-done.1, bf16[112,1024]{1,0:T(8,128)(2,1)S(1)} %collective-permute-done.refs_1_, bf16[112,1024]{1,0:T(8,128)(2,1)} %collective-permute-done.1.refs_2_, ...), custom_call_target="tpu_custom_call" | custom-call | tf_op jit(solution)/shard_map/partial_sums/pallas_call | solution.py:121
  51.2 26.7 %all_to_all.35 = bf16[64,8,512]{2,1,0:T(8,128)(2,1)S(1)} all-to-all(bf16[64,8,512]{2,1,0:T(8,128)(2,1)S(1)} %bitcast.27), channel_id=1, replica_groups={{0,4,8,12,16,20,24,28,32,36,40,44,48,52,56,60,64,68,72,76,80,84,88,92,9..., dimensions={0} | all-to-all | bytes 1048576 | tf_op jit(solution)/shard_map/all_to_all | solution.py:146
  78.0 0.1 slice_reduce_fusion
  78.1 0.7 maximum_select_fusion
  78.8 15.8 %all-to-all-start.2 = ((bf16[4,4,8,448]{3,2,1,0:T(8,128)(2,1)}), bf16[4,4,8,448]{3,2,1,0:T(8,128)(2,1)S(1)}, u32[]{:S(2)}, u32[]{:S(2)}) async-start(bf16[4,4,8,448]{3,2,1,0:T(8,128)(2,1)} %maximum_select_fusion), calls=%async_computation.2 | async-start | bytes 262144 | tf_op jit(solution)/shard_map/all_to_all | solution.py:167
  94.5 0.1 copy.37
  94.6 8.4 %all-to-all-done.2 = bf16[4,4,8,448]{3,2,1,0:T(8,128)(2,1)S(1)} async-done(((bf16[4,4,8,448]{3,2,1,0:T(8,128)(2,1)}), bf16[4,4,8,448]{3,2,1,0:T(8,128)(2,1)S(1)}, u32[]{:S(2)}, u32[]{:S(2)}) %all-to-all-start.2) | async-done | bytes 114720 | tf_op jit(solution)/shard_map/all_to_all | solution.py:167
  103.0 0.1 reshape.80
  103.2 0.1 reshape.82
  103.4 0.1 concatenate.12
  103.5 0.2 convolution_convert_fusion.1
  103.7 0.5 copy.39
  104.2 22.0 %all_to_all.36 = bf16[64,2,1792]{2,1,0:T(2,128)(2,1)S(1)} all-to-all(bf16[64,2,1792]{2,1,0:T(2,128)(2,1)S(1)} %copy.39), channel_id=1, replica_groups=mesh['plane'=2,'core'=2,'yh'=4,'yl'=2,'xh'=4,'xl'=2,'tensor'=4] {'yh','y..., dimensions={0} | all-to-all | bytes 917504 | tf_op jit(solution)/shard_map/all_to_all | solution.py:192
  126.2 1.0 reshape.84.routed
  127.2 6.1 %gate_up_product.1 = bf16[128,1024]{1,0:T(8,128)(2,1)} custom-call(bf16[128,1792]{1,0:T(8,128)(2,1)} %reshape.84.routed, bf16[1792,1024]{1,0:T(8,128)(2,1)} %bitcast.28), custom_call_target="tpu_custom_call" | custom-call | tf_op jit(solution)/shard_map/gate_up_product/pallas_call | solution.py:94
  133.2 13.4 %all_to_all.37 = bf16[4,32,1024]{2,1,0:T(8,128)(2,1)S(1)} all-to-all(bf16[4,32,1024]{2,1,0:T(8,128)(2,1)} %bitcast.31), channel_id=1, replica_groups=mesh['plane'=2,'core'=2,'yh'=4,'yl'=2,'xh'=4,'xl'=2,'tensor'=4] {'tensor'}, dimensions={0} | all-to-all | bytes 524288 | tf_op jit(solution)/shard_map/all_to_all | solution.py:196
  146.7 10.9 %all_to_all.38 = bf16[4,32,512]{2,1,0:T(8,128)(2,1)S(1)} all-to-all(bf16[4,32,512]{2,1,0:T(8,128)(2,1)S(1)} %broadcast_in_dim.34), channel_id=1, replica_groups=mesh['plane'=2,'core'=2,'yh'=4,'yl'=2,'xh'=4,'xl'=2,'tensor'=4] {'tensor'}, dimensions={0} | all-to-all | bytes 262144 | tf_op jit(solution)/shard_map/all_to_all | solution.py:201
  157.6 0.1 dot_general.12
  157.7 0.4 convolution_convert_fusion
  158.1 0.5 copy.41
  158.6 19.7 %all_to_all.39 = bf16[64,2,1792]{2,1,0:T(2,128)(2,1)S(1)} all-to-all(bf16[64,2,1792]{2,1,0:T(2,128)(2,1)S(1)} %copy.41), channel_id=1, replica_groups=mesh['plane'=2,'core'=2,'yh'=4,'yl'=2,'xh'=4,'xl'=2,'tensor'=4] {'yh','y..., dimensions={0} | all-to-all | bytes 917504 | tf_op jit(solution)/shard_map/all_to_all | solution.py:209
  178.3 0.2 reshape.87
  178.5 0.9 convolution_convert_fusion.2
  (32 shorter events, 0.2 us)
Async XLA Ops:
  0.6 157.1 %copy-start = (bf16[1,512,1792]{2,1,0:T(8,128)(2,1)S(1)}, bf16[1,512,1792]{2,1,0:T(8,128)(2,1)}, u32[]{:S(2)}) copy-start(bf16[1,512,1792]{2,1,0:T(8,128)(2,1)} %param.10) | copy-start | bytes 5505028
  3.4 46.0 %all-to-all-start = ((bf16[64,8,1024]{2,1,0:T(8,128)(2,1)}), bf16[64,8,1024]{2,1,0:T(8,128)(2,1)S(1)}, u32[]{:S(2)}, u32[]{:S(2)}) async-start(bf16[64,8,1024]{2,1,0:T(8,128)(2,1)} %get-tuple-element.14), calls=%async_computation | async-start | bytes 2097152 | tf_op jit(solution)/shard_map/all_to_all | solution.py:146
  20.7 28.7 %collective-permute-start = (bf16[112,1024]{1,0:T(8,128)(2,1)}, bf16[112,1024]{1,0:T(8,128)(2,1)S(1)}, u32[]{:S(2)}, u32[]{:S(2)}) collective-permute-start(bf16[112,1024]{1,0:T(8,128)(2,1)} %get-tuple-element.18), channel_id=1, source_target_pairs={{0,4},{4,0},{8,12},{12,8},{16,20},{20,16},{24,28},{28,24},{32,36},... | collective-permute-start | bytes 688136 | tf_op jit(solution)/shard_map/ppermute | solution.py:142
  23.1 26.2 %collective-permute-start.1 = (bf16[112,1024]{1,0:T(8,128)(2,1)}, bf16[112,1024]{1,0:T(8,128)(2,1)}, u32[]{:S(2)}, u32[]{:S(2)}) collective-permute-start(bf16[112,1024]{1,0:T(8,128)(2,1)} %get-tuple-element.19), channel_id=1, source_target_pairs={{0,32},{4,36},{8,40},{12,44},{16,48},{20,52},{24,56},{28,60},{32,0... | collective-permute-start | bytes 688136 | tf_op jit(solution)/shard_map/ppermute | solution.py:142
  26.6 22.8 %collective-permute-start.2 = (bf16[112,1024]{1,0:T(8,128)(2,1)}, bf16[112,1024]{1,0:T(8,128)(2,1)}, u32[]{:S(2)}, u32[]{:S(2)}) collective-permute-start(bf16[112,1024]{1,0:T(8,128)(2,1)} %get-tuple-element.20), channel_id=1, source_target_pairs={{0,36},{4,32},{8,44},{12,40},{16,52},{20,48},{24,60},{28,56},{32,4... | collective-permute-start | bytes 688136 | tf_op jit(solution)/shard_map/ppermute | solution.py:142
  29.9 4.9 %copy-start.3 = (f32[8,8]{1,0:T(8,128)S(1)}, f32[8,8]{1,0:T(8,128)}, u32[]{:S(2)}) copy-start(f32[8,8]{1,0:T(8,128)} %param.13) | copy-start | bytes 772
  29.9 4.9 %copy-start.4 = (s32[8,8]{1,0:T(8,128)S(1)}, s32[8,8]{1,0:T(8,128)}, u32[]{:S(2)}) copy-start(s32[8,8]{1,0:T(8,128)} %param.12) | copy-start | bytes 772
  29.9 4.9 %copy-start.5 = (s32[8,8]{1,0:T(8,128)S(1)}, s32[8,8]{1,0:T(8,128)}, u32[]{:S(2)}) copy-start(s32[8,8]{1,0:T(8,128)} %param.11) | copy-start | bytes 772
  29.9 19.4 %copy-start.1 = (bf16[112,1024]{1,0:T(8,128)(2,1)S(1)}, bf16[112,1024]{1,0:T(8,128)(2,1)}, u32[]{:S(2)}) copy-start(bf16[112,1024]{1,0:T(8,128)(2,1)} %get-tuple-element.17.refs_0_) | copy-start | bytes 688132
  78.8 24.2 %all-to-all-start.2 = ((bf16[4,4,8,448]{3,2,1,0:T(8,128)(2,1)}), bf16[4,4,8,448]{3,2,1,0:T(8,128)(2,1)S(1)}, u32[]{:S(2)}, u32[]{:S(2)}) async-start(bf16[4,4,8,448]{3,2,1,0:T(8,128)(2,1)} %maximum_select_fusion), calls=%async_computation.2 | async-start | bytes 262144 | tf_op jit(solution)/shard_map/all_to_all | solution.py:167
  103.5 29.7 %copy-start.2 = (bf16[8,1792]{1,0:T(8,128)(2,1)}, bf16[8,1792]{1,0:T(8,128)(2,1)S(1)}, u32[]{:S(2)}) copy-start(bf16[8,1792]{1,0:T(8,128)(2,1)S(1)} %broadcast_select_fusion) | copy-start | bytes 86020

commit v11 on v9

--- a/solution.py
+++ b/solution.py
@@ -59,11 +59,14 @@
     )(attn_out)
 
 
+PARTNERS = (0, 3, 1, 2)
+
+
 def cut_kernel(me, w_ref, *pieces):
     part = pieces[0].shape[1]
-    for d in range(4):
+    for i, d in enumerate(PARTNERS):
         start = pl.multiple_of((me[0] ^ d) * part, part)
-        pieces[d][...] = w_ref[:, pl.ds(start, part)]
+        pieces[i][...] = w_ref[:, pl.ds(start, part)]
 
 
 def cut(me, w_cols):
@@ -83,8 +86,8 @@
     cols = blocks[0].shape[0]
     spare = wide.shape[0] - 4 * cols
     wide[pl.ds(4 * cols, spare), :] = jnp.zeros((spare, wide.shape[1]), BF16)
-    for d in range(4):
-        wide[pl.ds(pl.multiple_of((me[0] ^ d) * cols, 16), cols), :] = blocks[d][...]
+    for i, d in enumerate(PARTNERS):
+        wide[pl.ds(pl.multiple_of((me[0] ^ d) * cols, 16), cols), :] = blocks[i][...]
     out_ref[...] = lax.dot_general(
         tokens[...], wide[...], (((1,), (1,)), ((), ())), preferred_element_type=F32
     ).astype(BF16)
@@ -129,8 +132,8 @@
     me = (lax.axis_index(("yl", "xl")) ^ (core * 3)).reshape(1).astype(jnp.int32)
     tokens = spread(address(attn_out))
     blocks = list(cut(me, w_proj.T))
-    for d in range(1, 4):
-        blocks[d] = trade(blocks[d], d)
+    for i in range(1, 4):
+        blocks[i] = trade(blocks[i], PARTNERS[i])
     lane = jnp.arange(4 * cols, dtype=jnp.int32)
     moves = jnp.broadcast_to((lane >= 2 * cols) & (core == 1), (rows, 4 * cols))
     tokens, beside, moves = lax.optimization_barrier((tokens, beside, moves))

time: 175 us -> 177 us (1.011)
  blocking collectives: 92.2 us -> 94.6 us
where the time goes in v11:
time: 177 us; the launch traced here: 176 us
  blocking collectives  94.6 us (53%)
  starting transfers between devices  42.1 us (24%)
  waiting for transfers between devices  20.7 us (12%)
  local copies, waits for them, and re-layouts  7.92 us (4%)
  Pallas kernels  4.91 us (3%)
  matrix products  4.25 us (2%)
    all_to_all x1, blocking collectives, spread(): lax.all_to_all(pieces, CHIPS, split_axis=0, concat_axis=0, tiled=True, ax...  27.5 us
    all_to_all x1, blocking collectives, per_device(): lax.all_to_all(outgoing, EXPERT, split_axis=0, concat_axis=0, tiled=True)  22.2 us
    all_to_all x1, blocking collectives, per_device(): lax.all_to_all(result.reshape(groups, CAP, width_block).astype(BF16), EXP...  21.5 us
    all_to_all x1, starting transfers between devices, spread(): lax.all_to_all(pieces, CHIPS, split_axis=0, concat_axis=0, tiled=True, ax...  17.3 us
    all_to_all x1, starting transfers between devices, project(): got = lax.all_to_all(got, 'tensor', split_axis=0, concat_axis=0, tiled=True)  15.6 us
    all_to_all x1, blocking collectives, per_device(): lax.all_to_all(gate_up.reshape(4, quarter, 2 * slice_units), 'tensor', sp...  12.5 us
    all_to_all x1, waiting for transfers between devices, spread(): lax.all_to_all(pieces, CHIPS, split_axis=0, concat_axis=0, tiled=True, ax...  11.5 us
    all_to_all x1, blocking collectives, per_device(): lax.all_to_all(jnp.broadcast_to(hidden[None], (4, quarter, slice_units)),...  10.9 us
  transfers between devices with their start and end apart: 5, of which 2 were waited for; matrix products, arithmetic and copies ran while one was open for 3% of the time, Pallas kernels for 1%

profile of v11, /device:TPU:2, one launch (start us, length us, event | category | flops | bytes accessed | tf_op | source)
XLA Modules:
  0.0 176.4 jit_solution(8864732738027943128)
XLA Ops:
  0.6 2.1 %address.1 = bf16[64,8,1024]{2,1,0:T(8,128)(2,1)} custom-call(bf16[8,4096]{1,0:T(8,128)(2,1)} %attn_ref.1), custom_call_target="tpu_custom_call" | custom-call | tf_op jit(solution)/shard_map/address/pallas_call | solution.py:47
  2.8 17.3 %all-to-all-start = ((bf16[64,8,1024]{2,1,0:T(8,128)(2,1)}), bf16[64,8,1024]{2,1,0:T(8,128)(2,1)S(1)}, u32[]{:S(2)}, u32[]{:S(2)}) async-start(bf16[64,8,1024]{2,1,0:T(8,128)(2,1)} %address.1), calls=%async_computation | async-start | bytes 2097152 | tf_op jit(solution)/shard_map/all_to_all | solution.py:124
  20.1 1.2 copy-done.1
  21.3 0.9 cut.1
  22.2 3.4 %collective-permute-start = (bf16[112,1024]{1,0:T(8,128)(2,1)}, bf16[112,1024]{1,0:T(8,128)(2,1)S(1)}, u32[]{:S(2)}, u32[]{:S(2)}) collective-permute-start(bf16[112,1024]{1,0:T(8,128)(2,1)} %get-tuple-element.16), channel_id=1, source_target_pairs={{0,36},{4,32},{8,44},{12,40},{16,52},{20,48},{24,60},{28,56},{32,4... | collective-permute-start | bytes 688136 | tf_op jit(solution)/shard_map/ppermute | solution.py:120
  25.6 3.4 %collective-permute-start.1 = (bf16[112,1024]{1,0:T(8,128)(2,1)}, bf16[112,1024]{1,0:T(8,128)(2,1)}, u32[]{:S(2)}, u32[]{:S(2)}) collective-permute-start(bf16[112,1024]{1,0:T(8,128)(2,1)} %get-tuple-element.17), channel_id=1, source_target_pairs={{0,4},{4,0},{8,12},{12,8},{16,20},{20,16},{24,28},{28,24},{32,36},... | collective-permute-start | bytes 688136 | tf_op jit(solution)/shard_map/ppermute | solution.py:120
  29.0 2.4 %collective-permute-start.2 = (bf16[112,1024]{1,0:T(8,128)(2,1)}, bf16[112,1024]{1,0:T(8,128)(2,1)}, u32[]{:S(2)}, u32[]{:S(2)}) collective-permute-start(bf16[112,1024]{1,0:T(8,128)(2,1)} %get-tuple-element.18), channel_id=1, source_target_pairs={{0,32},{4,36},{8,40},{12,44},{16,48},{20,52},{24,56},{28,60},{32,0... | collective-permute-start | bytes 688136 | tf_op jit(solution)/shard_map/ppermute | solution.py:120
  31.4 4.8 %copy.41 = bf16[224,8,2,512]{3,1,2,0:T(8,128)(2,1)} copy(bf16[224,8,2,512]{3,2,1,0:T(2,128)(2,1)} %bitcast.32) | data formatting | bytes 7340032
  36.3 0.1 select_reduce_fusion
  36.4 11.5 %all-to-all-done = bf16[64,8,1024]{2,1,0:T(8,128)(2,1)S(1)} async-done(((bf16[64,8,1024]{2,1,0:T(8,128)(2,1)}), bf16[64,8,1024]{2,1,0:T(8,128)(2,1)S(1)}, u32[]{:S(2)}, u32[]{:S(2)}) %all-to-all-start) | async-done | bytes 1048608 | tf_op jit(solution)/shard_map/all_to_all | solution.py:124
  48.0 1.9 %partial_sums.1 = bf16[512,512]{1,0:T(8,128)(2,1)S(1)} custom-call(s32[1]{0:T(128)} %bitcast.1.me, bf16[512,1024]{1,0:T(8,128)(2,1)S(1)} %bitcast.28, bf16[112,1024]{1,0:T(8,128)(2,1)S(1)} %get-tuple-element.15.refs_0_, bf16[112,1024]{1,0:T(8,128)(2,1)S(1)} %collective-permute-done.refs_1_, bf16[112,1024]{1,0:T(8,128)(2,1)} %collective-permute-done.1.refs_2_, ...), custom_call_target="tpu_custom_call" | custom-call | tf_op jit(solution)/shard_map/partial_sums/pallas_call | solution.py:99
  49.9 27.5 %all_to_all.35 = bf16[64,8,512]{2,1,0:T(8,128)(2,1)S(1)} all-to-all(bf16[64,8,512]{2,1,0:T(8,128)(2,1)S(1)} %bitcast.29), channel_id=1, replica_groups={{0,4,8,12,16,20,24,28,32,36,40,44,48,52,56,60,64,68,72,76,80,84,88,92,9..., dimensions={0} | all-to-all | bytes 1048576 | tf_op jit(solution)/shard_map/all_to_all | solution.py:124
  77.4 0.1 slice_reduce_fusion
  77.5 0.7 maximum_select_fusion
  78.2 15.6 %all-to-all-start.2 = ((bf16[4,4,8,448]{3,2,1,0:T(8,128)(2,1)}), bf16[4,4,8,448]{3,2,1,0:T(8,128)(2,1)S(1)}, u32[]{:S(2)}, u32[]{:S(2)}) async-start(bf16[4,4,8,448]{3,2,1,0:T(8,128)(2,1)} %maximum_select_fusion), calls=%async_computation.2 | async-start | bytes 262144 | tf_op jit(solution)/shard_map/all_to_all | solution.py:145
  93.8 0.1 copy.36
  93.9 9.2 %all-to-all-done.2 = bf16[4,4,8,448]{3,2,1,0:T(8,128)(2,1)S(1)} async-done(((bf16[4,4,8,448]{3,2,1,0:T(8,128)(2,1)}), bf16[4,4,8,448]{3,2,1,0:T(8,128)(2,1)S(1)}, u32[]{:S(2)}, u32[]{:S(2)}) %all-to-all-start.2) | async-done | bytes 114720 | tf_op jit(solution)/shard_map/all_to_all | solution.py:145
  103.2 0.1 reshape.80
  103.3 0.1 reshape.82
  103.5 0.1 concatenate.12
  103.6 0.2 convolution_convert_fusion.1
  103.9 0.5 copy.38
  104.4 22.2 %all_to_all.36 = bf16[64,2,1792]{2,1,0:T(2,128)(2,1)S(1)} all-to-all(bf16[64,2,1792]{2,1,0:T(2,128)(2,1)S(1)} %copy.38), channel_id=1, replica_groups=mesh['plane'=2,'core'=2,'yh'=4,'yl'=2,'xh'=4,'xl'=2,'tensor'=4] {'yh','y..., dimensions={0} | all-to-all | bytes 917504 | tf_op jit(solution)/shard_map/all_to_all | solution.py:170
  126.6 0.2 reshape.84
  126.8 2.7 %convolution_convert_fusion.3 = bf16[128,1024]{1,0:T(8,128)(2,1)S(1)} fusion(bf16[128,1792]{1,0:T(8,128)(2,1)S(1)} %reshape.84, bf16[1792,1024]{1,0:T(8,128)(2,1)} %bitcast.31), kind=kOutput, calls=%fused_computation.4 | convolution fusion | flops 469893120 | bytes 4390912 | tf_op jit(solution)/shard_map/dot_general | solution.py:172
  129.5 12.5 %all_to_all.37 = bf16[4,32,1024]{2,1,0:T(8,128)(2,1)S(1)} all-to-all(bf16[4,32,1024]{2,1,0:T(8,128)(2,1)S(1)} %bitcast.34), channel_id=1, replica_groups=mesh['plane'=2,'core'=2,'yh'=4,'yl'=2,'xh'=4,'xl'=2,'tensor'=4] {'tensor'}, dimensions={0} | all-to-all | bytes 524288 | tf_op jit(solution)/shard_map/all_to_all | solution.py:174
  142.0 10.9 %all_to_all.38 = bf16[4,32,512]{2,1,0:T(8,128)(2,1)S(1)} all-to-all(bf16[4,32,512]{2,1,0:T(8,128)(2,1)S(1)} %broadcast_in_dim.34), channel_id=1, replica_groups=mesh['plane'=2,'core'=2,'yh'=4,'yl'=2,'xh'=4,'xl'=2,'tensor'=4] {'tensor'}, dimensions={0} | all-to-all | bytes 262144 | tf_op jit(solution)/shard_map/all_to_all | solution.py:179
  153.0 0.4 convolution_convert_fusion
  153.4 0.5 copy.40
  153.9 21.5 %all_to_all.39 = bf16[64,2,1792]{2,1,0:T(2,128)(2,1)S(1)} all-to-all(bf16[64,2,1792]{2,1,0:T(2,128)(2,1)S(1)} %copy.40), channel_id=1, replica_groups=mesh['plane'=2,'core'=2,'yh'=4,'yl'=2,'xh'=4,'xl'=2,'tensor'=4] {'yh','y..., dimensions={0} | all-to-all | bytes 917504 | tf_op jit(solution)/shard_map/all_to_all | solution.py:187
  175.4 0.2 reshape.87
  175.5 0.9 convolution_convert_fusion.2
  (33 shorter events, 0.3 us)
Async XLA Ops:
  0.6 152.4 %copy-start = (bf16[1,512,1792]{2,1,0:T(8,128)(2,1)S(1)}, bf16[1,512,1792]{2,1,0:T(8,128)(2,1)}, u32[]{:S(2)}) copy-start(bf16[1,512,1792]{2,1,0:T(8,128)(2,1)} %param.10) | copy-start | bytes 5505028
  2.8 45.2 %all-to-all-start = ((bf16[64,8,1024]{2,1,0:T(8,128)(2,1)}), bf16[64,8,1024]{2,1,0:T(8,128)(2,1)S(1)}, u32[]{:S(2)}, u32[]{:S(2)}) async-start(bf16[64,8,1024]{2,1,0:T(8,128)(2,1)} %address.1), calls=%async_computation | async-start | bytes 2097152 | tf_op jit(solution)/shard_map/all_to_all | solution.py:124
  20.1 1.2 copy-start.1
  22.2 25.8 %collective-permute-start = (bf16[112,1024]{1,0:T(8,128)(2,1)}, bf16[112,1024]{1,0:T(8,128)(2,1)S(1)}, u32[]{:S(2)}, u32[]{:S(2)}) collective-permute-start(bf16[112,1024]{1,0:T(8,128)(2,1)} %get-tuple-element.16), channel_id=1, source_target_pairs={{0,36},{4,32},{8,44},{12,40},{16,52},{20,48},{24,60},{28,56},{32,4... | collective-permute-start | bytes 688136 | tf_op jit(solution)/shard_map/ppermute | solution.py:120
  25.6 22.4 %collective-permute-start.1 = (bf16[112,1024]{1,0:T(8,128)(2,1)}, bf16[112,1024]{1,0:T(8,128)(2,1)}, u32[]{:S(2)}, u32[]{:S(2)}) collective-permute-start(bf16[112,1024]{1,0:T(8,128)(2,1)} %get-tuple-element.17), channel_id=1, source_target_pairs={{0,4},{4,0},{8,12},{12,8},{16,20},{20,16},{24,28},{28,24},{32,36},... | collective-permute-start | bytes 688136 | tf_op jit(solution)/shard_map/ppermute | solution.py:120
  29.0 19.0 %collective-permute-start.2 = (bf16[112,1024]{1,0:T(8,128)(2,1)}, bf16[112,1024]{1,0:T(8,128)(2,1)}, u32[]{:S(2)}, u32[]{:S(2)}) collective-permute-start(bf16[112,1024]{1,0:T(8,128)(2,1)} %get-tuple-element.18), channel_id=1, source_target_pairs={{0,32},{4,36},{8,40},{12,44},{16,48},{20,52},{24,56},{28,60},{32,0... | collective-permute-start | bytes 688136 | tf_op jit(solution)/shard_map/ppermute | solution.py:120
  31.4 4.9 %copy-start.3 = (f32[8,8]{1,0:T(8,128)S(1)}, f32[8,8]{1,0:T(8,128)}, u32[]{:S(2)}) copy-start(f32[8,8]{1,0:T(8,128)} %param.13) | copy-start | bytes 772
  31.4 4.9 %copy-start.4 = (s32[8,8]{1,0:T(8,128)S(1)}, s32[8,8]{1,0:T(8,128)}, u32[]{:S(2)}) copy-start(s32[8,8]{1,0:T(8,128)} %param.12) | copy-start | bytes 772
  31.4 4.9 %copy-start.5 = (s32[8,8]{1,0:T(8,128)S(1)}, s32[8,8]{1,0:T(8,128)}, u32[]{:S(2)}) copy-start(s32[8,8]{1,0:T(8,128)} %param.11) | copy-start | bytes 772
  78.2 25.0 %all-to-all-start.2 = ((bf16[4,4,8,448]{3,2,1,0:T(8,128)(2,1)}), bf16[4,4,8,448]{3,2,1,0:T(8,128)(2,1)S(1)}, u32[]{:S(2)}, u32[]{:S(2)}) async-start(bf16[4,4,8,448]{3,2,1,0:T(8,128)(2,1)} %maximum_select_fusion), calls=%async_computation.2 | async-start | bytes 262144 | tf_op jit(solution)/shard_map/all_to_all | solution.py:145
  103.6 25.8 %copy-start.2 = (bf16[8,1792]{1,0:T(8,128)(2,1)}, bf16[8,1792]{1,0:T(8,128)(2,1)S(1)}, u32[]{:S(2)}) copy-start(bf16[8,1792]{1,0:T(8,128)(2,1)S(1)} %broadcast_select_fusion) | copy-start | bytes 86020
